TPU v7x, 32 devices: a whole 2x2x4 slice. The times are simulated.
32 devices in a mesh: groups: 2 (over x), rows: 16 (over z, y, core).
Axes of the slice: x: 2, y: 2, z: 4, core: 2. Of those that a mesh axis runs over, the one named last changes fastest.
Arguments:
- features: bfloat16 [131072, 1024], P(('groups', 'rows')), parts along dimension 0, may hold values from -6 to 6
- coef: bfloat16 [1024], replicated, may hold values from -0.1875 to 0.1875
- labels: int32 [131072], P(('groups', 'rows')), parts along dimension 0, may hold values 0 or 1
- passage_id: int32 [131072, 1], P(('groups', 'rows')), parts along dimension 0, may hold values from 0 to 127; in each aligned block of 4096 rows (0 to 4095, 4096 to 8191, ...) at most 64 rows name the same one
- slot_of: int32 [256], P('groups'), parts along dimension 0, may hold values from 0 to 127, each once
Outputs:
- hessian: float32 [2048, 1024], P(('groups', 'rows')), parts along dimension 0
- meat: float32 [2048, 1024], P(('groups', 'rows')), parts along dimension 0
- grad_sums: float32 [256, 1024], P(('groups', 'rows')), parts along dimension 0
There are 2 independent parts, one for each index of `groups`. A program takes and returns all parts, laid end to end along the dimension named above; an argument that names none is the same for every part. Nothing has to cross between parts.
Inputs may be any that keep to these rules, and one draw needn't show every extreme that they name: `passage_id`: on one device's rows each passage is named at most 64 times; every passage is named somewhere. `slot_of`: each slot once.
All inputs are finite; a program needn't handle non-finite values. No bound on the sum of `labels` on one device may be relied on, other than what follows from the above.
Results may differ from a plain program's by a relative error of at most 0.0028.
Values may be sent and summed in bfloat16 or wider, within the bound.
No kernel may reach another device: no remote copies, remote signals or barrier semaphores. Data moves between devices by JAX's collectives and lax.ppermute only.
A program may use at most 128 MiB of HBM per device.

v0:
```python
import jax
import jax.numpy as jnp
from jax import lax
from jax.sharding import PartitionSpec as P


def local(features, coef, labels, passage_id, slot_of):
    feat_dim = features.shape[1]
    rows_here = features.shape[0]
    devices = lax.axis_size("rows")
    clusters = slot_of.shape[0]
    per_owner = clusters // devices
    logits = jnp.dot(features, coef, preferred_element_type=jnp.float32)
    probability = jax.nn.sigmoid(logits)
    weighted = (features * (probability * (1.0 - probability))[:, None]).astype(jnp.bfloat16)
    scored = (features * (labels.astype(jnp.float32) - probability)[:, None]).astype(jnp.bfloat16)
    hessian = lax.psum_scatter(
        lax.dot_general(
            features, weighted, (((0,), (0,)), ((), ())), preferred_element_type=jnp.float32
        ),
        "rows",
        scatter_dimension=0,
        tiled=True,
    )
    cluster_ids = jnp.arange(clusters, dtype=jnp.int32)
    matches = passage_id == cluster_ids[None, :]
    slot_row = jnp.sum(jnp.where(matches, slot_of[None, :], 0), axis=1)
    capacity = 2 * rows_here // devices
    owner_dev = slot_row // per_owner
    local_id = slot_row % per_owner
    to_owner = (owner_dev[:, None] == jnp.arange(devices, dtype=jnp.int32)[None, :]).astype(
        jnp.int32
    )
    before = jnp.cumsum(to_owner, axis=0) - to_owner
    position = jnp.sum(before * to_owner, axis=1)
    target = owner_dev * capacity + position
    outgoing = jnp.zeros((devices * capacity, feat_dim), jnp.bfloat16).at[target].set(scored)
    tag_out = (
        jnp.full((devices * capacity,), -1.0, jnp.bfloat16)
        .at[target]
        .set(local_id.astype(jnp.bfloat16))
    )
    received, tag_rows = (
        lax.all_to_all(
            outgoing.reshape(devices, capacity, feat_dim),
            "rows",
            split_axis=0,
            concat_axis=0,
            tiled=True,
        ),
        lax.all_to_all(
            tag_out.reshape(devices, capacity), "rows", split_axis=0, concat_axis=0, tiled=True
        ),
    )
    slot_vals = jnp.arange(per_owner, dtype=jnp.int32).astype(jnp.bfloat16)
    member = (tag_rows.reshape(-1)[None, :] == slot_vals[:, None]).astype(jnp.bfloat16)
    grad_local = jnp.dot(member, received.reshape(-1, feat_dim), preferred_element_type=jnp.float32)
    meat = lax.psum_scatter(
        lax.dot_general(
            grad_local,
            grad_local,
            (((0,), (0,)), ((), ())),
            precision=lax.Precision.HIGHEST,
            preferred_element_type=jnp.float32,
        ),
        "rows",
        scatter_dimension=0,
        tiled=True,
    )
    return (hessian, meat, grad_local)


def solution(mesh):
    in_specs = (
        P(("groups", "rows"), None),
        P(),
        P(("groups", "rows")),
        P(("groups", "rows"), None),
        P("groups"),
    )
    out_specs = (
        P(("groups", "rows"), None),
        P(("groups", "rows"), None),
        P(("groups", "rows"), None),
    )
    return jax.shard_map(local, mesh=mesh, in_specs=in_specs, out_specs=out_specs, check_vma=False)
```

profile of v0, /device:TPU:0, one launch (start us, length us, event | category | flops | bytes accessed | tf_op | source)
XLA Modules:
  0.0 575.4 jit_solution(12921245089763668387)
XLA Ops:
  7.2 0.0 copy-start.1
  7.2 2.0 select_reduce_fusion
  9.2 4.6 reduce-window.6
  13.9 0.5 slice_reduce_fusion
  14.3 0.2 reduce-window.9
  14.5 0.1 broadcast_add_fusion
  14.7 0.2 fusion.14
  14.9 0.1 compare_select_fusion
  15.0 28.6 %scatter_custom_fusion = bf16[8192]{0:T(1024)(128)(2,1)S(1)} fusion(s32[4096]{0:T(1024)S(1)} %bitcast.60, bf16[4096]{0:T(1024)(128)(2,1)S(1)} %get-tuple-element.15, bf16[]{:T(256)} %constant.34.clone.1), kind=kCustom, calls=%fused_computation.53 | custom fusion | bytes 16386 | tf_op jit(solution)/shard_map/scatter | solution.py:41
  43.6 0.5 broadcast.150
  44.1 0.7 reduce.3
  44.8 0.6 reshape.141
  45.4 7.4 %all-to-all-start = ((bf16[16,2,256]{2,1,0:T(2,128)(2,1)}), bf16[16,2,256]{2,1,0:T(2,128)(2,1)S(1)}, u32[]{:S(2)}, u32[]{:S(2)}) async-start(bf16[16,2,256]{2,1,0:T(2,128)(2,1)} %reshape.141), calls=%async_computation | async-start | bytes 32768 | tf_op jit(solution)/shard_map/all_to_all | solution.py:51
  52.8 0.7 reshape.131
  53.5 5.6 fusion.28
  59.2 0.0 copy-done.1
  59.2 29.7 %scatter_custom_fusion.1 = bf16[8192,1024]{1,0:T(8,128)(2,1)} fusion(s32[4096]{0:T(1024)S(1)} %bitcast.61, bf16[4096,1024]{1,0:T(8,128)(2,1)} %param.5, f32[4096]{0:T(1024)S(1)} %get-tuple-element.17, bf16[]{:T(256)} %constant.43.clone.1), kind=kCustom, calls=%fused_computation.7 | custom fusion | flops 12582912 | bytes 25182210 | tf_op jit(solution)/shard_map/scatter | solution.py:37
  88.9 0.0 all-to-all-done
  88.9 6.1 %all-to-all-start.1 = ((bf16[16,512,1024]{2,1,0:T(8,128)(2,1)}), bf16[16,512,1024]{2,1,0:T(8,128)(2,1)}, u32[]{:S(2)}, u32[]{:S(2)}) async-start(bf16[16,512,1024]{2,1,0:T(8,128)(2,1)} %bitcast.52), calls=%async_computation.1 | async-start | bytes 33554432 | tf_op jit(solution)/shard_map/all_to_all | solution.py:44
  94.9 0.0 reduce-scatter.7.cloned.1.call-start
  95.0 15.3 %fusion.9 = f32[1024,1024]{0,1:T(8,128)} fusion(bf16[4096,1024]{1,0:T(8,128)(2,1)} %param.5, f32[4096]{0:T(1024)S(1)} %get-tuple-element.18), kind=kOutput, calls=%fused_computation.11 | convolution fusion | flops 8602517504 | bytes 12599296 | tf_op jit(solution)/shard_map/dot_general | solution.py:18
  110.3 5.4 copy.14
  115.7 0.0 reduce-scatter.7.cloned.1.call-update
  115.7 0.3 reduce-scatter.5.cloned.1.call-start
  116.0 0.1 reduce.1
  116.1 300.9 %all-to-all-done.1 = bf16[16,512,1024]{2,1,0:T(8,128)(2,1)} async-done(((bf16[16,512,1024]{2,1,0:T(8,128)(2,1)}), bf16[16,512,1024]{2,1,0:T(8,128)(2,1)}, u32[]{:S(2)}, u32[]{:S(2)}) %all-to-all-start.1) | async-done | bytes 16777248 | tf_op jit(solution)/shard_map/all_to_all | solution.py:44
  417.0 8.1 %fusion.16 = f32[8,1024]{1,0:T(8,128)S(1)} fusion(bf16[8192,1024]{1,0:T(8,128)(2,1)} %bitcast.9, bf16[8192]{0:T(1024)(128)(2,1)S(1)} %bitcast.55, bf16[8]{0:T(256)(128)(2,1)S(1)} %iota_convert_fusion), kind=kOutput, calls=%fused_computation.22 | convolution fusion | flops 134283264 | bytes 16826384 | tf_op jit(solution)/shard_map/dot_general | solution.py:57
  425.1 0.0 copy-start
  425.1 5.0 fusion.29
  430.1 0.0 reduce-scatter.5.cloned.1.call-update
  430.2 0.0 reduce-scatter.7.cloned.1.call-done
  430.2 138.3 %reduce-scatter.5.cloned.1.call-done = f32[64,1024]{1,0:T(8,128)} async-done(((f32[1024,1024]{1,0:T(8,128)}), f32[64,1024]{1,0:T(8,128)}) %reduce-scatter.5.cloned.1.call-update) | async-done | bytes 262160 | tf_op jit(solution)/shard_map/reduce_scatter | solution.py:58
  568.5 0.0 copy-done
  (8 shorter events, 0.1 us)
Async XLA Ops:
  7.2 52.0 %copy-start.1 = (s32[4096]{0:T(1024)S(1)}, s32[4096]{0:T(1024)}, u32[]{:S(2)}) copy-start(s32[4096]{0:T(1024)} %param.7) | copy-start | bytes 49156
  45.4 43.4 %all-to-all-start = ((bf16[16,2,256]{2,1,0:T(2,128)(2,1)}), bf16[16,2,256]{2,1,0:T(2,128)(2,1)S(1)}, u32[]{:S(2)}, u32[]{:S(2)}) async-start(bf16[16,2,256]{2,1,0:T(2,128)(2,1)} %reshape.141), calls=%async_computation | async-start | bytes 32768 | tf_op jit(solution)/shard_map/all_to_all | solution.py:51
  88.9 328.1 %all-to-all-start.1 = ((bf16[16,512,1024]{2,1,0:T(8,128)(2,1)}), bf16[16,512,1024]{2,1,0:T(8,128)(2,1)}, u32[]{:S(2)}, u32[]{:S(2)}) async-start(bf16[16,512,1024]{2,1,0:T(8,128)(2,1)} %bitcast.52), calls=%async_computation.1 | async-start | bytes 33554432 | tf_op jit(solution)/shard_map/all_to_all | solution.py:44
  94.9 335.3 %reduce-scatter.7.cloned.1.call-start = ((), (), s32[]{:S(2)}) async-start(), calls=%async_computation.5 | async-start | bytes 4456448
  115.7 452.9 %reduce-scatter.5.cloned.1.call-start = ((), (), s32[]{:S(2)}) async-start(), calls=%async_computation.4 | async-start | bytes 4456448 | tf_op jit(solution)/shard_map/reduce_scatter | solution.py:58
  425.1 143.4 %copy-start = (f32[8,1024]{1,0:T(8,128)}, f32[8,1024]{1,0:T(8,128)S(1)}, u32[]{:S(2)}) copy-start(f32[8,1024]{1,0:T(8,128)S(1)} %fusion.16) | copy-start | bytes 98308
Sparse Core Ops, SparseCore 0:
  115.8 283.1 reduce-scatter.6
  430.3 138.2 reduce-scatter.4
where the time goes:
time: 576 us; the launch traced here: 575 us
  waiting for transfers between devices  439 us (76%)
  other arithmetic  37.8 us (7%)
  local copies, waits for them, and re-layouts  36.3 us (6%)
  matrix products  34.1 us (6%)
  between operations  14.2 us (2%)
  starting transfers between devices  13.8 us (2%)
    all_to_all x1, waiting for transfers between devices, local(): lax.all_to_all(outgoing.reshape(devices, capacity, feat_dim), 'rows', spl...  301 us
    reduce_scatter x1, waiting for transfers between devices, local(): lax.psum_scatter(lax.dot_general(grad_local, grad_local, (((0,), (0,)), (...  138 us
    scatter x1, other arithmetic, local(): jnp.zeros((devices * capacity, feat_dim), jnp.bfloat16).at[target]  29.7 us
    scatter x1, local copies, waits for them, and re-layouts, local(): tag_out = jnp.full((devices * capacity,), -1.0, jnp.bfloat16).at[target]....  28.6 us
    dot_general x1, matrix products, local(): lax.dot_general(features, weighted, (((0,), (0,)), ((), ())), preferred_e...  15.3 us
  transfers between devices with their start and end apart: 4, of which 2 were waited for; matrix products, arithmetic and copies ran while one was open for 12% of the time, Pallas kernels for 0%

commit v1 on v0

v1 whole, which is shorter than its diff:
```python
import functools

import jax
import jax.numpy as jnp
from jax import lax
from jax.experimental import pallas as pl
from jax.experimental.pallas import tpu as pltpu
from jax.sharding import PartitionSpec as P

BF16 = jnp.bfloat16
F32 = jnp.float32
LANES = 128
VMEM_LIMIT = 48 * 1024 * 1024


def score_kernel(
    per_owner, place, x_ref, coef_ref, label_ref, pid_ref, slot_ref, w_ref, send_ref, keep_ref, names
):
    step = pl.program_id(0)
    clusters = slot_ref.shape[1]
    half = clusters // 2

    @pl.when(step == 0)
    def _():
        core = place[0]
        row = lax.broadcasted_iota(jnp.int32, (clusters, clusters), 0)
        mine = row >= half
        inner = jnp.where(mine, row - half, row)
        slot = (2 * (inner // per_owner) + jnp.where(mine, core, 1 - core)) * per_owner + inner % per_owner
        passage = lax.broadcasted_iota(jnp.int32, (clusters, clusters), 1)
        found = jnp.where(slot_ref[...] == slot, passage, 0)
        names[...] = jnp.broadcast_to(jnp.sum(found, axis=1, keepdims=True), names.shape)
        send_ref[...] = jnp.zeros_like(send_ref)
        keep_ref[...] = jnp.zeros_like(keep_ref)

    x = x_ref[...]
    rows = x.shape[0]
    coef = jnp.broadcast_to(coef_ref[...], (16, x.shape[1]))
    logits = lax.dot_general(coef, x, (((1,), (1,)), ((), ())), preferred_element_type=F32)[0:1]
    prob = 1.0 / (1.0 + jnp.exp(-logits))
    w_ref[...] = prob * (1.0 - prob)
    score = label_ref[...].astype(F32) - prob
    score = jnp.broadcast_to(score, (LANES, rows)).T
    wide = x.shape[1] // LANES
    scored = (x.astype(F32) * jnp.concatenate([score] * wide, axis=1)).astype(BF16)
    member = jnp.where(pid_ref[...] == names[:, 0:1], 1.0, 0.0).astype(BF16)
    sums = jnp.dot(member, scored, preferred_element_type=F32)
    send_ref[...] += sums[:half]
    keep_ref[...] += sums[half:]


def hessian_kernel(blk, place, x_ref, w_ref, send_ref, keep_ref, acc):
    step = pl.program_id(0)
    feat = x_ref.shape[1]
    parity, core = place[0], place[1]
    weight = w_ref[...]
    left = []
    for block in range(feat // (2 * LANES)):
        start = pl.multiple_of((2 * block + parity) * LANES, LANES)
        turned = x_ref[:, pl.ds(start, LANES)].astype(F32).T
        left.append((turned * weight).astype(BF16))
    term = jnp.dot(jnp.concatenate(left, axis=0), x_ref[...], preferred_element_type=F32)

    @pl.when(step == 0)
    def _():
        acc[...] = term

    @pl.when(step > 0)
    def _():
        acc[...] += term

    @pl.when(step == pl.num_programs(0) - 1)
    def _():
        for pair in range(acc.shape[0] // (2 * blk)):
            base = pair * 2 * blk
            out = pl.ds(pair * blk, blk)
            keep_ref[out, :] = acc[pl.ds(pl.multiple_of(base + core * blk, 8), blk), :]
            send_ref[out, :] = acc[pl.ds(pl.multiple_of(base + (1 - core) * blk, 8), blk), :].astype(BF16)


def scores(place, x, coef, labels, pid, slot_of, per_owner, tile=512):
    rows, feat = x.shape
    clusters = slot_of.shape[0]
    half = clusters // 2
    whole = lambda shape: pl.BlockSpec(shape, lambda i: (0, 0))
    return pl.pallas_call(
        functools.partial(score_kernel, per_owner),
        grid=(rows // tile,),
        in_specs=[
            pl.BlockSpec(memory_space=pltpu.SMEM),
            pl.BlockSpec((tile, feat), lambda i: (i, 0)),
            whole((1, feat)),
            pl.BlockSpec((1, tile), lambda i: (0, i)),
            pl.BlockSpec((1, tile), lambda i: (0, i)),
            whole((1, clusters)),
        ],
        out_specs=[pl.BlockSpec((1, tile), lambda i: (0, i)), whole((half, feat)), whole((half, feat))],
        out_shape=[
            jax.ShapeDtypeStruct((1, rows), F32),
            jax.ShapeDtypeStruct((half, feat), F32),
            jax.ShapeDtypeStruct((half, feat), F32),
        ],
        scratch_shapes=[pltpu.VMEM((clusters, LANES), jnp.int32)],
        compiler_params=pltpu.CompilerParams(vmem_limit_bytes=VMEM_LIMIT),
        name="scores",
    )(place, x, coef.reshape(1, feat), labels.reshape(1, rows), pid.reshape(1, rows), slot_of.reshape(1, clusters))


def hessian_half(place, x, w, blk, tile=1024):
    rows, feat = x.shape
    half, quarter = feat // 2, feat // 4
    whole = lambda shape: pl.BlockSpec(shape, lambda i: (0, 0))
    return pl.pallas_call(
        functools.partial(hessian_kernel, blk),
        grid=(rows // tile,),
        in_specs=[
            pl.BlockSpec(memory_space=pltpu.SMEM),
            pl.BlockSpec((tile, feat), lambda i: (i, 0)),
            pl.BlockSpec((1, tile), lambda i: (0, i)),
        ],
        out_specs=[whole((quarter, feat)), whole((quarter, feat))],
        out_shape=[
            jax.ShapeDtypeStruct((quarter, feat), BF16),
            jax.ShapeDtypeStruct((quarter, feat), F32),
        ],
        scratch_shapes=[pltpu.VMEM((half, feat), F32)],
        compiler_params=pltpu.CompilerParams(vmem_limit_bytes=VMEM_LIMIT),
        name="hessian_half",
    )(place, x, w)


def local(features, coef, labels, passage_id, slot_of):
    feat = features.shape[1]
    devices = lax.axis_size("rows")
    clusters = slot_of.shape[0]
    per_owner = clusters // devices
    blk = feat // devices
    me = lax.axis_index("rows")
    turn = LANES // blk
    core, parity = me % 2, (me // turn) % 2

    def swap(array, mask):
        return lax.ppermute(array, "rows", [(i, i ^ mask) for i in range(devices)])

    def rest(number):
        return (number // (2 * turn)) * (turn // 2) + (number % turn) // 2

    core_ref = core.astype(jnp.int32).reshape(1)
    w, sums_send, sums_keep = scores(core_ref, features, coef, labels, passage_id, slot_of, per_owner)
    sums = sums_keep + swap(sums_send, 1)
    masks = [m for m in range(1, devices) if not m & 1 and not m & turn]
    members = [
        [base ^ m for m in [0] + masks]
        for base in range(devices)
        if not rest(base)
    ]
    gathered = lax.all_gather(sums.astype(BF16), "rows", axis=0, axis_index_groups=members)

    far_send, far_keep = hessian_half(jnp.stack([1 - parity, core]), features, w, blk)
    far = (far_keep + swap(far_send, 1).astype(F32)).astype(BF16)
    arrived = swap(far, turn)
    near_send, near_keep = hessian_half(jnp.stack([parity, core]), features, w, blk)
    near = near_keep + swap(near_send, 1).astype(F32) + arrived.astype(F32)
    mine = rest(me)
    block = lambda n: lax.dynamic_slice_in_dim(near, n * blk, blk, 0)
    hessian = block(mine)
    parts = [swap(block(mine ^ rest(m)).astype(BF16), m) for m in masks]

    sums = jnp.sum(gathered.astype(F32), axis=0)
    sums = sums + swap(sums, turn)
    other = swap(sums, 1)
    chip = me // 2
    grad_local = lax.dynamic_slice_in_dim(sums, chip * per_owner, per_owner, 0)
    stack = jnp.concatenate([sums, other], axis=0)
    columns = lax.dynamic_slice_in_dim(stack, me * blk, blk, 1)
    meat = lax.dot_general(
        columns,
        stack,
        (((0,), (0,)), ((), ())),
        precision=lax.Precision.HIGHEST,
        preferred_element_type=F32,
    )
    for part in parts:
        hessian = hessian + part.astype(F32)
    return (hessian, meat, grad_local)


def solution(mesh):
    in_specs = (
        P(("groups", "rows"), None),
        P(),
        P(("groups", "rows")),
        P(("groups", "rows"), None),
        P("groups"),
    )
    out_specs = (
        P(("groups", "rows"), None),
        P(("groups", "rows"), None),
        P(("groups", "rows"), None),
    )
    return jax.shard_map(local, mesh=mesh, in_specs=in_specs, out_specs=out_specs, check_vma=False)
```

time: 576 us -> 75.3 us (0.13)
  waiting for transfers between devices: 439 us -> 17.1 us
  other arithmetic: 37.8 us -> 2.34 us
  matrix products: 34.1 us -> 1.18 us
  local copies, waits for them, and re-layouts: 36.3 us -> 3.45 us
  Pallas kernels: 0 us -> 25.5 us
  blocking collectives: 0 us -> 16.2 us
  between operations: 14.2 us -> 0.76 us
    all_to_all x2 -> x0, waiting for transfers between devices: 301 us -> none  [the longest x1 301 us: local(): lax.all_to_all(outgoing.reshape(devices, capacity, feat_dim), 'rows', spl...]
    reduce_scatter x1 -> x0, waiting for transfers between devices: 138 us -> none  [local(): lax.psum_scatter(lax.dot_general(grad_local, grad_local, (((0,), (0,)), (...]
    dot_general x4 -> x1, matrix products: 34.1 us -> 1.18 us  [local(): lax.dot_general(columns, stack, (((0,), (0,)), ((), ())), precision=lax.P...]
    scatter x1 -> x0, other arithmetic: 29.7 us -> none  [local(): jnp.zeros((devices * capacity, feat_dim), jnp.bfloat16).at[target]]
    scatter x1 -> x0, local copies, waits for them, and re-layouts: 28.6 us -> none  [local(): tag_out = jnp.full((devices * capacity,), -1.0, jnp.bfloat16).at[target]....]
    pallas_call x0 -> x3, Pallas kernels: none -> 25.5 us  [the longest x2 15.9 us: hessian_half(): pl.pallas_call(functools.partial(hessian_kernel, blk), grid=(rows // tile...]
    ppermute x0 -> x9, waiting for transfers between devices: none -> 17.1 us  [swap(): return lax.ppermute(array, 'rows', [(i, i ^ mask) for i in range(devices)])]
    all_gather x0 -> x1, blocking collectives: none -> 16.2 us  [local(): lax.all_gather(sums.astype(BF16), 'rows', axis=0, axis_index_groups=members)]
  transfers between devices with their start and end apart: 4 -> 9, of which waited for: 2 -> 4; matrix products, arithmetic and copies ran while one was open for 12% -> 4% of each run, Pallas kernels for 0% -> 11%
where the time goes in v1:
time: 75.3 us; the launch traced here: 74.7 us
  Pallas kernels  25.5 us (34%)
  waiting for transfers between devices  17.1 us (23%)
  blocking collectives  16.2 us (22%)
  starting transfers between devices  8.17 us (11%)
  local copies, waits for them, and re-layouts  3.45 us (5%)
  other arithmetic  2.34 us (3%)
  matrix products  1.18 us (2%)
  between operations  0.76 us (1%)
    ppermute x9, waiting for transfers between devices, swap(): return lax.ppermute(array, 'rows', [(i, i ^ mask) for i in range(devices)])  17.1 us
    all_gather x1, blocking collectives, local(): lax.all_gather(sums.astype(BF16), 'rows', axis=0, axis_index_groups=members)  16.2 us
    pallas_call x2, Pallas kernels, hessian_half(): pl.pallas_call(functools.partial(hessian_kernel, blk), grid=(rows // tile...  15.9 us
    pallas_call x1, Pallas kernels, scores(): pl.pallas_call(functools.partial(score_kernel, per_owner), grid=(rows //...  9.63 us
    ppermute x9, starting transfers between devices, swap(): return lax.ppermute(array, 'rows', [(i, i ^ mask) for i in range(devices)])  8.17 us
    unnamed x6, local copies, waits for them, and re-layouts  2.09 us
  transfers between devices with their start and end apart: 9, of which 4 were waited for; matrix products, arithmetic and copies ran while one was open for 4% of the time, Pallas kernels for 11%

profile of v1, /device:TPU:0, one launch (start us, length us, event | category | flops | bytes accessed | tf_op | source)
XLA Modules:
  0.0 74.7 jit_solution(9314458505154660403)
XLA Ops:
  0.7 0.7 reshape.19.coef_ref
  1.4 0.1 pad_add_fusion
  1.4 0.0 copy-start
  1.4 0.7 copy-done
  2.1 0.0 copy-start.1
  2.1 0.7 copy-done.1
  2.9 0.0 copy-start.2
  2.9 0.7 copy-done.2
  3.5 9.6 %scores.1 = (f32[1,4096]{1,0:T(1,128)S(1)}, f32[64,1024]{1,0:T(8,128)S(1)}, f32[64,1024]{1,0:T(8,128)S(1)}) custom-call(s32[1]{0:T(128)} %bitcast.1.place, bf16[4096,1024]{1,0:T(8,128)(2,1)} %x_ref.5, bf16[1,1024]{1,0:T(2,128)(2,1)S(1)} %reshape.19.coef_ref, s32[1,4096]{1,0:T(1,128)S(1)} %bitcast.8, s32[1,4096]{1,0:T(1,128)S(1)} %bitcast.9, ...), custom_call_target="tpu_custom_call" | custom-call | tf_op jit(solution)/shard_map/scores/pallas_call | solution.py:86
  13.2 7.9 %hessian_half.3 = (bf16[256,1024]{1,0:T(8,128)(2,1)S(1)}, f32[256,1024]{1,0:T(8,128)S(1)}) custom-call(s32[2]{0:T(128)S(1)} %get-tuple-element.21.place, bf16[4096,1024]{1,0:T(8,128)(2,1)} %x_ref.5, f32[1,4096]{1,0:T(1,128)S(1)} %get-tuple-element.10.w_ref), custom_call_target="tpu_custom_call" | custom-call | tf_op jit(solution)/shard_map/hessian_half/pallas_call | solution.py:113
  21.1 0.5 collective-permute-start.1
  21.6 0.1 collective-permute-start.6
  21.7 7.9 %hessian_half.2 = (bf16[256,1024]{1,0:T(8,128)(2,1)S(1)}, f32[256,1024]{1,0:T(8,128)S(1)}) custom-call(s32[2]{0:T(128)S(1)} %get-tuple-element.20.place, bf16[4096,1024]{1,0:T(8,128)(2,1)} %x_ref.5, f32[1,4096]{1,0:T(1,128)S(1)} %get-tuple-element.10.w_ref), custom_call_target="tpu_custom_call" | custom-call | tf_op jit(solution)/shard_map/hessian_half/pallas_call | solution.py:113
  29.6 0.5 collective-permute-start
  30.1 0.0 collective-permute-done.6
  30.2 0.0 collective-permute-done.1
  30.2 0.2 add_convert_fusion
  30.3 2.7 %collective-permute-start.2 = (bf16[256,1024]{1,0:T(8,128)(2,1)S(1)}, bf16[256,1024]{1,0:T(8,128)(2,1)S(1)}, u32[]{:S(2)}, u32[]{:S(2)}) collective-permute-start(bf16[256,1024]{1,0:T(8,128)(2,1)S(1)} %add_convert_fusion), channel_id=1, source_target_pairs={{0,2},{1,3},{2,0},{3,1},{4,6},{5,7},{6,4},{7,5},{8,10},{9,11},{10,... | collective-permute-start | bytes 1572872 | tf_op jit(solution)/shard_map/ppermute | solution.py:143
  33.0 16.2 %all-gather = bf16[256,1024]{1,0:T(8,128)(2,1)S(1)} all-gather(bf16[64,1024]{1,0:T(8,128)(2,1)S(1)} %add_convert_fusion.1), channel_id=2, replica_groups={{0,4,8,12},{1,5,9,13},{2,6,10,14},{3,7,11,15},{16,20,24,28},{17,21,25,2..., dimensions={0}, use_global_device_ids=true | all-gather | bytes 655360 | tf_op jit(solution)/shard_map/all_gather | solution.py:157
  49.2 0.1 convert_reduce_fusion
  49.3 0.6 collective-permute-start.7
  49.9 6.6 %collective-permute-done.7 = f32[64,1024]{1,0:T(8,128)} collective-permute-done((f32[64,1024]{1,0:T(8,128)S(1)}, f32[64,1024]{1,0:T(8,128)}, u32[]{:S(2)}, u32[]{:S(2)}) %collective-permute-start.7) | collective-permute-done | bytes 262176 | tf_op jit(solution)/shard_map/ppermute | solution.py:143
  56.5 1.0 %add.70 = f32[64,1024]{1,0:T(8,128)S(1)} add(f32[64,1024]{1,0:T(8,128)S(1)} %convert_reduce_fusion, f32[64,1024]{1,0:T(8,128)} %collective-permute-done.7) | non-fusion elementwise | flops 65536 | bytes 786432 | tf_op jit(solution)/shard_map/add | solution.py:170
  57.5 0.1 collective-permute-start.8
  57.5 0.0 collective-permute-done
  57.6 0.0 collective-permute-done.2
  57.6 0.2 convert_add_fusion
  57.8 0.1 dynamic-slice_convert_fusion.2
  57.9 1.2 %collective-permute-start.3 = (bf16[64,1024]{1,0:T(8,128)(2,1)S(1)}, bf16[64,1024]{1,0:T(8,128)(2,1)S(1)}, u32[]{:S(2)}, u32[]{:S(2)}) collective-permute-start(bf16[64,1024]{1,0:T(8,128)(2,1)S(1)} %get-tuple-element.17), channel_id=1, source_target_pairs={{0,4},{1,5},{2,6},{3,7},{4,0},{5,1},{6,2},{7,3},{8,12},{9,13},{10,... | collective-permute-start | bytes 393224 | tf_op jit(solution)/shard_map/ppermute | solution.py:143
  59.1 2.1 %collective-permute-start.5 = (bf16[64,1024]{1,0:T(8,128)(2,1)S(1)}, bf16[64,1024]{1,0:T(8,128)(2,1)S(1)}, u32[]{:S(2)}, u32[]{:S(2)}) collective-permute-start(bf16[64,1024]{1,0:T(8,128)(2,1)S(1)} %get-tuple-element.18), channel_id=1, source_target_pairs={{0,12},{1,13},{2,14},{3,15},{4,8},{5,9},{6,10},{7,11},{8,4},{9,5},... | collective-permute-start | bytes 393224 | tf_op jit(solution)/shard_map/ppermute | solution.py:143
  61.1 0.5 collective-permute-start.4
  61.6 0.6 constant_dynamic-slice_fusion
  62.3 0.0 collective-permute-done.8
  62.3 1.2 %fusion = f32[64,1024]{1,0:T(8,128)} fusion(f32[64,1024]{1,0:T(8,128)S(1)} %collective-permute-done.8, f32[64,1024]{1,0:T(8,128)S(1)} %add.70, s32[]{:T(128)S(6)} %select_n.51), kind=kOutput, calls=%fused_computation.6 | convolution fusion | flops 100802560 | bytes 1310724 | tf_op jit(solution)/shard_map/dot_general | solution.py:176
  63.4 0.4 collective-permute-done.3
  63.8 4.5 %collective-permute-done.5 = bf16[64,1024]{1,0:T(8,128)(2,1)S(1)} collective-permute-done((bf16[64,1024]{1,0:T(8,128)(2,1)S(1)}, bf16[64,1024]{1,0:T(8,128)(2,1)S(1)}, u32[]{:S(2)}, u32[]{:S(2)}) %collective-permute-start.5) | collective-permute-done | bytes 131104 | tf_op jit(solution)/shard_map/ppermute | solution.py:143
  68.3 5.6 %collective-permute-done.4 = bf16[64,1024]{1,0:T(8,128)(2,1)S(1)} collective-permute-done((bf16[64,1024]{1,0:T(8,128)(2,1)S(1)}, bf16[64,1024]{1,0:T(8,128)(2,1)S(1)}, u32[]{:S(2)}, u32[]{:S(2)}) %collective-permute-start.4) | collective-permute-done | bytes 131104 | tf_op jit(solution)/shard_map/ppermute | solution.py:143
  73.9 0.8 %convert_add_fusion.1 = f32[64,1024]{1,0:T(8,128)} fusion(bf16[64,1024]{1,0:T(8,128)(2,1)S(1)} %collective-permute-done.5, bf16[64,1024]{1,0:T(8,128)(2,1)S(1)} %collective-permute-done.4, bf16[64,1024]{1,0:T(8,128)(2,1)S(1)} %collective-permute-done.3, f32[256,1024]{1,0:T(8,128)S(1)} %convert_add_fusion, s32[]{:T(128)S(6)} %select_n.47), kind=kLoop, calls=%fused_computation.8 | loop fusion | flops 393216 | bytes 917508 | tf_op jit(solution)/shard_map/add | solution.py:184
  (1 shorter events, 0.0 us)
Async XLA Ops:
  1.4 0.7 copy-start
  2.1 0.7 copy-start.1
  2.9 0.7 copy-start.2
  21.1 9.1 %collective-permute-start.1 = (bf16[256,1024]{1,0:T(8,128)(2,1)S(1)}, bf16[256,1024]{1,0:T(8,128)(2,1)S(1)}, u32[]{:S(2)}, u32[]{:S(2)}) collective-permute-start(bf16[256,1024]{1,0:T(8,128)(2,1)S(1)} %get-tuple-element.14), channel_id=1, source_target_pairs={{0,1},{1,0},{2,3},{3,2},{4,5},{5,4},{6,7},{7,6},{8,9},{9,8},{10,11... | collective-permute-start | bytes 1572872 | tf_op jit(solution)/shard_map/ppermute | solution.py:143
  21.6 8.5 %collective-permute-start.6 = (f32[64,1024]{1,0:T(8,128)S(1)}, f32[64,1024]{1,0:T(8,128)S(1)}, u32[]{:S(2)}, u32[]{:S(2)}) collective-permute-start(f32[64,1024]{1,0:T(8,128)S(1)} %get-tuple-element.16), channel_id=1, source_target_pairs={{0,1},{1,0},{2,3},{3,2},{4,5},{5,4},{6,7},{7,6},{8,9},{9,8},{10,11... | collective-permute-start | bytes 786440 | tf_op jit(solution)/shard_map/ppermute | solution.py:143
  29.6 27.9 %collective-permute-start = (bf16[256,1024]{1,0:T(8,128)(2,1)S(1)}, bf16[256,1024]{1,0:T(8,128)(2,1)S(1)}, u32[]{:S(2)}, u32[]{:S(2)}) collective-permute-start(bf16[256,1024]{1,0:T(8,128)(2,1)S(1)} %get-tuple-element.12), channel_id=1, source_target_pairs={{0,1},{1,0},{2,3},{3,2},{4,5},{5,4},{6,7},{7,6},{8,9},{9,8},{10,11... | collective-permute-start | bytes 1572872 | tf_op jit(solution)/shard_map/ppermute | solution.py:143
  30.3 27.2 %collective-permute-start.2 = (bf16[256,1024]{1,0:T(8,128)(2,1)S(1)}, bf16[256,1024]{1,0:T(8,128)(2,1)S(1)}, u32[]{:S(2)}, u32[]{:S(2)}) collective-permute-start(bf16[256,1024]{1,0:T(8,128)(2,1)S(1)} %add_convert_fusion), channel_id=1, source_target_pairs={{0,2},{1,3},{2,0},{3,1},{4,6},{5,7},{6,4},{7,5},{8,10},{9,11},{10,... | collective-permute-start | bytes 1572872 | tf_op jit(solution)/shard_map/ppermute | solution.py:143
  49.3 7.2 %collective-permute-start.7 = (f32[64,1024]{1,0:T(8,128)S(1)}, f32[64,1024]{1,0:T(8,128)}, u32[]{:S(2)}, u32[]{:S(2)}) collective-permute-start(f32[64,1024]{1,0:T(8,128)S(1)} %convert_reduce_fusion), channel_id=1, source_target_pairs={{0,2},{1,3},{2,0},{3,1},{4,6},{5,7},{6,4},{7,5},{8,10},{9,11},{10,... | collective-permute-start | bytes 786440 | tf_op jit(solution)/shard_map/ppermute | solution.py:143
  57.5 4.8 %collective-permute-start.8 = (f32[64,1024]{1,0:T(8,128)S(1)}, f32[64,1024]{1,0:T(8,128)S(1)}, u32[]{:S(2)}, u32[]{:S(2)}) collective-permute-start(f32[64,1024]{1,0:T(8,128)S(1)} %add.70), channel_id=1, source_target_pairs={{0,1},{1,0},{2,3},{3,2},{4,5},{5,4},{6,7},{7,6},{8,9},{9,8},{10,11... | collective-permute-start | bytes 786440 | tf_op jit(solution)/shard_map/ppermute | solution.py:143
  57.9 5.9 %collective-permute-start.3 = (bf16[64,1024]{1,0:T(8,128)(2,1)S(1)}, bf16[64,1024]{1,0:T(8,128)(2,1)S(1)}, u32[]{:S(2)}, u32[]{:S(2)}) collective-permute-start(bf16[64,1024]{1,0:T(8,128)(2,1)S(1)} %get-tuple-element.17), channel_id=1, source_target_pairs={{0,4},{1,5},{2,6},{3,7},{4,0},{5,1},{6,2},{7,3},{8,12},{9,13},{10,... | collective-permute-start | bytes 393224 | tf_op jit(solution)/shard_map/ppermute | solution.py:143
  59.1 9.2 %collective-permute-start.5 = (bf16[64,1024]{1,0:T(8,128)(2,1)S(1)}, bf16[64,1024]{1,0:T(8,128)(2,1)S(1)}, u32[]{:S(2)}, u32[]{:S(2)}) collective-permute-start(bf16[64,1024]{1,0:T(8,128)(2,1)S(1)} %get-tuple-element.18), channel_id=1, source_target_pairs={{0,12},{1,13},{2,14},{3,15},{4,8},{5,9},{6,10},{7,11},{8,4},{9,5},... | collective-permute-start | bytes 393224 | tf_op jit(solution)/shard_map/ppermute | solution.py:143
  61.1 12.8 %collective-permute-start.4 = (bf16[64,1024]{1,0:T(8,128)(2,1)S(1)}, bf16[64,1024]{1,0:T(8,128)(2,1)S(1)}, u32[]{:S(2)}, u32[]{:S(2)}) collective-permute-start(bf16[64,1024]{1,0:T(8,128)(2,1)S(1)} %get-tuple-element.19), channel_id=1, source_target_pairs={{0,8},{1,9},{2,10},{3,11},{4,12},{5,13},{6,14},{7,15},{8,0},{9,1},... | collective-permute-start | bytes 393224 | tf_op jit(solution)/shard_map/ppermute | solution.py:143

commit v2 on v0

v2 whole, which is shorter than its diff:
```python
import functools

import jax
import jax.numpy as jnp
from jax import lax
from jax.experimental import pallas as pl
from jax.experimental.pallas import tpu as pltpu
from jax.sharding import PartitionSpec as P

BF16 = jnp.bfloat16
F32 = jnp.float32
LANES = 128
VMEM_LIMIT = 40 * 1024 * 1024


def blocks_of(x_ref, start, rows, parity, weight):
    left = []
    for block in range(x_ref.shape[1] // (2 * LANES)):
        lane = pl.multiple_of((2 * block + parity) * LANES, LANES)
        turned = x_ref[start : start + rows, pl.ds(lane, LANES)].T
        left.append((turned.astype(F32) * weight).astype(BF16))
    return jnp.concatenate(left, axis=0)


def split_by_core(blk, core, acc, send_ref, keep_ref):
    for pair in range(acc.shape[0] // (2 * blk)):
        base = pair * 2 * blk
        out = pl.ds(pair * blk, blk)
        keep_ref[out, :] = acc[pl.ds(pl.multiple_of(base + core * blk, 8), blk), :]
        send_ref[out, :] = acc[pl.ds(pl.multiple_of(base + (1 - core) * blk, 8), blk), :].astype(BF16)


def first_kernel(
    per_owner, blk, chunks, place, x_hbm, coef_hbm, label_hbm, pid_hbm, slot_hbm,
    x_ref, w_ref, sums_send, sums_keep, send_ref, keep_ref, cross_ref,
    acc, coef_ref, label_ref, pid_ref, slot_ref, x_sems, sems,
):
    core, parity = place[0], place[1]
    rows, feat = x_ref.shape
    clusters = slot_ref.shape[1]
    half = clusters // 2
    part = rows // chunks
    small = [
        pltpu.make_async_copy(source, target, sems.at[n])
        for n, (source, target) in enumerate(
            [(coef_hbm, coef_ref), (slot_hbm, slot_ref), (label_hbm, label_ref), (pid_hbm, pid_ref)]
        )
    ]
    large = [
        pltpu.make_async_copy(x_hbm.at[pl.ds(n * part, part)], x_ref.at[pl.ds(n * part, part)], x_sems.at[n])
        for n in range(chunks)
    ]
    for copy in small:
        copy.start()
    for copy in large:
        copy.start()
    for copy in small:
        copy.wait()
    row = lax.broadcasted_iota(jnp.int32, (clusters, clusters), 0)
    mine = row >= half
    inner = jnp.where(mine, row - half, row)
    slot = (2 * (inner // per_owner) + jnp.where(mine, core, 1 - core)) * per_owner + inner % per_owner
    passage = lax.broadcasted_iota(jnp.int32, (clusters, clusters), 1)
    names = jnp.sum(jnp.where(slot_ref[...] == slot, passage, 0), axis=1, keepdims=True)
    coef = jnp.broadcast_to(coef_ref[...].reshape(1, feat), (16, feat))
    for n in range(chunks):
        start = n * part
        here = slice(start, start + part)
        large[n].wait()
        x = x_ref[here, :]
        logits = lax.dot_general(coef, x, (((1,), (1,)), ((), ())), preferred_element_type=F32)[0:1]
        prob = 1.0 / (1.0 + jnp.exp(-logits))
        weight = prob * (1.0 - prob)
        w_ref[:, here] = weight
        score = label_ref[:, here].astype(F32) - prob
        score = jnp.broadcast_to(score, (LANES, part)).T
        scored = (x.astype(F32) * jnp.concatenate([score] * (feat // LANES), axis=1)).astype(BF16)
        member = jnp.where(pid_ref[:, here] == names, 1.0, 0.0).astype(BF16)
        sums = jnp.dot(member, scored, preferred_element_type=F32)
        term = jnp.dot(blocks_of(x_ref, start, part, 1 - parity, weight), x, preferred_element_type=F32)
        if n:
            sums_send[...] += sums[:half]
            sums_keep[...] += sums[half:]
            acc[...] += term
        else:
            sums_send[...] = sums[:half]
            sums_keep[...] = sums[half:]
            acc[...] = term
    split_by_core(blk, core, acc, send_ref, keep_ref)
    for block in range(feat // (2 * LANES)):
        lane = pl.multiple_of((2 * block + parity) * LANES, LANES)
        cross_ref[:, block * LANES : (block + 1) * LANES] = acc[:, pl.ds(lane, LANES)]


def second_kernel(blk, chunks, place, x_ref, w_ref, cross_ref, send_ref, keep_ref, acc):
    core, parity = place[0], place[1]
    rows, feat = x_ref.shape
    part = rows // chunks
    width = feat // (2 * LANES)
    total = None
    for n in range(chunks):
        start = n * part
        right = jnp.concatenate(
            [
                x_ref[start : start + part, pl.ds(pl.multiple_of((2 * b + parity) * LANES, LANES), LANES)]
                for b in range(width)
            ],
            axis=1,
        )
        left = blocks_of(x_ref, start, part, parity, w_ref[:, start : start + part])
        term = jnp.dot(left, right, preferred_element_type=F32)
        total = term if total is None else total + term
    turned = cross_ref[...].T
    for b in range(width):
        own = pl.multiple_of((2 * b + parity) * LANES, LANES)
        other = pl.multiple_of((2 * b + 1 - parity) * LANES, LANES)
        acc[:, pl.ds(own, LANES)] = total[:, b * LANES : (b + 1) * LANES]
        acc[:, pl.ds(other, LANES)] = turned[:, b * LANES : (b + 1) * LANES]
    split_by_core(blk, core, acc, send_ref, keep_ref)


VMEM_SPEC = pl.BlockSpec(memory_space=pltpu.VMEM)


def first(place, x, coef, labels, pid, slot_of, per_owner, blk, chunks=4):
    rows, feat = x.shape
    clusters = slot_of.shape[0]
    hbm = pl.BlockSpec(memory_space=pltpu.HBM)
    shape = jax.ShapeDtypeStruct
    return pl.pallas_call(
        functools.partial(first_kernel, per_owner, blk, chunks),
        in_specs=[pl.BlockSpec(memory_space=pltpu.SMEM)] + [hbm] * 5,
        out_specs=[VMEM_SPEC] * 7,
        out_shape=[
            shape((rows, feat), BF16),
            shape((1, rows), F32),
            shape((clusters // 2, feat), F32),
            shape((clusters // 2, feat), F32),
            shape((feat // 4, feat), BF16),
            shape((feat // 4, feat), F32),
            shape((feat // 2, feat // 2), F32),
        ],
        scratch_shapes=[
            pltpu.VMEM((feat // 2, feat), F32),
            pltpu.VMEM((feat,), BF16),
            pltpu.VMEM((1, rows), jnp.int32),
            pltpu.VMEM((1, rows), jnp.int32),
            pltpu.VMEM((1, clusters), jnp.int32),
            pltpu.SemaphoreType.DMA((chunks,)),
            pltpu.SemaphoreType.DMA((4,)),
        ],
        compiler_params=pltpu.CompilerParams(vmem_limit_bytes=VMEM_LIMIT),
        name="scores_and_far",
    )(place, x, coef, labels.reshape(1, rows), pid.reshape(1, rows), slot_of.reshape(1, clusters))


def second(place, x, w, cross, blk, chunks=4):
    rows, feat = x.shape
    return pl.pallas_call(
        functools.partial(second_kernel, blk, chunks),
        in_specs=[pl.BlockSpec(memory_space=pltpu.SMEM)] + [VMEM_SPEC] * 3,
        out_specs=[VMEM_SPEC] * 2,
        out_shape=[
            jax.ShapeDtypeStruct((feat // 4, feat), BF16),
            jax.ShapeDtypeStruct((feat // 4, feat), F32),
        ],
        scratch_shapes=[pltpu.VMEM((feat // 2, feat), F32)],
        compiler_params=pltpu.CompilerParams(vmem_limit_bytes=VMEM_LIMIT),
        name="near",
    )(place, x, w, cross)


def local(features, coef, labels, passage_id, slot_of):
    feat = features.shape[1]
    devices = lax.axis_size("rows")
    clusters = slot_of.shape[0]
    per_owner = clusters // devices
    blk = feat // devices
    me = lax.axis_index("rows")
    turn = LANES // blk
    core, parity = me % 2, (me // turn) % 2

    def swap(array, mask):
        return lax.ppermute(array, "rows", [(i, i ^ mask) for i in range(devices)])

    def rest(number):
        return (number // (2 * turn)) * (turn // 2) + (number % turn) // 2

    place = jnp.stack([core, parity])
    x, w, sums_send, sums_keep, far_send, far_keep, cross = first(
        place, features, coef, labels, passage_id, slot_of, per_owner, blk
    )
    masks = [m for m in range(1, devices) if not m & 1 and not m & turn]
    mine = rest(me)
    far = (far_keep + swap(far_send, 1).astype(F32)).astype(BF16)
    sums = sums_keep + swap(sums_send, 1)
    arrived = swap(far, turn)
    sums_out = sums.astype(BF16)
    sums_in = [swap(sums_out, m) for m in masks]
    near_send, near_keep = second(place, x, w, cross, blk)
    near = near_keep + swap(near_send, 1).astype(F32) + arrived.astype(F32)
    block = lambda n: lax.dynamic_slice_in_dim(near, n * blk, blk, 0)
    hessian = block(mine)
    parts = [swap(block(mine ^ rest(m)).astype(BF16), m) for m in masks]

    for part in sums_in:
        sums = sums + part.astype(F32)
    sums = sums + swap(sums, turn)
    other = swap(sums, 1)
    chip = me // 2
    grad_local = lax.dynamic_slice_in_dim(sums, chip * per_owner, per_owner, 0)
    stack = jnp.concatenate([sums, other], axis=0)
    columns = lax.dynamic_slice_in_dim(stack, me * blk, blk, 1)
    meat = lax.dot_general(
        columns,
        stack,
        (((0,), (0,)), ((), ())),
        precision=lax.Precision.HIGHEST,
        preferred_element_type=F32,
    )
    for part in parts:
        hessian = hessian + part.astype(F32)
    return (hessian, meat, grad_local)


def solution(mesh):
    in_specs = (
        P(("groups", "rows"), None),
        P(),
        P(("groups", "rows")),
        P(("groups", "rows"), None),
        P("groups"),
    )
    out_specs = (
        P(("groups", "rows"), None),
        P(("groups", "rows"), None),
        P(("groups", "rows"), None),
    )
    return jax.shard_map(local, mesh=mesh, in_specs=in_specs, out_specs=out_specs, check_vma=False)
```

time: 576 us -> 63.7 us (0.11)
  waiting for transfers between devices: 439 us -> 25.2 us
  other arithmetic: 37.8 us -> 2.32 us
  matrix products: 34.1 us -> 1.18 us
  local copies, waits for them, and re-layouts: 36.3 us -> 3.44 us
  Pallas kernels: 0 us -> 16.3 us
  between operations: 14.2 us -> 0.76 us
    all_to_all x2 -> x0, waiting for transfers between devices: 301 us -> none  [the longest x1 301 us: local(): lax.all_to_all(outgoing.reshape(devices, capacity, feat_dim), 'rows', spl...]
    reduce_scatter x1 -> x0, waiting for transfers between devices: 138 us -> none  [local(): lax.psum_scatter(lax.dot_general(grad_local, grad_local, (((0,), (0,)), (...]
    dot_general x4 -> x1, matrix products: 34.1 us -> 1.18 us  [local(): lax.dot_general(columns, stack, (((0,), (0,)), ((), ())), precision=lax.P...]
    scatter x1 -> x0, other arithmetic: 29.7 us -> none  [local(): jnp.zeros((devices * capacity, feat_dim), jnp.bfloat16).at[target]]
    scatter x1 -> x0, local copies, waits for them, and re-layouts: 28.6 us -> none  [local(): tag_out = jnp.full((devices * capacity,), -1.0, jnp.bfloat16).at[target]....]
    ppermute x0 -> x12, waiting for transfers between devices: none -> 25.2 us  [swap(): return lax.ppermute(array, 'rows', [(i, i ^ mask) for i in range(devices)])]
    pallas_call x0 -> x2, Pallas kernels: none -> 16.3 us  [the longest x1 12.9 us: first(): pl.pallas_call(functools.partial(first_kernel, per_owner, blk, chunks), i...]
    ppermute x0 -> x12, starting transfers between devices: none -> 14.2 us  [swap(): return lax.ppermute(array, 'rows', [(i, i ^ mask) for i in range(devices)])]
  transfers between devices with their start and end apart: 4 -> 12, of which waited for: 2 -> 5; matrix products, arithmetic and copies ran while one was open for 12% -> 5% of each run, Pallas kernels for 0% -> 5%
where the time goes in v2:
time: 63.7 us; the launch traced here: 63.4 us
  waiting for transfers between devices  25.2 us (40%)
  Pallas kernels  16.3 us (26%)
  starting transfers between devices  14.2 us (22%)
  local copies, waits for them, and re-layouts  3.44 us (5%)
  other arithmetic  2.32 us (4%)
  matrix products  1.18 us (2%)
  between operations  0.76 us (1%)
    ppermute x12, waiting for transfers between devices, swap(): return lax.ppermute(array, 'rows', [(i, i ^ mask) for i in range(devices)])  25.2 us
    ppermute x12, starting transfers between devices, swap(): return lax.ppermute(array, 'rows', [(i, i ^ mask) for i in range(devices)])  14.2 us
    pallas_call x1, Pallas kernels, first(): pl.pallas_call(functools.partial(first_kernel, per_owner, blk, chunks), i...  12.9 us
    pallas_call x1, Pallas kernels, second(): pl.pallas_call(functools.partial(second_kernel, blk, chunks), in_specs=[p...  3.31 us
    unnamed x8, local copies, waits for them, and re-layouts  2.77 us
  transfers between devices with their start and end apart: 12, of which 5 were waited for; matrix products, arithmetic and copies ran while one was open for 5% of the time, Pallas kernels for 5%

profile of v2, /device:TPU:0, one launch (start us, length us, event | category | flops | bytes accessed | tf_op | source)
XLA Modules:
  0.0 63.4 jit_solution(15839705567871339995)
XLA Ops:
  0.7 0.1 pad_add_fusion.place
  0.7 0.0 copy-start
  0.7 0.7 %copy-done = s32[4096]{0:T(1024)S(1)} copy-done((s32[4096]{0:T(1024)S(1)}, s32[4096]{0:T(1024)}, u32[]{:S(2)}) %copy-start) | copy-done | bytes 16408
  1.5 0.0 copy-start.1
  1.5 0.7 %copy-done.1 = s32[4096,1]{0,1:T(1,128)S(1)} copy-done((s32[4096,1]{0,1:T(1,128)S(1)}, s32[4096,1]{0,1:T(1,128)}, u32[]{:S(2)}) %copy-start.1) | copy-done | bytes 16408
  2.2 0.0 copy-start.2
  2.2 0.7 %copy-done.2 = bf16[1024]{0:T(1024)(128)(2,1)S(1)} copy-done((bf16[1024]{0:T(1024)(128)(2,1)S(1)}, bf16[1024]{0:T(1024)(128)(2,1)}, u32[]{:S(2)}) %copy-start.2) | copy-done | bytes 2072
  2.9 0.0 copy-start.3
  2.9 0.7 %copy-done.3 = s32[128]{0:T(128)S(1)} copy-done((s32[128]{0:T(128)S(1)}, s32[128]{0:T(128)}, u32[]{:S(2)}) %copy-start.3) | copy-done | bytes 536
  3.5 12.9 %scores_and_far.1 = (bf16[4096,1024]{1,0:T(8,128)(2,1)S(1)}, f32[1,4096]{1,0:T(1,128)S(1)}, f32[64,1024]{1,0:T(8,128)S(1)}, f32[64,1024]{1,0:T(8,128)S(1)}, bf16...) custom-call(s32[2]{0:T(128)S(1)} %pad_add_fusion.place, bf16[4096,1024]{1,0:T(8,128)(2,1)} %x_hbm.1, ...), custom_call_target="tpu_custom_call" | custom-call | tf_op jit(solution)/shard_map/scores_and_far/pallas_call | solution.py:130
  16.5 0.5 collective-permute-start.1
  17.0 0.1 collective-permute-start.6
  17.1 3.3 %near.1 = (bf16[256,1024]{1,0:T(8,128)(2,1)S(1)}, f32[256,1024]{1,0:T(8,128)S(1)}) custom-call(s32[2]{0:T(128)S(1)} %pad_add_fusion.place, bf16[4096,1024]{1,0:T(8,128)(2,1)S(1)} %get-tuple-element.12.x_ref, f32[1,4096]{1,0:T(1,128)S(1)} %get-tuple-element.13.w_ref, f32[512,512]{1,0:T(8,128)S(1)} %get-tuple-element.14.cross_ref), custom_call_target="tpu_custom_call" | custom-call | tf_op jit(solution)/shard_map/near/pallas_call | solution.py:159
  20.4 0.5 collective-permute-start
  20.9 0.0 collective-permute-done.6
  20.9 4.7 %collective-permute-start.9 = (bf16[64,1024]{1,0:T(8,128)(2,1)S(1)}, bf16[64,1024]{1,0:T(8,128)(2,1)S(1)}, u32[]{:S(2)}, u32[]{:S(2)}) collective-permute-start(bf16[64,1024]{1,0:T(8,128)(2,1)S(1)} %get-tuple-element.21), channel_id=1, source_target_pairs={{0,12},{1,13},{2,14},{3,15},{4,8},{5,9},{6,10},{7,11},{8,4},{9,5},... | collective-permute-start | bytes 393224 | tf_op jit(solution)/shard_map/ppermute | solution.py:184
  25.7 0.0 collective-permute-start.8
  25.7 0.6 %collective-permute-start.7 = (bf16[64,1024]{1,0:T(8,128)(2,1)S(1)}, bf16[64,1024]{1,0:T(8,128)(2,1)S(1)}, u32[]{:S(2)}, u32[]{:S(2)}) collective-permute-start(bf16[64,1024]{1,0:T(8,128)(2,1)S(1)} %get-tuple-element.21), channel_id=1, source_target_pairs={{0,4},{1,5},{2,6},{3,7},{4,0},{5,1},{6,2},{7,3},{8,12},{9,13},{10,... | collective-permute-start | bytes 393224 | tf_op jit(solution)/shard_map/ppermute | solution.py:184
  26.3 0.0 collective-permute-done.1
  26.3 0.2 add_convert_fusion
  26.5 1.6 %collective-permute-start.2 = (bf16[256,1024]{1,0:T(8,128)(2,1)S(1)}, bf16[256,1024]{1,0:T(8,128)(2,1)S(1)}, u32[]{:S(2)}, u32[]{:S(2)}) collective-permute-start(bf16[256,1024]{1,0:T(8,128)(2,1)S(1)} %add_convert_fusion), channel_id=1, source_target_pairs={{0,2},{1,3},{2,0},{3,1},{4,6},{5,7},{6,4},{7,5},{8,10},{9,11},{10,... | collective-permute-start | bytes 1572872 | tf_op jit(solution)/shard_map/ppermute | solution.py:184
  28.1 2.0 %collective-permute-done.9 = bf16[64,1024]{1,0:T(8,128)(2,1)S(1)} collective-permute-done((bf16[64,1024]{1,0:T(8,128)(2,1)S(1)}, bf16[64,1024]{1,0:T(8,128)(2,1)S(1)}, u32[]{:S(2)}, u32[]{:S(2)}) %collective-permute-start.9) | collective-permute-done | bytes 131104 | tf_op jit(solution)/shard_map/ppermute | solution.py:184
  30.1 7.2 %collective-permute-done.8 = bf16[64,1024]{1,0:T(8,128)(2,1)S(1)} collective-permute-done((bf16[64,1024]{1,0:T(8,128)(2,1)S(1)}, bf16[64,1024]{1,0:T(8,128)(2,1)S(1)}, u32[]{:S(2)}, u32[]{:S(2)}) %collective-permute-start.8) | collective-permute-done | bytes 131104 | tf_op jit(solution)/shard_map/ppermute | solution.py:184
  37.4 0.0 collective-permute-done.7
  37.4 0.1 convert_add_fusion.1
  37.4 1.5 %collective-permute-start.10 = (f32[64,1024]{1,0:T(8,128)S(1)}, f32[64,1024]{1,0:T(8,128)}, u32[]{:S(2)}, u32[]{:S(2)}) collective-permute-start(f32[64,1024]{1,0:T(8,128)S(1)} %convert_add_fusion.1), channel_id=1, source_target_pairs={{0,2},{1,3},{2,0},{3,1},{4,6},{5,7},{6,4},{7,5},{8,10},{9,11},{10,... | collective-permute-start | bytes 786440 | tf_op jit(solution)/shard_map/ppermute | solution.py:184
  38.9 7.1 %collective-permute-done.10 = f32[64,1024]{1,0:T(8,128)} collective-permute-done((f32[64,1024]{1,0:T(8,128)S(1)}, f32[64,1024]{1,0:T(8,128)}, u32[]{:S(2)}, u32[]{:S(2)}) %collective-permute-start.10) | collective-permute-done | bytes 262176 | tf_op jit(solution)/shard_map/ppermute | solution.py:184
  46.0 1.0 %add.82 = f32[64,1024]{1,0:T(8,128)S(1)} add(f32[64,1024]{1,0:T(8,128)S(1)} %convert_add_fusion.1, f32[64,1024]{1,0:T(8,128)} %collective-permute-done.10) | non-fusion elementwise | flops 65536 | bytes 786432 | tf_op jit(solution)/shard_map/add | solution.py:208
  47.0 0.1 collective-permute-start.11
  47.1 0.0 collective-permute-done
  47.1 0.0 collective-permute-done.2
  47.1 0.2 convert_add_fusion
  47.3 0.1 dynamic-slice_convert_fusion.2
  47.4 3.5 %collective-permute-start.5 = (bf16[64,1024]{1,0:T(8,128)(2,1)S(1)}, bf16[64,1024]{1,0:T(8,128)(2,1)S(1)}, u32[]{:S(2)}, u32[]{:S(2)}) collective-permute-start(bf16[64,1024]{1,0:T(8,128)(2,1)S(1)} %get-tuple-element.24), channel_id=1, source_target_pairs={{0,12},{1,13},{2,14},{3,15},{4,8},{5,9},{6,10},{7,11},{8,4},{9,5},... | collective-permute-start | bytes 393224 | tf_op jit(solution)/shard_map/ppermute | solution.py:184
  50.9 0.0 collective-permute-start.4
  50.9 0.9 %collective-permute-start.3 = (bf16[64,1024]{1,0:T(8,128)(2,1)S(1)}, bf16[64,1024]{1,0:T(8,128)(2,1)S(1)}, u32[]{:S(2)}, u32[]{:S(2)}) collective-permute-start(bf16[64,1024]{1,0:T(8,128)(2,1)S(1)} %get-tuple-element.23), channel_id=1, source_target_pairs={{0,4},{1,5},{2,6},{3,7},{4,0},{5,1},{6,2},{7,3},{8,12},{9,13},{10,... | collective-permute-start | bytes 393224 | tf_op jit(solution)/shard_map/ppermute | solution.py:184
  51.8 0.6 constant_dynamic-slice_fusion
  52.5 0.0 collective-permute-done.11
  52.5 1.2 %fusion = f32[64,1024]{1,0:T(8,128)} fusion(f32[64,1024]{1,0:T(8,128)S(1)} %collective-permute-done.11, f32[64,1024]{1,0:T(8,128)S(1)} %add.82, s32[]{:T(128)S(6)} %select_n.51), kind=kOutput, calls=%fused_computation.5 | convolution fusion | flops 100802560 | bytes 1310724 | tf_op jit(solution)/shard_map/dot_general | solution.py:214
  53.6 2.0 %collective-permute-done.5 = bf16[64,1024]{1,0:T(8,128)(2,1)S(1)} collective-permute-done((bf16[64,1024]{1,0:T(8,128)(2,1)S(1)}, bf16[64,1024]{1,0:T(8,128)(2,1)S(1)}, u32[]{:S(2)}, u32[]{:S(2)}) %collective-permute-start.5) | collective-permute-done | bytes 131104 | tf_op jit(solution)/shard_map/ppermute | solution.py:184
  55.6 6.9 %collective-permute-done.4 = bf16[64,1024]{1,0:T(8,128)(2,1)S(1)} collective-permute-done((bf16[64,1024]{1,0:T(8,128)(2,1)S(1)}, bf16[64,1024]{1,0:T(8,128)(2,1)S(1)}, u32[]{:S(2)}, u32[]{:S(2)}) %collective-permute-start.4) | collective-permute-done | bytes 131104 | tf_op jit(solution)/shard_map/ppermute | solution.py:184
  62.6 0.0 collective-permute-done.3
  62.6 0.8 %convert_add_fusion.2 = f32[64,1024]{1,0:T(8,128)} fusion(bf16[64,1024]{1,0:T(8,128)(2,1)S(1)} %collective-permute-done.5, bf16[64,1024]{1,0:T(8,128)(2,1)S(1)} %collective-permute-done.4, bf16[64,1024]{1,0:T(8,128)(2,1)S(1)} %collective-permute-done.3, f32[256,1024]{1,0:T(8,128)S(1)} %convert_add_fusion, s32[]{:T(128)S(6)} %select_n.47), kind=kLoop, calls=%fused_computation.7 | loop fusion | flops 393216 | bytes 917508 | tf_op jit(solution)/shard_map/add | solution.py:222
  (1 shorter events, 0.0 us)
Async XLA Ops:
  0.7 0.7 %copy-start = (s32[4096]{0:T(1024)S(1)}, s32[4096]{0:T(1024)}, u32[]{:S(2)}) copy-start(s32[4096]{0:T(1024)} %param.7) | copy-start | bytes 49156
  1.5 0.7 %copy-start.1 = (s32[4096,1]{0,1:T(1,128)S(1)}, s32[4096,1]{0,1:T(1,128)}, u32[]{:S(2)}) copy-start(s32[4096,1]{0,1:T(1,128)} %param.8) | copy-start | bytes 49156
  2.2 0.7 %copy-start.2 = (bf16[1024]{0:T(1024)(128)(2,1)S(1)}, bf16[1024]{0:T(1024)(128)(2,1)}, u32[]{:S(2)}) copy-start(bf16[1024]{0:T(1024)(128)(2,1)} %coef_hbm.1) | copy-start | bytes 6148
  2.9 0.7 %copy-start.3 = (s32[128]{0:T(128)S(1)}, s32[128]{0:T(128)}, u32[]{:S(2)}) copy-start(s32[128]{0:T(128)} %param.9) | copy-start | bytes 1540
  16.5 9.9 %collective-permute-start.1 = (bf16[256,1024]{1,0:T(8,128)(2,1)S(1)}, bf16[256,1024]{1,0:T(8,128)(2,1)S(1)}, u32[]{:S(2)}, u32[]{:S(2)}) collective-permute-start(bf16[256,1024]{1,0:T(8,128)(2,1)S(1)} %get-tuple-element.18), channel_id=1, source_target_pairs={{0,1},{1,0},{2,3},{3,2},{4,5},{5,4},{6,7},{7,6},{8,9},{9,8},{10,11... | collective-permute-start | bytes 1572872 | tf_op jit(solution)/shard_map/ppermute | solution.py:184
  17.0 3.9 %collective-permute-start.6 = (f32[64,1024]{1,0:T(8,128)S(1)}, f32[64,1024]{1,0:T(8,128)S(1)}, u32[]{:S(2)}, u32[]{:S(2)}) collective-permute-start(f32[64,1024]{1,0:T(8,128)S(1)} %get-tuple-element.20), channel_id=1, source_target_pairs={{0,1},{1,0},{2,3},{3,2},{4,5},{5,4},{6,7},{7,6},{8,9},{9,8},{10,11... | collective-permute-start | bytes 786440 | tf_op jit(solution)/shard_map/ppermute | solution.py:184
  20.4 26.7 %collective-permute-start = (bf16[256,1024]{1,0:T(8,128)(2,1)S(1)}, bf16[256,1024]{1,0:T(8,128)(2,1)S(1)}, u32[]{:S(2)}, u32[]{:S(2)}) collective-permute-start(bf16[256,1024]{1,0:T(8,128)(2,1)S(1)} %get-tuple-element.16), channel_id=1, source_target_pairs={{0,1},{1,0},{2,3},{3,2},{4,5},{5,4},{6,7},{7,6},{8,9},{9,8},{10,11... | collective-permute-start | bytes 1572872 | tf_op jit(solution)/shard_map/ppermute | solution.py:184
  20.9 9.2 %collective-permute-start.9 = (bf16[64,1024]{1,0:T(8,128)(2,1)S(1)}, bf16[64,1024]{1,0:T(8,128)(2,1)S(1)}, u32[]{:S(2)}, u32[]{:S(2)}) collective-permute-start(bf16[64,1024]{1,0:T(8,128)(2,1)S(1)} %get-tuple-element.21), channel_id=1, source_target_pairs={{0,12},{1,13},{2,14},{3,15},{4,8},{5,9},{6,10},{7,11},{8,4},{9,5},... | collective-permute-start | bytes 393224 | tf_op jit(solution)/shard_map/ppermute | solution.py:184
  25.7 11.7 %collective-permute-start.8 = (bf16[64,1024]{1,0:T(8,128)(2,1)S(1)}, bf16[64,1024]{1,0:T(8,128)(2,1)S(1)}, u32[]{:S(2)}, u32[]{:S(2)}) collective-permute-start(bf16[64,1024]{1,0:T(8,128)(2,1)S(1)} %get-tuple-element.21), channel_id=1, source_target_pairs={{0,8},{1,9},{2,10},{3,11},{4,12},{5,13},{6,14},{7,15},{8,0},{9,1},... | collective-permute-start | bytes 393224 | tf_op jit(solution)/shard_map/ppermute | solution.py:184
  25.7 11.7 %collective-permute-start.7 = (bf16[64,1024]{1,0:T(8,128)(2,1)S(1)}, bf16[64,1024]{1,0:T(8,128)(2,1)S(1)}, u32[]{:S(2)}, u32[]{:S(2)}) collective-permute-start(bf16[64,1024]{1,0:T(8,128)(2,1)S(1)} %get-tuple-element.21), channel_id=1, source_target_pairs={{0,4},{1,5},{2,6},{3,7},{4,0},{5,1},{6,2},{7,3},{8,12},{9,13},{10,... | collective-permute-start | bytes 393224 | tf_op jit(solution)/shard_map/ppermute | solution.py:184
  26.5 20.6 %collective-permute-start.2 = (bf16[256,1024]{1,0:T(8,128)(2,1)S(1)}, bf16[256,1024]{1,0:T(8,128)(2,1)S(1)}, u32[]{:S(2)}, u32[]{:S(2)}) collective-permute-start(bf16[256,1024]{1,0:T(8,128)(2,1)S(1)} %add_convert_fusion), channel_id=1, source_target_pairs={{0,2},{1,3},{2,0},{3,1},{4,6},{5,7},{6,4},{7,5},{8,10},{9,11},{10,... | collective-permute-start | bytes 1572872 | tf_op jit(solution)/shard_map/ppermute | solution.py:184
  37.4 8.6 %collective-permute-start.10 = (f32[64,1024]{1,0:T(8,128)S(1)}, f32[64,1024]{1,0:T(8,128)}, u32[]{:S(2)}, u32[]{:S(2)}) collective-permute-start(f32[64,1024]{1,0:T(8,128)S(1)} %convert_add_fusion.1), channel_id=1, source_target_pairs={{0,2},{1,3},{2,0},{3,1},{4,6},{5,7},{6,4},{7,5},{8,10},{9,11},{10,... | collective-permute-start | bytes 786440 | tf_op jit(solution)/shard_map/ppermute | solution.py:184
  47.0 5.5 %collective-permute-start.11 = (f32[64,1024]{1,0:T(8,128)S(1)}, f32[64,1024]{1,0:T(8,128)S(1)}, u32[]{:S(2)}, u32[]{:S(2)}) collective-permute-start(f32[64,1024]{1,0:T(8,128)S(1)} %add.82), channel_id=1, source_target_pairs={{0,1},{1,0},{2,3},{3,2},{4,5},{5,4},{6,7},{7,6},{8,9},{9,8},{10,11... | collective-permute-start | bytes 786440 | tf_op jit(solution)/shard_map/ppermute | solution.py:184
  47.4 8.3 %collective-permute-start.5 = (bf16[64,1024]{1,0:T(8,128)(2,1)S(1)}, bf16[64,1024]{1,0:T(8,128)(2,1)S(1)}, u32[]{:S(2)}, u32[]{:S(2)}) collective-permute-start(bf16[64,1024]{1,0:T(8,128)(2,1)S(1)} %get-tuple-element.24), channel_id=1, source_target_pairs={{0,12},{1,13},{2,14},{3,15},{4,8},{5,9},{6,10},{7,11},{8,4},{9,5},... | collective-permute-start | bytes 393224 | tf_op jit(solution)/shard_map/ppermute | solution.py:184
  50.9 11.7 %collective-permute-start.4 = (bf16[64,1024]{1,0:T(8,128)(2,1)S(1)}, bf16[64,1024]{1,0:T(8,128)(2,1)S(1)}, u32[]{:S(2)}, u32[]{:S(2)}) collective-permute-start(bf16[64,1024]{1,0:T(8,128)(2,1)S(1)} %get-tuple-element.25), channel_id=1, source_target_pairs={{0,8},{1,9},{2,10},{3,11},{4,12},{5,13},{6,14},{7,15},{8,0},{9,1},... | collective-permute-start | bytes 393224 | tf_op jit(solution)/shard_map/ppermute | solution.py:184
  50.9 11.7 %collective-permute-start.3 = (bf16[64,1024]{1,0:T(8,128)(2,1)S(1)}, bf16[64,1024]{1,0:T(8,128)(2,1)S(1)}, u32[]{:S(2)}, u32[]{:S(2)}) collective-permute-start(bf16[64,1024]{1,0:T(8,128)(2,1)S(1)} %get-tuple-element.23), channel_id=1, source_target_pairs={{0,4},{1,5},{2,6},{3,7},{4,0},{5,1},{6,2},{7,3},{8,12},{9,13},{10,... | collective-permute-start | bytes 393224 | tf_op jit(solution)/shard_map/ppermute | solution.py:184

commit v3 on v2

v3 whole, which is shorter than its diff:
```python
import functools

import jax
import jax.numpy as jnp
from jax import lax
from jax.experimental import pallas as pl
from jax.experimental.pallas import tpu as pltpu
from jax.sharding import PartitionSpec as P

BF16 = jnp.bfloat16
F32 = jnp.float32
LANES = 128
VMEM_LIMIT = 28 * 1024 * 1024


def turned_block(x_ref, here, lane, weight):
    return (x_ref[here, pl.ds(lane, LANES)].T.astype(F32) * weight).astype(BF16)


def lane_of(block, parity):
    return pl.multiple_of((2 * block + parity) * LANES, LANES)


def core_rows(blk, core, pairs):
    for pair in range(pairs):
        base = 2 * pair * blk
        yield pl.ds(pair * blk, blk), [
            pl.ds(pl.multiple_of(base + number * blk, 16), blk) for number in (core, 1 - core)
        ]


def first_kernel(
    per_owner, blk, chunks, place, x_hbm, coef_hbm, label_hbm, pid_hbm, slot_hbm,
    x_ref, w_ref, sums_send, sums_keep, send_ref, keep_ref,
    left, send_acc, coef_ref, label_ref, pid_ref, slot_ref, x_sems, sems,
):
    core, parity = place[0], place[1]
    rows, feat = x_ref.shape
    clusters = slot_ref.shape[1]
    half = clusters // 2
    starts = [rows * sum(chunks[:n]) // sum(chunks) for n in range(len(chunks) + 1)]
    spans = [slice(a, b) for a, b in zip(starts, starts[1:])]
    small = [
        pltpu.make_async_copy(source, target, sems.at[n])
        for n, (source, target) in enumerate(
            [(coef_hbm, coef_ref), (slot_hbm, slot_ref), (label_hbm, label_ref), (pid_hbm, pid_ref)]
        )
    ]
    large = [
        pltpu.make_async_copy(x_hbm.at[here], x_ref.at[here], x_sems.at[n])
        for n, here in enumerate(spans)
    ]
    for copy in small:
        copy.start()
    for copy in large:
        copy.start()
    for copy in small:
        copy.wait()
    row = lax.broadcasted_iota(jnp.int32, (clusters, clusters), 0)
    mine = row >= half
    inner = jnp.where(mine, row - half, row)
    slot = (2 * (inner // per_owner) + jnp.where(mine, core, 1 - core)) * per_owner + inner % per_owner
    passage = lax.broadcasted_iota(jnp.int32, (clusters, clusters), 1)
    names = jnp.sum(jnp.where(slot_ref[...] == slot, passage, 0), axis=1, keepdims=True)
    coef = jnp.broadcast_to(coef_ref[...].reshape(1, feat), (16, feat))
    def probabilities(n):
        here = spans[n]
        large[n].wait()
        logits = lax.dot_general(coef, x_ref[here, :], (((1,), (1,)), ((), ())), preferred_element_type=F32)[0:1]
        prob = 1.0 / (1.0 + jnp.exp(-logits))
        return prob * (1.0 - prob), label_ref[:, here].astype(F32) - prob

    def use(n, weight, score):
        here = spans[n]
        w_ref[:, here] = weight
        score = jnp.broadcast_to(score, (LANES, here.stop - here.start)).T
        score = jnp.concatenate([score] * (feat // LANES), axis=1)
        scored = (x_ref[here, :].astype(F32) * score).astype(BF16)
        member = jnp.where(pid_ref[:, here] == names, 1.0, 0.0).astype(BF16)
        sums = jnp.dot(member, scored, preferred_element_type=F32)
        for block in range(feat // (2 * LANES)):
            turned = turned_block(x_ref, here, lane_of(block, 1 - parity), weight)
            for pair in range(LANES // (2 * blk)):
                out = (block * LANES // (2 * blk) + pair) * blk
                for number in range(2):
                    start = out + jnp.where(core == number, 0, feat // 4)
                    at = (2 * pair + number) * blk
                    left[pl.ds(pl.multiple_of(start, 16), blk), here] = turned[at : at + blk]
        add(sums_send, sums[:half], n)
        add(sums_keep, sums[half:], n)

    def add(ref, term, n):
        if n:
            ref[...] += term
        else:
            ref[...] = term

    def multiply(n):
        term = jnp.dot(left[:, spans[n]], x_ref[spans[n], :], preferred_element_type=F32)
        add(keep_ref, term[: feat // 4], n)
        if n < len(spans) - 1:
            add(send_acc, term[feat // 4 :], n)
        else:
            term = term[feat // 4 :]
            send_ref[...] = (term + send_acc[...] if n else term).astype(BF16)

    held = probabilities(0)
    for n in range(len(spans)):
        ahead = probabilities(n + 1) if n + 1 < len(spans) else None
        use(n, *held)
        multiply(n)
        held = ahead


def second_kernel(blk, chunks, place, x_ref, w_ref, far_send, far_keep, send_ref, keep_ref, acc, cross):
    core, parity = place[0], place[1]
    rows, feat = x_ref.shape
    part = rows // chunks
    width = feat // (2 * LANES)
    for packed, (kept, sent) in core_rows(blk, core, feat // (4 * blk)):
        for b in range(width):
            lanes, lane = slice(b * LANES, (b + 1) * LANES), pl.ds(lane_of(b, parity), LANES)
            cross[kept, lanes] = far_keep[packed, lane]
            cross[sent, lanes] = far_send[packed, lane].astype(F32)
    total = None
    for n in range(chunks):
        here = slice(n * part, n * part + part)
        right = jnp.concatenate([x_ref[here, pl.ds(lane_of(b, parity), LANES)] for b in range(width)], axis=1)
        weight = w_ref[:, here]
        left = jnp.concatenate([turned_block(x_ref, here, lane_of(b, parity), weight) for b in range(width)], axis=0)
        term = jnp.dot(left, right, preferred_element_type=F32)
        total = term if total is None else total + term
    turned = cross[...].T
    for b in range(width):
        lanes = slice(b * LANES, (b + 1) * LANES)
        acc[:, pl.ds(lane_of(b, parity), LANES)] = total[:, lanes]
        acc[:, pl.ds(lane_of(b, 1 - parity), LANES)] = turned[:, lanes]
    for packed, (kept, sent) in core_rows(blk, core, feat // (4 * blk)):
        keep_ref[packed, :] = acc[kept, :]
        send_ref[packed, :] = acc[sent, :].astype(BF16)


VMEM_SPEC = pl.BlockSpec(memory_space=pltpu.VMEM)


def first(place, x, coef, labels, pid, slot_of, per_owner, blk, chunks=(1, 2, 5)):
    rows, feat = x.shape
    clusters = slot_of.shape[0]
    hbm = pl.BlockSpec(memory_space=pltpu.HBM)
    shape = jax.ShapeDtypeStruct
    arrays = [x, coef, labels.reshape(1, rows), pid.reshape(1, rows), slot_of.reshape(1, clusters)]
    return pl.pallas_call(
        functools.partial(first_kernel, per_owner, blk, chunks),
        in_specs=[pl.BlockSpec(memory_space=pltpu.SMEM)] + [hbm] * 5,
        out_specs=[VMEM_SPEC] * 6,
        out_shape=[
            shape((rows, feat), BF16),
            shape((1, rows), F32),
            shape((clusters // 2, feat), F32),
            shape((clusters // 2, feat), F32),
            shape((feat // 4, feat), BF16),
            shape((feat // 4, feat), F32),
        ],
        scratch_shapes=[
            pltpu.VMEM((feat // 2, rows), BF16),
            pltpu.VMEM((feat // 4, feat), F32),
            pltpu.VMEM((feat,), BF16),
            pltpu.VMEM((1, rows), jnp.int32),
            pltpu.VMEM((1, rows), jnp.int32),
            pltpu.VMEM((1, clusters), jnp.int32),
            pltpu.SemaphoreType.DMA((len(chunks),)),
            pltpu.SemaphoreType.DMA((4,)),
        ],
        compiler_params=pltpu.CompilerParams(vmem_limit_bytes=VMEM_LIMIT),
        name="scores_and_far",
    )(place, *[pltpu.with_memory_space_constraint(array, pltpu.HBM) for array in arrays])


def second(place, x, w, far_send, far_keep, blk, chunks=4):
    feat = x.shape[1]
    return pl.pallas_call(
        functools.partial(second_kernel, blk, chunks),
        in_specs=[pl.BlockSpec(memory_space=pltpu.SMEM)] + [VMEM_SPEC] * 4,
        out_specs=[VMEM_SPEC] * 2,
        out_shape=[
            jax.ShapeDtypeStruct((feat // 4, feat), BF16),
            jax.ShapeDtypeStruct((feat // 4, feat), F32),
        ],
        scratch_shapes=[pltpu.VMEM((feat // 2, feat), F32), pltpu.VMEM((feat // 2, feat // 2), F32)],
        compiler_params=pltpu.CompilerParams(vmem_limit_bytes=VMEM_LIMIT),
        name="near",
    )(place, x, w, far_send, far_keep)


def local(features, coef, labels, passage_id, slot_of):
    feat = features.shape[1]
    devices = lax.axis_size("rows")
    clusters = slot_of.shape[0]
    per_owner = clusters // devices
    blk = feat // devices
    me = lax.axis_index("rows").astype(jnp.int32)
    turn = LANES // blk
    core, parity = me & 1, (me & turn) // turn

    def swap(array, mask):
        return lax.ppermute(array, "rows", [(i, i ^ mask) for i in range(devices)])

    def rest(number):
        return (number // (2 * turn)) * (turn // 2) + (number % turn) // 2

    place = jnp.stack([core, parity])
    x, w, sums_send, sums_keep, far_send, far_keep = first(
        place, features, coef, labels, passage_id, slot_of, per_owner, blk
    )
    masks = [m for m in range(1, devices) if not m & 1 and not m & turn]
    far_in, sums_in = swap(far_send, 1), swap(sums_send, 1)
    near_send, near_keep = second(place, x, w, far_send, far_keep, blk)
    near_in = swap(near_send, 1)
    far = (far_keep + far_in.astype(F32)).astype(BF16)
    sums = sums_keep + sums_in
    sums_out = sums.astype(BF16)
    arrived = swap(far, turn)
    sums_parts = [swap(sums_out, m) for m in masks]
    near = near_keep + near_in.astype(F32) + arrived.astype(F32)
    block = lambda n: lax.dynamic_slice_in_dim(near, (rest(me) ^ n) * blk, blk, 0)
    hessian = block(0)
    parts = [block(rest(m)).astype(BF16) for m in masks]
    sums_parts, parts = lax.optimization_barrier((sums_parts, parts))
    parts = [swap(part, m) for part, m in zip(parts, masks)]
    for part in sums_parts:
        sums = sums + part.astype(F32)
    sums = sums + swap(sums, turn)
    other = swap(sums, 1)
    chip = me // 2
    grad_local = lax.dynamic_slice_in_dim(sums, chip * per_owner, per_owner, 0)
    stack = jnp.concatenate([sums, other], axis=0)
    columns = lax.dynamic_slice_in_dim(stack, me * blk, blk, 1)
    meat = lax.dot_general(
        columns,
        stack,
        (((0,), (0,)), ((), ())),
        precision=lax.Precision.HIGHEST,
        preferred_element_type=F32,
    )
    for part in parts:
        hessian = hessian + part.astype(F32)
    return (hessian, meat, grad_local)


def solution(mesh):
    in_specs = (
        P(("groups", "rows"), None),
        P(),
        P(("groups", "rows")),
        P(("groups", "rows"), None),
        P("groups"),
    )
    out_specs = (
        P(("groups", "rows"), None),
        P(("groups", "rows"), None),
        P(("groups", "rows"), None),
    )
    return jax.shard_map(local, mesh=mesh, in_specs=in_specs, out_specs=out_specs, check_vma=False)
```

time: 63.7 us -> 53.9 us (0.85)
  waiting for transfers between devices: 25.2 us -> 20.6 us
  local copies, waits for them, and re-layouts: 3.44 us -> 0.68 us
  Pallas kernels: 16.3 us -> 15 us
  starting transfers between devices: 14.2 us -> 13.5 us
    ppermute x12, waiting for transfers between devices: 25.2 us -> 20.6 us  [swap(): return lax.ppermute(array, 'rows', [(i, i ^ mask) for i in range(devices)])]
    unnamed x8 -> x0, local copies, waits for them, and re-layouts: 2.77 us -> none
    pallas_call x1, Pallas kernels: 12.9 us -> 11.6 us  [first(): pl.pallas_call(functools.partial(first_kernel, per_owner, blk, chunks), i...]
    add x1, other arithmetic: 0.98 us -> 0.03 us  [local(): sums = sums + swap(sums, turn)]
    convert_element_type x1, other arithmetic: 0.16 us -> 0.94 us  [local(): far = (far_keep + far_in.astype(F32)).astype(BF16)]
    ppermute x12, starting transfers between devices: 14.2 us -> 13.5 us  [swap(): return lax.ppermute(array, 'rows', [(i, i ^ mask) for i in range(devices)])]
  transfers between devices with their start and end apart: 12 -> 12, of which waited for: 5 -> 6; matrix products, arithmetic and copies ran while one was open for 5% -> 5% of each run, Pallas kernels for 5% -> 6%
where the time goes in v3:
time: 53.9 us; the launch traced here: 53.8 us
  waiting for transfers between devices  20.6 us (38%)
  Pallas kernels  15 us (28%)
  starting transfers between devices  13.5 us (25%)
  other arithmetic  2.14 us (4%)
  matrix products  1.18 us (2%)
  between operations  0.72 us (1%)
  local copies, waits for them, and re-layouts  0.68 us (1%)
    ppermute x12, waiting for transfers between devices, swap(): return lax.ppermute(array, 'rows', [(i, i ^ mask) for i in range(devices)])  20.6 us
    ppermute x12, starting transfers between devices, swap(): return lax.ppermute(array, 'rows', [(i, i ^ mask) for i in range(devices)])  13.5 us
    pallas_call x1, Pallas kernels, first(): pl.pallas_call(functools.partial(first_kernel, per_owner, blk, chunks), i...  11.6 us
    pallas_call x1, Pallas kernels, second(): pl.pallas_call(functools.partial(second_kernel, blk, chunks), in_specs=[p...  3.41 us
    dot_general x1, matrix products, local(): lax.dot_general(columns, stack, (((0,), (0,)), ((), ())), precision=lax.P...  1.18 us
  transfers between devices with their start and end apart: 12, of which 6 were waited for; matrix products, arithmetic and copies ran while one was open for 5% of the time, Pallas kernels for 6%

profile of v3, /device:TPU:0, one launch (start us, length us, event | category | flops | bytes accessed | tf_op | source)
XLA Modules:
  0.0 53.8 jit_solution(3554734541957090234)
XLA Ops:
  0.6 0.1 pad_add_fusion.place
  0.7 11.6 %scores_and_far.1 = (bf16[4096,1024]{1,0:T(8,128)(2,1)S(1)}, f32[1,4096]{1,0:T(1,128)S(1)}, f32[64,1024]{1,0:T(8,128)S(1)}, f32[64,1024]{1,0:T(8,128)S(1)}, bf16...) custom-call(s32[2]{0:T(128)S(1)} %pad_add_fusion.place, bf16[4096,1024]{1,0:T(8,128)(2,1)} %x_hbm.1, ...), custom_call_target="tpu_custom_call" | custom-call | tf_op jit(solution)/shard_map/scores_and_far/pallas_call | solution.py:152
  12.3 0.5 collective-permute-start.1
  12.9 3.4 %near.1 = (bf16[256,1024]{1,0:T(8,128)(2,1)S(1)}, f32[256,1024]{1,0:T(8,128)S(1)}) custom-call(s32[2]{0:T(128)S(1)} %pad_add_fusion.place, bf16[4096,1024]{1,0:T(8,128)(2,1)S(1)} %get-tuple-element.17.x_ref, f32[1,4096]{1,0:T(1,128)S(1)} %get-tuple-element.18.w_ref, bf16[256,1024]{1,0:T(8,128)(2,1)S(1)} %get-tuple-element.19.far_send, ...), custom_call_target="tpu_custom_call" | custom-call | tf_op jit(solution)/shard_map/near/pallas_call | solution.py:181
  16.3 0.1 collective-permute-start
  16.4 0.0 collective-permute-done.1
  16.4 0.9 %add_convert_fusion = bf16[256,1024]{1,0:T(8,128)(2,1)} fusion(f32[256,1024]{1,0:T(8,128)S(1)} %get-tuple-element.20.far_keep, bf16[256,1024]{1,0:T(8,128)(2,1)S(1)} %collective-permute-done.1), kind=kLoop, calls=%fused_computation.1 | loop fusion | flops 786432 | bytes 2097152 | tf_op jit(solution)/shard_map/convert_element_type | solution.py:219
  17.3 3.0 %collective-permute-start.2 = (bf16[256,1024]{1,0:T(8,128)(2,1)}, bf16[256,1024]{1,0:T(8,128)(2,1)S(1)}, u32[]{:S(2)}, u32[]{:S(2)}) collective-permute-start(bf16[256,1024]{1,0:T(8,128)(2,1)} %add_convert_fusion), channel_id=1, source_target_pairs={{0,2},{1,3},{2,0},{3,1},{4,6},{5,7},{6,4},{7,5},{8,10},{9,11},{10,... | collective-permute-start | bytes 1572872 | tf_op jit(solution)/shard_map/ppermute | solution.py:206
  20.3 0.0 collective-permute-start.3
  20.3 1.5 %collective-permute-done.3 = f32[64,1024]{1,0:T(8,128)S(1)} collective-permute-done((f32[64,1024]{1,0:T(8,128)S(1)}, f32[64,1024]{1,0:T(8,128)S(1)}, u32[]{:S(2)}, u32[]{:S(2)}) %collective-permute-start.3) | collective-permute-done | bytes 262176 | tf_op jit(solution)/shard_map/ppermute | solution.py:206
  21.9 1.7 %collective-permute-start.4 = (bf16[64,1024]{1,0:T(8,128)(2,1)S(1)}, bf16[64,1024]{1,0:T(8,128)(2,1)S(1)}, u32[]{:S(2)}, u32[]{:S(2)}) collective-permute-start(bf16[64,1024]{1,0:T(8,128)(2,1)S(1)} %get-tuple-element.31), channel_id=1, source_target_pairs={{0,4},{1,5},{2,6},{3,7},{4,0},{5,1},{6,2},{7,3},{8,12},{9,13},{10,... | collective-permute-start | bytes 393224 | tf_op jit(solution)/shard_map/ppermute | solution.py:206
  23.5 2.6 %collective-permute-start.5 = (bf16[64,1024]{1,0:T(8,128)(2,1)S(1)}, bf16[64,1024]{1,0:T(8,128)(2,1)S(1)}, u32[]{:S(2)}, u32[]{:S(2)}) collective-permute-start(bf16[64,1024]{1,0:T(8,128)(2,1)S(1)} %get-tuple-element.31), channel_id=1, source_target_pairs={{0,8},{1,9},{2,10},{3,11},{4,12},{5,13},{6,14},{7,15},{8,0},{9,1},... | collective-permute-start | bytes 393224 | tf_op jit(solution)/shard_map/ppermute | solution.py:206
  26.1 0.2 collective-permute-start.6
  26.3 0.0 collective-permute-done
  26.3 6.3 %collective-permute-done.2 = bf16[256,1024]{1,0:T(8,128)(2,1)S(1)} collective-permute-done((bf16[256,1024]{1,0:T(8,128)(2,1)}, bf16[256,1024]{1,0:T(8,128)(2,1)S(1)}, u32[]{:S(2)}, u32[]{:S(2)}) %collective-permute-start.2) | collective-permute-done | bytes 524320 | tf_op jit(solution)/shard_map/ppermute | solution.py:206
  32.6 0.2 convert_add_fusion
  32.8 0.1 dynamic-slice_convert_fusion
  32.9 0.0 collective-permute-done.4
  32.9 3.5 %collective-permute-done.5 = bf16[64,1024]{1,0:T(8,128)(2,1)S(1)} collective-permute-done((bf16[64,1024]{1,0:T(8,128)(2,1)S(1)}, bf16[64,1024]{1,0:T(8,128)(2,1)S(1)}, u32[]{:S(2)}, u32[]{:S(2)}) %collective-permute-start.5) | collective-permute-done | bytes 131104 | tf_op jit(solution)/shard_map/ppermute | solution.py:206
  36.4 0.0 collective-permute-done.6
  36.4 0.1 convert_add_fusion.1
  36.5 0.6 %collective-permute-start.10 = (f32[64,1024]{1,0:T(8,128)S(1)}, f32[64,1024]{1,0:T(8,128)S(1)}, u32[]{:S(2)}, u32[]{:S(2)}) collective-permute-start(f32[64,1024]{1,0:T(8,128)S(1)} %convert_add_fusion.1), channel_id=1, source_target_pairs={{0,2},{1,3},{2,0},{3,1},{4,6},{5,7},{6,4},{7,5},{8,10},{9,11},{10,... | collective-permute-start | bytes 786440 | tf_op jit(solution)/shard_map/ppermute | solution.py:206
  37.0 2.3 %collective-permute-start.7 = (bf16[64,1024]{1,0:T(8,128)(2,1)S(1)}, bf16[64,1024]{1,0:T(8,128)(2,1)S(1)}, u32[]{:S(2)}, u32[]{:S(2)}) collective-permute-start(bf16[64,1024]{1,0:T(8,128)(2,1)S(1)} %get-tuple-element.25), channel_id=1, source_target_pairs={{0,4},{1,5},{2,6},{3,7},{4,0},{5,1},{6,2},{7,3},{8,12},{9,13},{10,... | collective-permute-start | bytes 393224 | tf_op jit(solution)/shard_map/ppermute | solution.py:206
  39.3 1.0 %collective-permute-start.8 = (bf16[64,1024]{1,0:T(8,128)(2,1)S(1)}, bf16[64,1024]{1,0:T(8,128)(2,1)S(1)}, u32[]{:S(2)}, u32[]{:S(2)}) collective-permute-start(bf16[64,1024]{1,0:T(8,128)(2,1)S(1)} %get-tuple-element.26), channel_id=1, source_target_pairs={{0,8},{1,9},{2,10},{3,11},{4,12},{5,13},{6,14},{7,15},{8,0},{9,1},... | collective-permute-start | bytes 393224 | tf_op jit(solution)/shard_map/ppermute | solution.py:206
  40.4 1.5 %collective-permute-start.9 = (bf16[64,1024]{1,0:T(8,128)(2,1)S(1)}, bf16[64,1024]{1,0:T(8,128)(2,1)S(1)}, u32[]{:S(2)}, u32[]{:S(2)}) collective-permute-start(bf16[64,1024]{1,0:T(8,128)(2,1)S(1)} %get-tuple-element.27), channel_id=1, source_target_pairs={{0,12},{1,13},{2,14},{3,15},{4,8},{5,9},{6,10},{7,11},{8,4},{9,5},... | collective-permute-start | bytes 393224 | tf_op jit(solution)/shard_map/ppermute | solution.py:206
  41.8 1.1 %collective-permute-done.10 = f32[64,1024]{1,0:T(8,128)S(1)} collective-permute-done((f32[64,1024]{1,0:T(8,128)S(1)}, f32[64,1024]{1,0:T(8,128)S(1)}, u32[]{:S(2)}, u32[]{:S(2)}) %collective-permute-start.10) | collective-permute-done | bytes 262176 | tf_op jit(solution)/shard_map/ppermute | solution.py:206
  42.9 0.1 collective-permute-start.11
  43.0 0.6 %collective-permute-done.7 = bf16[64,1024]{1,0:T(8,128)(2,1)S(1)} collective-permute-done((bf16[64,1024]{1,0:T(8,128)(2,1)S(1)}, bf16[64,1024]{1,0:T(8,128)(2,1)S(1)}, u32[]{:S(2)}, u32[]{:S(2)}) %collective-permute-start.7) | collective-permute-done | bytes 131104 | tf_op jit(solution)/shard_map/ppermute | solution.py:206
  43.6 7.6 %collective-permute-done.8 = bf16[64,1024]{1,0:T(8,128)(2,1)S(1)} collective-permute-done((bf16[64,1024]{1,0:T(8,128)(2,1)S(1)}, bf16[64,1024]{1,0:T(8,128)(2,1)S(1)}, u32[]{:S(2)}, u32[]{:S(2)}) %collective-permute-start.8) | collective-permute-done | bytes 131104 | tf_op jit(solution)/shard_map/ppermute | solution.py:206
  51.2 0.0 collective-permute-done.9
  51.2 0.8 %convert_add_fusion.2 = f32[64,1024]{1,0:T(8,128)} fusion(bf16[64,1024]{1,0:T(8,128)(2,1)S(1)} %collective-permute-done.9, bf16[64,1024]{1,0:T(8,128)(2,1)S(1)} %collective-permute-done.8, bf16[64,1024]{1,0:T(8,128)(2,1)S(1)} %collective-permute-done.7, f32[256,1024]{1,0:T(8,128)S(1)} %convert_add_fusion, s32[]{:T(128)S(6)} %select_n.54), kind=kLoop, calls=%fused_computation.7 | loop fusion | flops 393216 | bytes 917508 | tf_op jit(solution)/shard_map/add | solution.py:246
  51.9 0.6 %constant_dynamic-slice_fusion = f32[8,1024]{1,0:T(8,128)} fusion(f32[64,1024]{1,0:T(8,128)S(1)} %add.84, s32[]{:T(128)S(6)} %select_n.60), kind=kLoop, calls=%fused_computation.12 | loop fusion | bytes 65540 | tf_op jit(solution)/shard_map/dynamic_slice | solution.py:235
  52.6 0.0 collective-permute-done.11
  52.6 1.2 %fusion = f32[64,1024]{1,0:T(8,128)} fusion(f32[64,1024]{1,0:T(8,128)S(1)} %collective-permute-done.11, f32[64,1024]{1,0:T(8,128)S(1)} %add.84, s32[]{:T(128)S(6)} %select_n.58), kind=kOutput, calls=%fused_computation.5 | convolution fusion | flops 100802560 | bytes 1310724 | tf_op jit(solution)/shard_map/dot_general | solution.py:238
  (2 shorter events, 0.1 us)
Async XLA Ops:
  12.3 4.1 %collective-permute-start.1 = (bf16[256,1024]{1,0:T(8,128)(2,1)S(1)}, bf16[256,1024]{1,0:T(8,128)(2,1)S(1)}, u32[]{:S(2)}, u32[]{:S(2)}) collective-permute-start(bf16[256,1024]{1,0:T(8,128)(2,1)S(1)} %get-tuple-element.19.far_send), channel_id=1, source_target_pairs={{0,1},{1,0},{2,3},{3,2},{4,5},{5,4},{6,7},{7,6},{8,9},{9,8},{10,11... | collective-permute-start | bytes 1572872 | tf_op jit(solution)/shard_map/ppermute | solution.py:206
  16.3 10.0 %collective-permute-start = (bf16[256,1024]{1,0:T(8,128)(2,1)S(1)}, bf16[256,1024]{1,0:T(8,128)(2,1)S(1)}, u32[]{:S(2)}, u32[]{:S(2)}) collective-permute-start(bf16[256,1024]{1,0:T(8,128)(2,1)S(1)} %get-tuple-element.22), channel_id=1, source_target_pairs={{0,1},{1,0},{2,3},{3,2},{4,5},{5,4},{6,7},{7,6},{8,9},{9,8},{10,11... | collective-permute-start | bytes 1572872 | tf_op jit(solution)/shard_map/ppermute | solution.py:206
  17.3 15.3 %collective-permute-start.2 = (bf16[256,1024]{1,0:T(8,128)(2,1)}, bf16[256,1024]{1,0:T(8,128)(2,1)S(1)}, u32[]{:S(2)}, u32[]{:S(2)}) collective-permute-start(bf16[256,1024]{1,0:T(8,128)(2,1)} %add_convert_fusion), channel_id=1, source_target_pairs={{0,2},{1,3},{2,0},{3,1},{4,6},{5,7},{6,4},{7,5},{8,10},{9,11},{10,... | collective-permute-start | bytes 1572872 | tf_op jit(solution)/shard_map/ppermute | solution.py:206
  20.3 1.5 %collective-permute-start.3 = (f32[64,1024]{1,0:T(8,128)S(1)}, f32[64,1024]{1,0:T(8,128)S(1)}, u32[]{:S(2)}, u32[]{:S(2)}) collective-permute-start(f32[64,1024]{1,0:T(8,128)S(1)} %get-tuple-element.24), channel_id=1, source_target_pairs={{0,1},{1,0},{2,3},{3,2},{4,5},{5,4},{6,7},{7,6},{8,9},{9,8},{10,11... | collective-permute-start | bytes 786440 | tf_op jit(solution)/shard_map/ppermute | solution.py:206
  21.9 11.1 %collective-permute-start.4 = (bf16[64,1024]{1,0:T(8,128)(2,1)S(1)}, bf16[64,1024]{1,0:T(8,128)(2,1)S(1)}, u32[]{:S(2)}, u32[]{:S(2)}) collective-permute-start(bf16[64,1024]{1,0:T(8,128)(2,1)S(1)} %get-tuple-element.31), channel_id=1, source_target_pairs={{0,4},{1,5},{2,6},{3,7},{4,0},{5,1},{6,2},{7,3},{8,12},{9,13},{10,... | collective-permute-start | bytes 393224 | tf_op jit(solution)/shard_map/ppermute | solution.py:206
  23.5 12.9 %collective-permute-start.5 = (bf16[64,1024]{1,0:T(8,128)(2,1)S(1)}, bf16[64,1024]{1,0:T(8,128)(2,1)S(1)}, u32[]{:S(2)}, u32[]{:S(2)}) collective-permute-start(bf16[64,1024]{1,0:T(8,128)(2,1)S(1)} %get-tuple-element.31), channel_id=1, source_target_pairs={{0,8},{1,9},{2,10},{3,11},{4,12},{5,13},{6,14},{7,15},{8,0},{9,1},... | collective-permute-start | bytes 393224 | tf_op jit(solution)/shard_map/ppermute | solution.py:206
  26.1 10.3 %collective-permute-start.6 = (bf16[64,1024]{1,0:T(8,128)(2,1)S(1)}, bf16[64,1024]{1,0:T(8,128)(2,1)S(1)}, u32[]{:S(2)}, u32[]{:S(2)}) collective-permute-start(bf16[64,1024]{1,0:T(8,128)(2,1)S(1)} %get-tuple-element.31), channel_id=1, source_target_pairs={{0,12},{1,13},{2,14},{3,15},{4,8},{5,9},{6,10},{7,11},{8,4},{9,5},... | collective-permute-start | bytes 393224 | tf_op jit(solution)/shard_map/ppermute | solution.py:206
  36.5 6.4 %collective-permute-start.10 = (f32[64,1024]{1,0:T(8,128)S(1)}, f32[64,1024]{1,0:T(8,128)S(1)}, u32[]{:S(2)}, u32[]{:S(2)}) collective-permute-start(f32[64,1024]{1,0:T(8,128)S(1)} %convert_add_fusion.1), channel_id=1, source_target_pairs={{0,2},{1,3},{2,0},{3,1},{4,6},{5,7},{6,4},{7,5},{8,10},{9,11},{10,... | collective-permute-start | bytes 786440 | tf_op jit(solution)/shard_map/ppermute | solution.py:206
  37.0 6.6 %collective-permute-start.7 = (bf16[64,1024]{1,0:T(8,128)(2,1)S(1)}, bf16[64,1024]{1,0:T(8,128)(2,1)S(1)}, u32[]{:S(2)}, u32[]{:S(2)}) collective-permute-start(bf16[64,1024]{1,0:T(8,128)(2,1)S(1)} %get-tuple-element.25), channel_id=1, source_target_pairs={{0,4},{1,5},{2,6},{3,7},{4,0},{5,1},{6,2},{7,3},{8,12},{9,13},{10,... | collective-permute-start | bytes 393224 | tf_op jit(solution)/shard_map/ppermute | solution.py:206
  39.3 11.8 %collective-permute-start.8 = (bf16[64,1024]{1,0:T(8,128)(2,1)S(1)}, bf16[64,1024]{1,0:T(8,128)(2,1)S(1)}, u32[]{:S(2)}, u32[]{:S(2)}) collective-permute-start(bf16[64,1024]{1,0:T(8,128)(2,1)S(1)} %get-tuple-element.26), channel_id=1, source_target_pairs={{0,8},{1,9},{2,10},{3,11},{4,12},{5,13},{6,14},{7,15},{8,0},{9,1},... | collective-permute-start | bytes 393224 | tf_op jit(solution)/shard_map/ppermute | solution.py:206
  40.4 10.8 %collective-permute-start.9 = (bf16[64,1024]{1,0:T(8,128)(2,1)S(1)}, bf16[64,1024]{1,0:T(8,128)(2,1)S(1)}, u32[]{:S(2)}, u32[]{:S(2)}) collective-permute-start(bf16[64,1024]{1,0:T(8,128)(2,1)S(1)} %get-tuple-element.27), channel_id=1, source_target_pairs={{0,12},{1,13},{2,14},{3,15},{4,8},{5,9},{6,10},{7,11},{8,4},{9,5},... | collective-permute-start | bytes 393224 | tf_op jit(solution)/shard_map/ppermute | solution.py:206
  42.9 9.6 %collective-permute-start.11 = (f32[64,1024]{1,0:T(8,128)S(1)}, f32[64,1024]{1,0:T(8,128)S(1)}, u32[]{:S(2)}, u32[]{:S(2)}) collective-permute-start(f32[64,1024]{1,0:T(8,128)S(1)} %add.84), channel_id=1, source_target_pairs={{0,1},{1,0},{2,3},{3,2},{4,5},{5,4},{6,7},{7,6},{8,9},{9,8},{10,11... | collective-permute-start | bytes 786440 | tf_op jit(solution)/shard_map/ppermute | solution.py:206

commit v4 on v3

--- a/solution.py
+++ b/solution.py
@@ -57,9 +57,14 @@
     for copy in small:
         copy.wait()
     row = lax.broadcasted_iota(jnp.int32, (clusters, clusters), 0)
-    mine = row >= half
-    inner = jnp.where(mine, row - half, row)
-    slot = (2 * (inner // per_owner) + jnp.where(mine, core, 1 - core)) * per_owner + inner % per_owner
+    turn = LANES // blk
+    core_of = jnp.where(row >= half, core, 1 - core)
+    inner = row % half
+    parity_of = jnp.where(inner >= half // 2, parity, 1 - parity)
+    inner = inner % (half // 2)
+    rest = inner // per_owner
+    owner = (rest // (turn // 2)) * (2 * turn) + parity_of * turn + (rest % (turn // 2)) * 2 + core_of
+    slot = owner * per_owner + inner % per_owner
     passage = lax.broadcasted_iota(jnp.int32, (clusters, clusters), 1)
     names = jnp.sum(jnp.where(slot_ref[...] == slot, passage, 0), axis=1, keepdims=True)
     coef = jnp.broadcast_to(coef_ref[...].reshape(1, feat), (16, feat))
@@ -217,23 +222,25 @@
     near_send, near_keep = second(place, x, w, far_send, far_keep, blk)
     near_in = swap(near_send, 1)
     far = (far_keep + far_in.astype(F32)).astype(BF16)
+    sums_keep, _ = lax.optimization_barrier((sums_keep, near_keep))
     sums = sums_keep + sums_in
+    quarter = clusters // 4
+    sums_far, sums_near = sums[:quarter], sums[quarter:]
+    sums = sums_near + swap(sums_far.astype(BF16), turn).astype(F32)
+    arrived = swap(far, turn)
     sums_out = sums.astype(BF16)
-    arrived = swap(far, turn)
     sums_parts = [swap(sums_out, m) for m in masks]
     near = near_keep + near_in.astype(F32) + arrived.astype(F32)
     block = lambda n: lax.dynamic_slice_in_dim(near, (rest(me) ^ n) * blk, blk, 0)
     hessian = block(0)
     parts = [block(rest(m)).astype(BF16) for m in masks]
-    sums_parts, parts = lax.optimization_barrier((sums_parts, parts))
-    parts = [swap(part, m) for part, m in zip(parts, masks)]
     for part in sums_parts:
         sums = sums + part.astype(F32)
-    sums = sums + swap(sums, turn)
-    other = swap(sums, 1)
-    chip = me // 2
-    grad_local = lax.dynamic_slice_in_dim(sums, chip * per_owner, per_owner, 0)
-    stack = jnp.concatenate([sums, other], axis=0)
+    sums, parts = lax.optimization_barrier((sums, parts))
+    parts = [swap(part, m) for part, m in zip(parts, masks)]
+    grad_local = lax.dynamic_slice_in_dim(sums, rest(me) * per_owner, per_owner, 0)
+    sums = jnp.concatenate([sums, swap(sums, turn)], axis=0)
+    stack = jnp.concatenate([sums, swap(sums, 1)], axis=0)
     columns = lax.dynamic_slice_in_dim(stack, me * blk, blk, 1)
     meat = lax.dot_general(
         columns,
@@ -242,6 +249,7 @@
         precision=lax.Precision.HIGHEST,
         preferred_element_type=F32,
     )
+    parts, meat = lax.optimization_barrier((parts, meat))
     for part in parts:
         hessian = hessian + part.astype(F32)
     return (hessian, meat, grad_local)

time: 53.9 us -> 50.3 us (0.933)
  waiting for transfers between devices: 20.6 us -> 16.9 us
    ppermute x12 -> x13, waiting for transfers between devices: 20.6 us -> 16.9 us  [swap(): return lax.ppermute(array, 'rows', [(i, i ^ mask) for i in range(devices)])]
    ppermute x12 -> x13, starting transfers between devices: 13.5 us -> 13.4 us  [swap(): return lax.ppermute(array, 'rows', [(i, i ^ mask) for i in range(devices)])]
  transfers between devices with their start and end apart: 12 -> 13, of which waited for: 6 -> 7; matrix products, arithmetic and copies ran while one was open for 5% -> 6% of each run, Pallas kernels for 6% -> 7%
where the time goes in v4:
time: 50.3 us; the launch traced here: 50.1 us
  waiting for transfers between devices  16.9 us (34%)
  Pallas kernels  15 us (30%)
  starting transfers between devices  13.4 us (27%)
  other arithmetic  2.14 us (4%)
  matrix products  1.19 us (2%)
  between operations  0.74 us (1%)
  local copies, waits for them, and re-layouts  0.73 us (1%)
    ppermute x13, waiting for transfers between devices, swap(): return lax.ppermute(array, 'rows', [(i, i ^ mask) for i in range(devices)])  16.9 us
    ppermute x13, starting transfers between devices, swap(): return lax.ppermute(array, 'rows', [(i, i ^ mask) for i in range(devices)])  13.4 us
    pallas_call x1, Pallas kernels, first(): pl.pallas_call(functools.partial(first_kernel, per_owner, blk, chunks), i...  11.6 us
    pallas_call x1, Pallas kernels, second(): pl.pallas_call(functools.partial(second_kernel, blk, chunks), in_specs=[p...  3.41 us
    dot_general x1, matrix products, local(): lax.dot_general(columns, stack, (((0,), (0,)), ((), ())), precision=lax.P...  1.19 us
  transfers between devices with their start and end apart: 13, of which 7 were waited for; matrix products, arithmetic and copies ran while one was open for 6% of the time, Pallas kernels for 7%

profile of v4, /device:TPU:0, one launch (start us, length us, event | category | flops | bytes accessed | tf_op | source)
XLA Modules:
  0.0 50.1 jit_solution(991572144032981914)
XLA Ops:
  0.6 0.1 pad_add_fusion.place
  0.7 11.6 %scores_and_far.1 = (bf16[4096,1024]{1,0:T(8,128)(2,1)S(1)}, f32[1,4096]{1,0:T(1,128)S(1)}, f32[64,1024]{1,0:T(8,128)S(1)}, f32[64,1024]{1,0:T(8,128)S(1)}, bf16...) custom-call(s32[2]{0:T(128)S(1)} %pad_add_fusion.place, bf16[4096,1024]{1,0:T(8,128)(2,1)} %x_hbm.1, ...), custom_call_target="tpu_custom_call" | custom-call | tf_op jit(solution)/shard_map/scores_and_far/pallas_call | solution.py:157
  12.3 0.5 %collective-permute-start.1 = (bf16[256,1024]{1,0:T(8,128)(2,1)S(1)}, bf16[256,1024]{1,0:T(8,128)(2,1)S(1)}, u32[]{:S(2)}, u32[]{:S(2)}) collective-permute-start(bf16[256,1024]{1,0:T(8,128)(2,1)S(1)} %get-tuple-element.22.far_send), channel_id=1, source_target_pairs={{0,1},{1,0},{2,3},{3,2},{4,5},{5,4},{6,7},{7,6},{8,9},{9,8},{10,11... | collective-permute-start | bytes 1572872 | tf_op jit(solution)/shard_map/ppermute | solution.py:211
  12.9 0.1 collective-permute-start.3
  12.9 3.4 %near.1 = (bf16[256,1024]{1,0:T(8,128)(2,1)S(1)}, f32[256,1024]{1,0:T(8,128)S(1)}) custom-call(s32[2]{0:T(128)S(1)} %pad_add_fusion.place, bf16[4096,1024]{1,0:T(8,128)(2,1)S(1)} %get-tuple-element.20.x_ref, f32[1,4096]{1,0:T(1,128)S(1)} %get-tuple-element.21.w_ref, bf16[256,1024]{1,0:T(8,128)(2,1)S(1)} %get-tuple-element.22.far_send, ...), custom_call_target="tpu_custom_call" | custom-call | tf_op jit(solution)/shard_map/near/pallas_call | solution.py:186
  16.3 0.5 collective-permute-start
  16.8 0.0 collective-permute-done.3
  16.9 2.7 %collective-permute-start.4 = (bf16[32,1024]{1,0:T(8,128)(2,1)S(1)}, bf16[32,1024]{1,0:T(8,128)(2,1)S(1)}, u32[]{:S(2)}, u32[]{:S(2)}) collective-permute-start(bf16[32,1024]{1,0:T(8,128)(2,1)S(1)} %slice.17), channel_id=1, source_target_pairs={{0,2},{1,3},{2,0},{3,1},{4,6},{5,7},{6,4},{7,5},{8,10},{9,11},{10,... | collective-permute-start | bytes 196616 | tf_op jit(solution)/shard_map/ppermute | solution.py:211
  19.6 0.0 collective-permute-done.1
  19.6 1.0 %add_convert_fusion = bf16[256,1024]{1,0:T(8,128)(2,1)} fusion(f32[256,1024]{1,0:T(8,128)S(1)} %get-tuple-element.23.far_keep, bf16[256,1024]{1,0:T(8,128)(2,1)S(1)} %collective-permute-done.1), kind=kLoop, calls=%fused_computation.1 | loop fusion | flops 786432 | bytes 2097152 | tf_op jit(solution)/shard_map/convert_element_type | solution.py:224
  20.5 0.0 collective-permute-start.2
  20.5 1.7 %collective-permute-done.4 = bf16[32,1024]{1,0:T(8,128)(2,1)S(1)} collective-permute-done((bf16[32,1024]{1,0:T(8,128)(2,1)S(1)}, bf16[32,1024]{1,0:T(8,128)(2,1)S(1)}, u32[]{:S(2)}, u32[]{:S(2)}) %collective-permute-start.4) | collective-permute-done | bytes 65568 | tf_op jit(solution)/shard_map/ppermute | solution.py:211
  22.3 3.9 %collective-permute-start.7 = (bf16[32,1024]{1,0:T(8,128)(2,1)S(1)}, bf16[32,1024]{1,0:T(8,128)(2,1)S(1)}, u32[]{:S(2)}, u32[]{:S(2)}) collective-permute-start(bf16[32,1024]{1,0:T(8,128)(2,1)S(1)} %fusion), channel_id=1, source_target_pairs={{0,12},{1,13},{2,14},{3,15},{4,8},{5,9},{6,10},{7,11},{8,4},{9,5},... | collective-permute-start | bytes 196616 | tf_op jit(solution)/shard_map/ppermute | solution.py:211
  26.2 0.0 collective-permute-start.6
  26.2 0.6 %collective-permute-start.5 = (bf16[32,1024]{1,0:T(8,128)(2,1)S(1)}, bf16[32,1024]{1,0:T(8,128)(2,1)S(1)}, u32[]{:S(2)}, u32[]{:S(2)}) collective-permute-start(bf16[32,1024]{1,0:T(8,128)(2,1)S(1)} %fusion), channel_id=1, source_target_pairs={{0,4},{1,5},{2,6},{3,7},{4,0},{5,1},{6,2},{7,3},{8,12},{9,13},{10,... | collective-permute-start | bytes 196616 | tf_op jit(solution)/shard_map/ppermute | solution.py:211
  26.8 2.0 %collective-permute-done.7 = bf16[32,1024]{1,0:T(8,128)(2,1)S(1)} collective-permute-done((bf16[32,1024]{1,0:T(8,128)(2,1)S(1)}, bf16[32,1024]{1,0:T(8,128)(2,1)S(1)}, u32[]{:S(2)}, u32[]{:S(2)}) %collective-permute-start.7) | collective-permute-done | bytes 65568 | tf_op jit(solution)/shard_map/ppermute | solution.py:211
  28.9 2.7 %collective-permute-done.6 = bf16[32,1024]{1,0:T(8,128)(2,1)S(1)} collective-permute-done((bf16[32,1024]{1,0:T(8,128)(2,1)S(1)}, bf16[32,1024]{1,0:T(8,128)(2,1)S(1)}, u32[]{:S(2)}, u32[]{:S(2)}) %collective-permute-start.6) | collective-permute-done | bytes 65568 | tf_op jit(solution)/shard_map/ppermute | solution.py:211
  31.6 0.0 collective-permute-done.5
  31.7 0.0 collective-permute-done
  31.7 3.1 %collective-permute-done.2 = bf16[256,1024]{1,0:T(8,128)(2,1)S(1)} collective-permute-done((bf16[256,1024]{1,0:T(8,128)(2,1)}, bf16[256,1024]{1,0:T(8,128)(2,1)S(1)}, u32[]{:S(2)}, u32[]{:S(2)}) %collective-permute-start.2) | collective-permute-done | bytes 524320 | tf_op jit(solution)/shard_map/ppermute | solution.py:211
  34.7 0.2 convert_add_fusion
  35.0 0.1 dynamic-slice_convert_fusion
  35.0 0.6 %collective-permute-start.11 = (f32[32,1024]{1,0:T(8,128)S(1)}, f32[32,1024]{1,0:T(8,128)S(1)}, u32[]{:S(2)}, u32[]{:S(2)}) collective-permute-start(f32[32,1024]{1,0:T(8,128)S(1)} %convert_add_fusion.2), channel_id=1, source_target_pairs={{0,2},{1,3},{2,0},{3,1},{4,6},{5,7},{6,4},{7,5},{8,10},{9,11},{10,... | collective-permute-start | bytes 393224 | tf_op jit(solution)/shard_map/ppermute | solution.py:211
  35.6 1.6 %collective-permute-start.8 = (bf16[64,1024]{1,0:T(8,128)(2,1)S(1)}, bf16[64,1024]{1,0:T(8,128)(2,1)S(1)}, u32[]{:S(2)}, u32[]{:S(2)}) collective-permute-start(bf16[64,1024]{1,0:T(8,128)(2,1)S(1)} %get-tuple-element.29), channel_id=1, source_target_pairs={{0,4},{1,5},{2,6},{3,7},{4,0},{5,1},{6,2},{7,3},{8,12},{9,13},{10,... | collective-permute-start | bytes 393224 | tf_op jit(solution)/shard_map/ppermute | solution.py:211
  37.2 2.6 %collective-permute-start.9 = (bf16[64,1024]{1,0:T(8,128)(2,1)S(1)}, bf16[64,1024]{1,0:T(8,128)(2,1)S(1)}, u32[]{:S(2)}, u32[]{:S(2)}) collective-permute-start(bf16[64,1024]{1,0:T(8,128)(2,1)S(1)} %get-tuple-element.30), channel_id=1, source_target_pairs={{0,8},{1,9},{2,10},{3,11},{4,12},{5,13},{6,14},{7,15},{8,0},{9,1},... | collective-permute-start | bytes 393224 | tf_op jit(solution)/shard_map/ppermute | solution.py:211
  39.8 0.2 collective-permute-start.10
  40.0 0.1 collective-permute-done.11
  40.1 0.1 collective-permute-start.12
  40.2 0.6 %constant_dynamic-slice_fusion = f32[8,1024]{1,0:T(8,128)} fusion(f32[32,1024]{1,0:T(8,128)S(1)} %convert_add_fusion.2, s32[]{:T(128)S(6)} %select_n.60), kind=kLoop, calls=%fused_computation.16 | loop fusion | bytes 65540 | tf_op jit(solution)/shard_map/dynamic_slice | solution.py:241
  40.8 0.9 %collective-permute-done.12 = f32[64,1024]{1,0:T(8,128)S(1)} collective-permute-done((f32[64,1024]{1,0:T(8,128)S(1)}, f32[64,1024]{1,0:T(8,128)S(1)}, u32[]{:S(2)}, u32[]{:S(2)}) %collective-permute-start.12) | collective-permute-done | bytes 262176 | tf_op jit(solution)/shard_map/ppermute | solution.py:211
  41.7 1.2 %fusion.1 = f32[64,1024]{1,0:T(8,128)} fusion(f32[128,1024]{1,0:T(8,128)S(1)} %constant_dynamic-update-slice_fusion, s32[]{:T(128)S(6)} %select_n.59), kind=kOutput, calls=%fused_computation.11 | convolution fusion | flops 100663296 | bytes 851972 | tf_op jit(solution)/shard_map/dot_general | solution.py:245
  42.9 0.0 collective-permute-done.8
  42.9 6.4 %collective-permute-done.9 = bf16[64,1024]{1,0:T(8,128)(2,1)S(1)} collective-permute-done((bf16[64,1024]{1,0:T(8,128)(2,1)S(1)}, bf16[64,1024]{1,0:T(8,128)(2,1)S(1)}, u32[]{:S(2)}, u32[]{:S(2)}) %collective-permute-start.9) | collective-permute-done | bytes 131104 | tf_op jit(solution)/shard_map/ppermute | solution.py:211
  49.3 0.0 collective-permute-done.10
  49.3 0.8 %convert_add_fusion.1 = f32[64,1024]{1,0:T(8,128)} fusion(bf16[64,1024]{1,0:T(8,128)(2,1)S(1)} %collective-permute-done.10, bf16[64,1024]{1,0:T(8,128)(2,1)S(1)} %collective-permute-done.9, bf16[64,1024]{1,0:T(8,128)(2,1)S(1)} %collective-permute-done.8, f32[256,1024]{1,0:T(8,128)S(1)} %convert_add_fusion, s32[]{:T(128)S(6)} %select_n.55), kind=kLoop, calls=%fused_computation.3 | loop fusion | flops 393216 | bytes 917508 | tf_op jit(solution)/shard_map/add | solution.py:254
  (8 shorter events, 0.2 us)
Async XLA Ops:
  12.3 7.2 %collective-permute-start.1 = (bf16[256,1024]{1,0:T(8,128)(2,1)S(1)}, bf16[256,1024]{1,0:T(8,128)(2,1)S(1)}, u32[]{:S(2)}, u32[]{:S(2)}) collective-permute-start(bf16[256,1024]{1,0:T(8,128)(2,1)S(1)} %get-tuple-element.22.far_send), channel_id=1, source_target_pairs={{0,1},{1,0},{2,3},{3,2},{4,5},{5,4},{6,7},{7,6},{8,9},{9,8},{10,11... | collective-permute-start | bytes 1572872 | tf_op jit(solution)/shard_map/ppermute | solution.py:211
  12.9 4.0 %collective-permute-start.3 = (f32[64,1024]{1,0:T(8,128)S(1)}, f32[64,1024]{1,0:T(8,128)S(1)}, u32[]{:S(2)}, u32[]{:S(2)}) collective-permute-start(f32[64,1024]{1,0:T(8,128)S(1)} %get-tuple-element.28), channel_id=1, source_target_pairs={{0,1},{1,0},{2,3},{3,2},{4,5},{5,4},{6,7},{7,6},{8,9},{9,8},{10,11... | collective-permute-start | bytes 786440 | tf_op jit(solution)/shard_map/ppermute | solution.py:211
  16.3 15.3 %collective-permute-start = (bf16[256,1024]{1,0:T(8,128)(2,1)S(1)}, bf16[256,1024]{1,0:T(8,128)(2,1)S(1)}, u32[]{:S(2)}, u32[]{:S(2)}) collective-permute-start(bf16[256,1024]{1,0:T(8,128)(2,1)S(1)} %get-tuple-element.25), channel_id=1, source_target_pairs={{0,1},{1,0},{2,3},{3,2},{4,5},{5,4},{6,7},{7,6},{8,9},{9,8},{10,11... | collective-permute-start | bytes 1572872 | tf_op jit(solution)/shard_map/ppermute | solution.py:211
  16.9 5.3 %collective-permute-start.4 = (bf16[32,1024]{1,0:T(8,128)(2,1)S(1)}, bf16[32,1024]{1,0:T(8,128)(2,1)S(1)}, u32[]{:S(2)}, u32[]{:S(2)}) collective-permute-start(bf16[32,1024]{1,0:T(8,128)(2,1)S(1)} %slice.17), channel_id=1, source_target_pairs={{0,2},{1,3},{2,0},{3,1},{4,6},{5,7},{6,4},{7,5},{8,10},{9,11},{10,... | collective-permute-start | bytes 196616 | tf_op jit(solution)/shard_map/ppermute | solution.py:211
  20.5 14.2 %collective-permute-start.2 = (bf16[256,1024]{1,0:T(8,128)(2,1)}, bf16[256,1024]{1,0:T(8,128)(2,1)S(1)}, u32[]{:S(2)}, u32[]{:S(2)}) collective-permute-start(bf16[256,1024]{1,0:T(8,128)(2,1)} %add_convert_fusion), channel_id=1, source_target_pairs={{0,2},{1,3},{2,0},{3,1},{4,6},{5,7},{6,4},{7,5},{8,10},{9,11},{10,... | collective-permute-start | bytes 1572872 | tf_op jit(solution)/shard_map/ppermute | solution.py:211
  22.3 6.6 %collective-permute-start.7 = (bf16[32,1024]{1,0:T(8,128)(2,1)S(1)}, bf16[32,1024]{1,0:T(8,128)(2,1)S(1)}, u32[]{:S(2)}, u32[]{:S(2)}) collective-permute-start(bf16[32,1024]{1,0:T(8,128)(2,1)S(1)} %fusion), channel_id=1, source_target_pairs={{0,12},{1,13},{2,14},{3,15},{4,8},{5,9},{6,10},{7,11},{8,4},{9,5},... | collective-permute-start | bytes 196616 | tf_op jit(solution)/shard_map/ppermute | solution.py:211
  26.2 5.4 %collective-permute-start.6 = (bf16[32,1024]{1,0:T(8,128)(2,1)S(1)}, bf16[32,1024]{1,0:T(8,128)(2,1)S(1)}, u32[]{:S(2)}, u32[]{:S(2)}) collective-permute-start(bf16[32,1024]{1,0:T(8,128)(2,1)S(1)} %fusion), channel_id=1, source_target_pairs={{0,8},{1,9},{2,10},{3,11},{4,12},{5,13},{6,14},{7,15},{8,0},{9,1},... | collective-permute-start | bytes 196616 | tf_op jit(solution)/shard_map/ppermute | solution.py:211
  26.2 5.4 %collective-permute-start.5 = (bf16[32,1024]{1,0:T(8,128)(2,1)S(1)}, bf16[32,1024]{1,0:T(8,128)(2,1)S(1)}, u32[]{:S(2)}, u32[]{:S(2)}) collective-permute-start(bf16[32,1024]{1,0:T(8,128)(2,1)S(1)} %fusion), channel_id=1, source_target_pairs={{0,4},{1,5},{2,6},{3,7},{4,0},{5,1},{6,2},{7,3},{8,12},{9,13},{10,... | collective-permute-start | bytes 196616 | tf_op jit(solution)/shard_map/ppermute | solution.py:211
  35.0 5.0 %collective-permute-start.11 = (f32[32,1024]{1,0:T(8,128)S(1)}, f32[32,1024]{1,0:T(8,128)S(1)}, u32[]{:S(2)}, u32[]{:S(2)}) collective-permute-start(f32[32,1024]{1,0:T(8,128)S(1)} %convert_add_fusion.2), channel_id=1, source_target_pairs={{0,2},{1,3},{2,0},{3,1},{4,6},{5,7},{6,4},{7,5},{8,10},{9,11},{10,... | collective-permute-start | bytes 393224 | tf_op jit(solution)/shard_map/ppermute | solution.py:211
  35.6 7.3 %collective-permute-start.8 = (bf16[64,1024]{1,0:T(8,128)(2,1)S(1)}, bf16[64,1024]{1,0:T(8,128)(2,1)S(1)}, u32[]{:S(2)}, u32[]{:S(2)}) collective-permute-start(bf16[64,1024]{1,0:T(8,128)(2,1)S(1)} %get-tuple-element.29), channel_id=1, source_target_pairs={{0,4},{1,5},{2,6},{3,7},{4,0},{5,1},{6,2},{7,3},{8,12},{9,13},{10,... | collective-permute-start | bytes 393224 | tf_op jit(solution)/shard_map/ppermute | solution.py:211
  37.2 12.1 %collective-permute-start.9 = (bf16[64,1024]{1,0:T(8,128)(2,1)S(1)}, bf16[64,1024]{1,0:T(8,128)(2,1)S(1)}, u32[]{:S(2)}, u32[]{:S(2)}) collective-permute-start(bf16[64,1024]{1,0:T(8,128)(2,1)S(1)} %get-tuple-element.30), channel_id=1, source_target_pairs={{0,8},{1,9},{2,10},{3,11},{4,12},{5,13},{6,14},{7,15},{8,0},{9,1},... | collective-permute-start | bytes 393224 | tf_op jit(solution)/shard_map/ppermute | solution.py:211
  39.8 9.6 %collective-permute-start.10 = (bf16[64,1024]{1,0:T(8,128)(2,1)S(1)}, bf16[64,1024]{1,0:T(8,128)(2,1)S(1)}, u32[]{:S(2)}, u32[]{:S(2)}) collective-permute-start(bf16[64,1024]{1,0:T(8,128)(2,1)S(1)} %get-tuple-element.31), channel_id=1, source_target_pairs={{0,12},{1,13},{2,14},{3,15},{4,8},{5,9},{6,10},{7,11},{8,4},{9,5},... | collective-permute-start | bytes 393224 | tf_op jit(solution)/shard_map/ppermute | solution.py:211
  40.1 1.6 %collective-permute-start.12 = (f32[64,1024]{1,0:T(8,128)S(1)}, f32[64,1024]{1,0:T(8,128)S(1)}, u32[]{:S(2)}, u32[]{:S(2)}) collective-permute-start(f32[64,1024]{1,0:T(8,128)S(1)} %pad_maximum_fusion), channel_id=1, source_target_pairs={{0,1},{1,0},{2,3},{3,2},{4,5},{5,4},{6,7},{7,6},{8,9},{9,8},{10,11... | collective-permute-start | bytes 786440 | tf_op jit(solution)/shard_map/ppermute | solution.py:211

commit v5 on v4

--- a/solution.py
+++ b/solution.py
@@ -10,7 +10,7 @@
 BF16 = jnp.bfloat16
 F32 = jnp.float32
 LANES = 128
-VMEM_LIMIT = 28 * 1024 * 1024
+VMEM_LIMIT = 20 * 1024 * 1024
 
 
 def turned_block(x_ref, here, lane, weight):
@@ -127,14 +127,19 @@
             lanes, lane = slice(b * LANES, (b + 1) * LANES), pl.ds(lane_of(b, parity), LANES)
             cross[kept, lanes] = far_keep[packed, lane]
             cross[sent, lanes] = far_send[packed, lane].astype(F32)
-    total = None
+    total = corner = None
+    middle = width * LANES // 2
     for n in range(chunks):
         here = slice(n * part, n * part + part)
         right = jnp.concatenate([x_ref[here, pl.ds(lane_of(b, parity), LANES)] for b in range(width)], axis=1)
         weight = w_ref[:, here]
         left = jnp.concatenate([turned_block(x_ref, here, lane_of(b, parity), weight) for b in range(width)], axis=0)
-        term = jnp.dot(left, right, preferred_element_type=F32)
+        term = jnp.dot(left[:middle], right, preferred_element_type=F32)
         total = term if total is None else total + term
+        term = jnp.dot(left[middle:], right[:, middle:], preferred_element_type=F32)
+        corner = term if corner is None else corner + term
+    corner = jnp.concatenate([total[:, middle:].T, corner], axis=1)
+    total = jnp.concatenate([total, corner], axis=0)
     turned = cross[...].T
     for b in range(width):
         lanes = slice(b * LANES, (b + 1) * LANES)
@@ -218,6 +223,7 @@
         place, features, coef, labels, passage_id, slot_of, per_owner, blk
     )
     masks = [m for m in range(1, devices) if not m & 1 and not m & turn]
+    masks = masks[1:] + masks[:1]
     far_in, sums_in = swap(far_send, 1), swap(sums_send, 1)
     near_send, near_keep = second(place, x, w, far_send, far_keep, blk)
     near_in = swap(near_send, 1)

time: 50.3 us -> 49 us (0.974)
  waiting for transfers between devices: 16.9 us -> 16.3 us
    ppermute x13, waiting for transfers between devices: 16.9 us -> 16.3 us  [swap(): return lax.ppermute(array, 'rows', [(i, i ^ mask) for i in range(devices)])]
  transfers between devices with their start and end apart: 13 -> 13, of which waited for: 7 -> 8; matrix products, arithmetic and copies ran while one was open for 6% -> 6% of each run, Pallas kernels for 7% -> 6%
where the time goes in v5:
time: 49 us; the launch traced here: 48.8 us
  waiting for transfers between devices  16.3 us (33%)
  Pallas kernels  14.6 us (30%)
  starting transfers between devices  13.1 us (27%)
  other arithmetic  2.14 us (4%)
  matrix products  1.19 us (2%)
  between operations  0.74 us (2%)
  local copies, waits for them, and re-layouts  0.73 us (1%)
    ppermute x13, waiting for transfers between devices, swap(): return lax.ppermute(array, 'rows', [(i, i ^ mask) for i in range(devices)])  16.3 us
    ppermute x13, starting transfers between devices, swap(): return lax.ppermute(array, 'rows', [(i, i ^ mask) for i in range(devices)])  13.1 us
    pallas_call x1, Pallas kernels, first(): pl.pallas_call(functools.partial(first_kernel, per_owner, blk, chunks), i...  11.6 us
    pallas_call x1, Pallas kernels, second(): pl.pallas_call(functools.partial(second_kernel, blk, chunks), in_specs=[p...  3.03 us
    dot_general x1, matrix products, local(): lax.dot_general(columns, stack, (((0,), (0,)), ((), ())), precision=lax.P...  1.19 us
  transfers between devices with their start and end apart: 13, of which 8 were waited for; matrix products, arithmetic and copies ran while one was open for 6% of the time, Pallas kernels for 6%

profile of v5, /device:TPU:0, one launch (start us, length us, event | category | flops | bytes accessed | tf_op | source)
XLA Modules:
  0.0 48.8 jit_solution(16691348940561151507)
XLA Ops:
  0.6 0.1 pad_add_fusion.place
  0.7 11.6 %scores_and_far.1 = (bf16[4096,1024]{1,0:T(8,128)(2,1)S(1)}, f32[1,4096]{1,0:T(1,128)S(1)}, f32[64,1024]{1,0:T(8,128)S(1)}, f32[64,1024]{1,0:T(8,128)S(1)}, bf16...) custom-call(s32[2]{0:T(128)S(1)} %pad_add_fusion.place, bf16[4096,1024]{1,0:T(8,128)(2,1)} %x_hbm.1, ...), custom_call_target="tpu_custom_call" | custom-call | tf_op jit(solution)/shard_map/scores_and_far/pallas_call | solution.py:162
  12.3 0.5 %collective-permute-start.1 = (bf16[256,1024]{1,0:T(8,128)(2,1)S(1)}, bf16[256,1024]{1,0:T(8,128)(2,1)S(1)}, u32[]{:S(2)}, u32[]{:S(2)}) collective-permute-start(bf16[256,1024]{1,0:T(8,128)(2,1)S(1)} %get-tuple-element.22.far_send), channel_id=1, source_target_pairs={{0,1},{1,0},{2,3},{3,2},{4,5},{5,4},{6,7},{7,6},{8,9},{9,8},{10,11... | collective-permute-start | bytes 1572872 | tf_op jit(solution)/shard_map/ppermute | solution.py:216
  12.9 0.1 collective-permute-start.3
  12.9 3.0 %near.1 = (bf16[256,1024]{1,0:T(8,128)(2,1)S(1)}, f32[256,1024]{1,0:T(8,128)S(1)}) custom-call(s32[2]{0:T(128)S(1)} %pad_add_fusion.place, bf16[4096,1024]{1,0:T(8,128)(2,1)S(1)} %get-tuple-element.20.x_ref, f32[1,4096]{1,0:T(1,128)S(1)} %get-tuple-element.21.w_ref, bf16[256,1024]{1,0:T(8,128)(2,1)S(1)} %get-tuple-element.22.far_send, ...), custom_call_target="tpu_custom_call" | custom-call | tf_op jit(solution)/shard_map/near/pallas_call | solution.py:191
  16.0 0.5 %collective-permute-start = (bf16[256,1024]{1,0:T(8,128)(2,1)S(1)}, bf16[256,1024]{1,0:T(8,128)(2,1)S(1)}, u32[]{:S(2)}, u32[]{:S(2)}) collective-permute-start(bf16[256,1024]{1,0:T(8,128)(2,1)S(1)} %get-tuple-element.25), channel_id=1, source_target_pairs={{0,1},{1,0},{2,3},{3,2},{4,5},{5,4},{6,7},{7,6},{8,9},{9,8},{10,11... | collective-permute-start | bytes 1572872 | tf_op jit(solution)/shard_map/ppermute | solution.py:216
  16.5 0.0 collective-permute-done.3
  16.5 2.7 %collective-permute-start.4 = (bf16[32,1024]{1,0:T(8,128)(2,1)S(1)}, bf16[32,1024]{1,0:T(8,128)(2,1)S(1)}, u32[]{:S(2)}, u32[]{:S(2)}) collective-permute-start(bf16[32,1024]{1,0:T(8,128)(2,1)S(1)} %slice.17), channel_id=1, source_target_pairs={{0,2},{1,3},{2,0},{3,1},{4,6},{5,7},{6,4},{7,5},{8,10},{9,11},{10,... | collective-permute-start | bytes 196616 | tf_op jit(solution)/shard_map/ppermute | solution.py:216
  19.2 0.0 collective-permute-done.1
  19.2 1.0 %add_convert_fusion = bf16[256,1024]{1,0:T(8,128)(2,1)} fusion(f32[256,1024]{1,0:T(8,128)S(1)} %get-tuple-element.23.far_keep, bf16[256,1024]{1,0:T(8,128)(2,1)S(1)} %collective-permute-done.1), kind=kLoop, calls=%fused_computation.1 | loop fusion | flops 786432 | bytes 2097152 | tf_op jit(solution)/shard_map/convert_element_type | solution.py:230
  20.1 0.0 collective-permute-start.2
  20.2 1.7 %collective-permute-done.4 = bf16[32,1024]{1,0:T(8,128)(2,1)S(1)} collective-permute-done((bf16[32,1024]{1,0:T(8,128)(2,1)S(1)}, bf16[32,1024]{1,0:T(8,128)(2,1)S(1)}, u32[]{:S(2)}, u32[]{:S(2)}) %collective-permute-start.4) | collective-permute-done | bytes 65568 | tf_op jit(solution)/shard_map/ppermute | solution.py:216
  21.9 1.9 %collective-permute-start.7 = (bf16[32,1024]{1,0:T(8,128)(2,1)S(1)}, bf16[32,1024]{1,0:T(8,128)(2,1)S(1)}, u32[]{:S(2)}, u32[]{:S(2)}) collective-permute-start(bf16[32,1024]{1,0:T(8,128)(2,1)S(1)} %fusion), channel_id=1, source_target_pairs={{0,4},{1,5},{2,6},{3,7},{4,0},{5,1},{6,2},{7,3},{8,12},{9,13},{10,... | collective-permute-start | bytes 196616 | tf_op jit(solution)/shard_map/ppermute | solution.py:216
  23.8 2.5 %collective-permute-start.6 = (bf16[32,1024]{1,0:T(8,128)(2,1)S(1)}, bf16[32,1024]{1,0:T(8,128)(2,1)S(1)}, u32[]{:S(2)}, u32[]{:S(2)}) collective-permute-start(bf16[32,1024]{1,0:T(8,128)(2,1)S(1)} %fusion), channel_id=1, source_target_pairs={{0,12},{1,13},{2,14},{3,15},{4,8},{5,9},{6,10},{7,11},{8,4},{9,5},... | collective-permute-start | bytes 196616 | tf_op jit(solution)/shard_map/ppermute | solution.py:216
  26.2 0.1 collective-permute-start.5
  26.4 0.0 collective-permute-done.7
  26.4 4.1 %collective-permute-done.6 = bf16[32,1024]{1,0:T(8,128)(2,1)S(1)} collective-permute-done((bf16[32,1024]{1,0:T(8,128)(2,1)S(1)}, bf16[32,1024]{1,0:T(8,128)(2,1)S(1)}, u32[]{:S(2)}, u32[]{:S(2)}) %collective-permute-start.6) | collective-permute-done | bytes 65568 | tf_op jit(solution)/shard_map/ppermute | solution.py:216
  30.5 2.1 %collective-permute-done.5 = bf16[32,1024]{1,0:T(8,128)(2,1)S(1)} collective-permute-done((bf16[32,1024]{1,0:T(8,128)(2,1)S(1)}, bf16[32,1024]{1,0:T(8,128)(2,1)S(1)}, u32[]{:S(2)}, u32[]{:S(2)}) %collective-permute-start.5) | collective-permute-done | bytes 65568 | tf_op jit(solution)/shard_map/ppermute | solution.py:216
  32.6 0.0 collective-permute-done
  32.6 1.8 %collective-permute-done.2 = bf16[256,1024]{1,0:T(8,128)(2,1)S(1)} collective-permute-done((bf16[256,1024]{1,0:T(8,128)(2,1)}, bf16[256,1024]{1,0:T(8,128)(2,1)S(1)}, u32[]{:S(2)}, u32[]{:S(2)}) %collective-permute-start.2) | collective-permute-done | bytes 524320 | tf_op jit(solution)/shard_map/ppermute | solution.py:216
  34.3 0.2 convert_add_fusion
  34.6 0.1 dynamic-slice_convert_fusion
  34.6 0.6 %collective-permute-start.11 = (f32[32,1024]{1,0:T(8,128)S(1)}, f32[32,1024]{1,0:T(8,128)S(1)}, u32[]{:S(2)}, u32[]{:S(2)}) collective-permute-start(f32[32,1024]{1,0:T(8,128)S(1)} %convert_add_fusion.2), channel_id=1, source_target_pairs={{0,2},{1,3},{2,0},{3,1},{4,6},{5,7},{6,4},{7,5},{8,10},{9,11},{10,... | collective-permute-start | bytes 393224 | tf_op jit(solution)/shard_map/ppermute | solution.py:216
  35.2 2.6 %collective-permute-start.8 = (bf16[64,1024]{1,0:T(8,128)(2,1)S(1)}, bf16[64,1024]{1,0:T(8,128)(2,1)S(1)}, u32[]{:S(2)}, u32[]{:S(2)}) collective-permute-start(bf16[64,1024]{1,0:T(8,128)(2,1)S(1)} %get-tuple-element.29), channel_id=1, source_target_pairs={{0,8},{1,9},{2,10},{3,11},{4,12},{5,13},{6,14},{7,15},{8,0},{9,1},... | collective-permute-start | bytes 393224 | tf_op jit(solution)/shard_map/ppermute | solution.py:216
  37.8 1.3 %collective-permute-start.9 = (bf16[64,1024]{1,0:T(8,128)(2,1)S(1)}, bf16[64,1024]{1,0:T(8,128)(2,1)S(1)}, u32[]{:S(2)}, u32[]{:S(2)}) collective-permute-start(bf16[64,1024]{1,0:T(8,128)(2,1)S(1)} %get-tuple-element.30), channel_id=1, source_target_pairs={{0,12},{1,13},{2,14},{3,15},{4,8},{5,9},{6,10},{7,11},{8,4},{9,5},... | collective-permute-start | bytes 393224 | tf_op jit(solution)/shard_map/ppermute | solution.py:216
  39.2 0.2 collective-permute-start.10
  39.4 0.3 collective-permute-done.11
  39.7 0.1 collective-permute-start.12
  39.8 0.6 %constant_dynamic-slice_fusion = f32[8,1024]{1,0:T(8,128)} fusion(f32[32,1024]{1,0:T(8,128)S(1)} %convert_add_fusion.2, s32[]{:T(128)S(6)} %select_n.60), kind=kLoop, calls=%fused_computation.16 | loop fusion | bytes 65540 | tf_op jit(solution)/shard_map/dynamic_slice | solution.py:247
  40.4 0.9 %collective-permute-done.12 = f32[64,1024]{1,0:T(8,128)S(1)} collective-permute-done((f32[64,1024]{1,0:T(8,128)S(1)}, f32[64,1024]{1,0:T(8,128)S(1)}, u32[]{:S(2)}, u32[]{:S(2)}) %collective-permute-start.12) | collective-permute-done | bytes 262176 | tf_op jit(solution)/shard_map/ppermute | solution.py:216
  41.3 1.2 %fusion.1 = f32[64,1024]{1,0:T(8,128)} fusion(f32[128,1024]{1,0:T(8,128)S(1)} %constant_dynamic-update-slice_fusion, s32[]{:T(128)S(6)} %select_n.59), kind=kOutput, calls=%fused_computation.11 | convolution fusion | flops 100663296 | bytes 851972 | tf_op jit(solution)/shard_map/dot_general | solution.py:251
  42.5 4.9 %collective-permute-done.8 = bf16[64,1024]{1,0:T(8,128)(2,1)S(1)} collective-permute-done((bf16[64,1024]{1,0:T(8,128)(2,1)S(1)}, bf16[64,1024]{1,0:T(8,128)(2,1)S(1)}, u32[]{:S(2)}, u32[]{:S(2)}) %collective-permute-start.8) | collective-permute-done | bytes 131104 | tf_op jit(solution)/shard_map/ppermute | solution.py:216
  47.4 0.0 collective-permute-done.9
  47.4 0.6 %collective-permute-done.10 = bf16[64,1024]{1,0:T(8,128)(2,1)S(1)} collective-permute-done((bf16[64,1024]{1,0:T(8,128)(2,1)S(1)}, bf16[64,1024]{1,0:T(8,128)(2,1)S(1)}, u32[]{:S(2)}, u32[]{:S(2)}) %collective-permute-start.10) | collective-permute-done | bytes 131104 | tf_op jit(solution)/shard_map/ppermute | solution.py:216
  48.0 0.8 %convert_add_fusion.1 = f32[64,1024]{1,0:T(8,128)} fusion(bf16[64,1024]{1,0:T(8,128)(2,1)S(1)} %collective-permute-done.10, bf16[64,1024]{1,0:T(8,128)(2,1)S(1)} %collective-permute-done.9, bf16[64,1024]{1,0:T(8,128)(2,1)S(1)} %collective-permute-done.8, f32[256,1024]{1,0:T(8,128)S(1)} %convert_add_fusion, s32[]{:T(128)S(6)} %select_n.55), kind=kLoop, calls=%fused_computation.3 | loop fusion | flops 393216 | bytes 917508 | tf_op jit(solution)/shard_map/add | solution.py:260
  (8 shorter events, 0.2 us)
Async XLA Ops:
  12.3 6.8 %collective-permute-start.1 = (bf16[256,1024]{1,0:T(8,128)(2,1)S(1)}, bf16[256,1024]{1,0:T(8,128)(2,1)S(1)}, u32[]{:S(2)}, u32[]{:S(2)}) collective-permute-start(bf16[256,1024]{1,0:T(8,128)(2,1)S(1)} %get-tuple-element.22.far_send), channel_id=1, source_target_pairs={{0,1},{1,0},{2,3},{3,2},{4,5},{5,4},{6,7},{7,6},{8,9},{9,8},{10,11... | collective-permute-start | bytes 1572872 | tf_op jit(solution)/shard_map/ppermute | solution.py:216
  12.9 3.6 %collective-permute-start.3 = (f32[64,1024]{1,0:T(8,128)S(1)}, f32[64,1024]{1,0:T(8,128)S(1)}, u32[]{:S(2)}, u32[]{:S(2)}) collective-permute-start(f32[64,1024]{1,0:T(8,128)S(1)} %get-tuple-element.28), channel_id=1, source_target_pairs={{0,1},{1,0},{2,3},{3,2},{4,5},{5,4},{6,7},{7,6},{8,9},{9,8},{10,11... | collective-permute-start | bytes 786440 | tf_op jit(solution)/shard_map/ppermute | solution.py:216
  16.0 16.6 %collective-permute-start = (bf16[256,1024]{1,0:T(8,128)(2,1)S(1)}, bf16[256,1024]{1,0:T(8,128)(2,1)S(1)}, u32[]{:S(2)}, u32[]{:S(2)}) collective-permute-start(bf16[256,1024]{1,0:T(8,128)(2,1)S(1)} %get-tuple-element.25), channel_id=1, source_target_pairs={{0,1},{1,0},{2,3},{3,2},{4,5},{5,4},{6,7},{7,6},{8,9},{9,8},{10,11... | collective-permute-start | bytes 1572872 | tf_op jit(solution)/shard_map/ppermute | solution.py:216
  16.5 5.3 %collective-permute-start.4 = (bf16[32,1024]{1,0:T(8,128)(2,1)S(1)}, bf16[32,1024]{1,0:T(8,128)(2,1)S(1)}, u32[]{:S(2)}, u32[]{:S(2)}) collective-permute-start(bf16[32,1024]{1,0:T(8,128)(2,1)S(1)} %slice.17), channel_id=1, source_target_pairs={{0,2},{1,3},{2,0},{3,1},{4,6},{5,7},{6,4},{7,5},{8,10},{9,11},{10,... | collective-permute-start | bytes 196616 | tf_op jit(solution)/shard_map/ppermute | solution.py:216
  20.1 14.2 %collective-permute-start.2 = (bf16[256,1024]{1,0:T(8,128)(2,1)}, bf16[256,1024]{1,0:T(8,128)(2,1)S(1)}, u32[]{:S(2)}, u32[]{:S(2)}) collective-permute-start(bf16[256,1024]{1,0:T(8,128)(2,1)} %add_convert_fusion), channel_id=1, source_target_pairs={{0,2},{1,3},{2,0},{3,1},{4,6},{5,7},{6,4},{7,5},{8,10},{9,11},{10,... | collective-permute-start | bytes 1572872 | tf_op jit(solution)/shard_map/ppermute | solution.py:216
  21.9 4.5 %collective-permute-start.7 = (bf16[32,1024]{1,0:T(8,128)(2,1)S(1)}, bf16[32,1024]{1,0:T(8,128)(2,1)S(1)}, u32[]{:S(2)}, u32[]{:S(2)}) collective-permute-start(bf16[32,1024]{1,0:T(8,128)(2,1)S(1)} %fusion), channel_id=1, source_target_pairs={{0,4},{1,5},{2,6},{3,7},{4,0},{5,1},{6,2},{7,3},{8,12},{9,13},{10,... | collective-permute-start | bytes 196616 | tf_op jit(solution)/shard_map/ppermute | solution.py:216
  23.8 6.7 %collective-permute-start.6 = (bf16[32,1024]{1,0:T(8,128)(2,1)S(1)}, bf16[32,1024]{1,0:T(8,128)(2,1)S(1)}, u32[]{:S(2)}, u32[]{:S(2)}) collective-permute-start(bf16[32,1024]{1,0:T(8,128)(2,1)S(1)} %fusion), channel_id=1, source_target_pairs={{0,12},{1,13},{2,14},{3,15},{4,8},{5,9},{6,10},{7,11},{8,4},{9,5},... | collective-permute-start | bytes 196616 | tf_op jit(solution)/shard_map/ppermute | solution.py:216
  26.2 6.3 %collective-permute-start.5 = (bf16[32,1024]{1,0:T(8,128)(2,1)S(1)}, bf16[32,1024]{1,0:T(8,128)(2,1)S(1)}, u32[]{:S(2)}, u32[]{:S(2)}) collective-permute-start(bf16[32,1024]{1,0:T(8,128)(2,1)S(1)} %fusion), channel_id=1, source_target_pairs={{0,8},{1,9},{2,10},{3,11},{4,12},{5,13},{6,14},{7,15},{8,0},{9,1},... | collective-permute-start | bytes 196616 | tf_op jit(solution)/shard_map/ppermute | solution.py:216
  34.6 5.0 %collective-permute-start.11 = (f32[32,1024]{1,0:T(8,128)S(1)}, f32[32,1024]{1,0:T(8,128)S(1)}, u32[]{:S(2)}, u32[]{:S(2)}) collective-permute-start(f32[32,1024]{1,0:T(8,128)S(1)} %convert_add_fusion.2), channel_id=1, source_target_pairs={{0,2},{1,3},{2,0},{3,1},{4,6},{5,7},{6,4},{7,5},{8,10},{9,11},{10,... | collective-permute-start | bytes 393224 | tf_op jit(solution)/shard_map/ppermute | solution.py:216
  35.2 12.2 %collective-permute-start.8 = (bf16[64,1024]{1,0:T(8,128)(2,1)S(1)}, bf16[64,1024]{1,0:T(8,128)(2,1)S(1)}, u32[]{:S(2)}, u32[]{:S(2)}) collective-permute-start(bf16[64,1024]{1,0:T(8,128)(2,1)S(1)} %get-tuple-element.29), channel_id=1, source_target_pairs={{0,8},{1,9},{2,10},{3,11},{4,12},{5,13},{6,14},{7,15},{8,0},{9,1},... | collective-permute-start | bytes 393224 | tf_op jit(solution)/shard_map/ppermute | solution.py:216
  37.8 9.6 %collective-permute-start.9 = (bf16[64,1024]{1,0:T(8,128)(2,1)S(1)}, bf16[64,1024]{1,0:T(8,128)(2,1)S(1)}, u32[]{:S(2)}, u32[]{:S(2)}) collective-permute-start(bf16[64,1024]{1,0:T(8,128)(2,1)S(1)} %get-tuple-element.30), channel_id=1, source_target_pairs={{0,12},{1,13},{2,14},{3,15},{4,8},{5,9},{6,10},{7,11},{8,4},{9,5},... | collective-permute-start | bytes 393224 | tf_op jit(solution)/shard_map/ppermute | solution.py:216
  39.2 8.9 %collective-permute-start.10 = (bf16[64,1024]{1,0:T(8,128)(2,1)S(1)}, bf16[64,1024]{1,0:T(8,128)(2,1)S(1)}, u32[]{:S(2)}, u32[]{:S(2)}) collective-permute-start(bf16[64,1024]{1,0:T(8,128)(2,1)S(1)} %get-tuple-element.31), channel_id=1, source_target_pairs={{0,4},{1,5},{2,6},{3,7},{4,0},{5,1},{6,2},{7,3},{8,12},{9,13},{10,... | collective-permute-start | bytes 393224 | tf_op jit(solution)/shard_map/ppermute | solution.py:216
  39.7 1.6 %collective-permute-start.12 = (f32[64,1024]{1,0:T(8,128)S(1)}, f32[64,1024]{1,0:T(8,128)S(1)}, u32[]{:S(2)}, u32[]{:S(2)}) collective-permute-start(f32[64,1024]{1,0:T(8,128)S(1)} %pad_maximum_fusion), channel_id=1, source_target_pairs={{0,1},{1,0},{2,3},{3,2},{4,5},{5,4},{6,7},{7,6},{8,9},{9,8},{10,11... | collective-permute-start | bytes 786440 | tf_op jit(solution)/shard_map/ppermute | solution.py:216

commit v6 on v5

--- a/solution.py
+++ b/solution.py
@@ -225,17 +225,17 @@
     masks = [m for m in range(1, devices) if not m & 1 and not m & turn]
     masks = masks[1:] + masks[:1]
     far_in, sums_in = swap(far_send, 1), swap(sums_send, 1)
+    far = (far_keep + far_in.astype(F32)).astype(BF16)
+    sums = sums_keep + sums_in
+    quarter = clusters // 4
+    sums_far, sums_near = sums[:quarter].astype(BF16), sums[quarter:]
+    w, _ = lax.optimization_barrier((w, (far, sums_far)))
     near_send, near_keep = second(place, x, w, far_send, far_keep, blk)
     near_in = swap(near_send, 1)
-    far = (far_keep + far_in.astype(F32)).astype(BF16)
-    sums_keep, _ = lax.optimization_barrier((sums_keep, near_keep))
-    sums = sums_keep + sums_in
-    quarter = clusters // 4
-    sums_far, sums_near = sums[:quarter], sums[quarter:]
-    sums = sums_near + swap(sums_far.astype(BF16), turn).astype(F32)
+    sums = sums_near + swap(sums_far, turn).astype(F32)
     arrived = swap(far, turn)
     sums_out = sums.astype(BF16)
-    sums_parts = [swap(sums_out, m) for m in masks]
+    sums_parts = [swap(sums_out, m) for m in sorted(masks)]
     near = near_keep + near_in.astype(F32) + arrived.astype(F32)
     block = lambda n: lax.dynamic_slice_in_dim(near, (rest(me) ^ n) * blk, blk, 0)
     hessian = block(0)

time: 49 us -> 48.1 us (0.982)
  waiting for transfers between devices: 16.3 us -> 14 us
  starting transfers between devices: 13.1 us -> 14.2 us
    ppermute x13, waiting for transfers between devices: 16.3 us -> 14 us  [swap(): return lax.ppermute(array, 'rows', [(i, i ^ mask) for i in range(devices)])]
    ppermute x13, starting transfers between devices: 13.1 us -> 14.2 us  [swap(): return lax.ppermute(array, 'rows', [(i, i ^ mask) for i in range(devices)])]
    add x1, other arithmetic: 0.24 us -> 1.28 us  [local(): near = near_keep + near_in.astype(F32) + arrived.astype(F32)]
    convert_element_type x1, other arithmetic: 0.95 us -> 0.16 us  [local(): far = (far_keep + far_in.astype(F32)).astype(BF16)]
  transfers between devices with their start and end apart: 13 -> 13, of which waited for: 8 -> 7; matrix products, arithmetic and copies ran while one was open for 6% -> 4% of each run, Pallas kernels for 6% -> 6%
where the time goes in v6:
time: 48.1 us; the launch traced here: 47.9 us
  Pallas kernels  14.6 us (30%)
  starting transfers between devices  14.2 us (30%)
  waiting for transfers between devices  14 us (29%)
  other arithmetic  2.39 us (5%)
  matrix products  1.19 us (2%)
  between operations  0.76 us (2%)
  local copies, waits for them, and re-layouts  0.73 us (2%)
    ppermute x13, starting transfers between devices, swap(): return lax.ppermute(array, 'rows', [(i, i ^ mask) for i in range(devices)])  14.2 us
    ppermute x13, waiting for transfers between devices, swap(): return lax.ppermute(array, 'rows', [(i, i ^ mask) for i in range(devices)])  14 us
    pallas_call x1, Pallas kernels, first(): pl.pallas_call(functools.partial(first_kernel, per_owner, blk, chunks), i...  11.6 us
    pallas_call x1, Pallas kernels, second(): pl.pallas_call(functools.partial(second_kernel, blk, chunks), in_specs=[p...  3.02 us
    add x1, other arithmetic, local(): near = near_keep + near_in.astype(F32) + arrived.astype(F32)  1.28 us
    dot_general x1, matrix products, local(): lax.dot_general(columns, stack, (((0,), (0,)), ((), ())), precision=lax.P...  1.19 us
  transfers between devices with their start and end apart: 13, of which 7 were waited for; matrix products, arithmetic and copies ran while one was open for 4% of the time, Pallas kernels for 6%

profile of v6, /device:TPU:0, one launch (start us, length us, event | category | flops | bytes accessed | tf_op | source)
XLA Modules:
  0.0 47.9 jit_solution(1847040196298640710)
XLA Ops:
  0.6 0.1 pad_add_fusion.place
  0.7 11.6 %scores_and_far.1 = (bf16[4096,1024]{1,0:T(8,128)(2,1)S(1)}, f32[1,4096]{1,0:T(1,128)S(1)}, f32[64,1024]{1,0:T(8,128)S(1)}, f32[64,1024]{1,0:T(8,128)S(1)}, bf16...) custom-call(s32[2]{0:T(128)S(1)} %pad_add_fusion.place, bf16[4096,1024]{1,0:T(8,128)(2,1)} %x_hbm.1, ...), custom_call_target="tpu_custom_call" | custom-call | tf_op jit(solution)/shard_map/scores_and_far/pallas_call | solution.py:162
  12.3 0.5 %collective-permute-start = (bf16[256,1024]{1,0:T(8,128)(2,1)S(1)}, bf16[256,1024]{1,0:T(8,128)(2,1)S(1)}, u32[]{:S(2)}, u32[]{:S(2)}) collective-permute-start(bf16[256,1024]{1,0:T(8,128)(2,1)S(1)} %get-tuple-element.23.far_send), channel_id=1, source_target_pairs={{0,1},{1,0},{2,3},{3,2},{4,5},{5,4},{6,7},{7,6},{8,9},{9,8},{10,11... | collective-permute-start | bytes 1572872 | tf_op jit(solution)/shard_map/ppermute | solution.py:216
  12.9 0.1 collective-permute-start.1
  12.9 1.8 %collective-permute-done.1 = f32[64,1024]{1,0:T(8,128)S(1)} collective-permute-done((f32[64,1024]{1,0:T(8,128)S(1)}, f32[64,1024]{1,0:T(8,128)S(1)}, u32[]{:S(2)}, u32[]{:S(2)}) %collective-permute-start.1) | collective-permute-done | bytes 262176 | tf_op jit(solution)/shard_map/ppermute | solution.py:216
  14.8 2.9 %collective-permute-start.4 = (bf16[32,1024]{1,0:T(8,128)(2,1)S(1)}, bf16[32,1024]{1,0:T(8,128)(2,1)S(1)}, u32[]{:S(2)}, u32[]{:S(2)}) collective-permute-start(bf16[32,1024]{1,0:T(8,128)(2,1)S(1)} %slice.17), channel_id=1, source_target_pairs={{0,2},{1,3},{2,0},{3,1},{4,6},{5,7},{6,4},{7,5},{8,10},{9,11},{10,... | collective-permute-start | bytes 196616 | tf_op jit(solution)/shard_map/ppermute | solution.py:216
  17.8 0.0 collective-permute-done
  17.8 0.2 add_convert_fusion
  17.9 0.1 collective-permute-start.3
  18.0 3.0 %near.1 = (bf16[256,1024]{1,0:T(8,128)(2,1)S(1)}, f32[256,1024]{1,0:T(8,128)S(1)}) custom-call(s32[2]{0:T(128)S(1)} %pad_add_fusion.place, bf16[4096,1024]{1,0:T(8,128)(2,1)S(1)} %get-tuple-element.20.x_ref, f32[1,4096]{1,0:T(1,128)S(1)} %get-tuple-element.26.w_ref, bf16[256,1024]{1,0:T(8,128)(2,1)S(1)} %get-tuple-element.23.far_send, ...), custom_call_target="tpu_custom_call" | custom-call | tf_op jit(solution)/shard_map/near/pallas_call | solution.py:191
  21.1 0.1 collective-permute-start.2
  21.1 0.0 collective-permute-done.4
  21.2 4.2 %collective-permute-start.7 = (bf16[32,1024]{1,0:T(8,128)(2,1)S(1)}, bf16[32,1024]{1,0:T(8,128)(2,1)S(1)}, u32[]{:S(2)}, u32[]{:S(2)}) collective-permute-start(bf16[32,1024]{1,0:T(8,128)(2,1)S(1)} %fusion), channel_id=1, source_target_pairs={{0,12},{1,13},{2,14},{3,15},{4,8},{5,9},{6,10},{7,11},{8,4},{9,5},... | collective-permute-start | bytes 196616 | tf_op jit(solution)/shard_map/ppermute | solution.py:216
  25.3 0.0 collective-permute-start.6
  25.3 0.6 %collective-permute-start.5 = (bf16[32,1024]{1,0:T(8,128)(2,1)S(1)}, bf16[32,1024]{1,0:T(8,128)(2,1)S(1)}, u32[]{:S(2)}, u32[]{:S(2)}) collective-permute-start(bf16[32,1024]{1,0:T(8,128)(2,1)S(1)} %fusion), channel_id=1, source_target_pairs={{0,4},{1,5},{2,6},{3,7},{4,0},{5,1},{6,2},{7,3},{8,12},{9,13},{10,... | collective-permute-start | bytes 196616 | tf_op jit(solution)/shard_map/ppermute | solution.py:216
  26.0 2.3 %collective-permute-done.7 = bf16[32,1024]{1,0:T(8,128)(2,1)S(1)} collective-permute-done((bf16[32,1024]{1,0:T(8,128)(2,1)S(1)}, bf16[32,1024]{1,0:T(8,128)(2,1)S(1)}, u32[]{:S(2)}, u32[]{:S(2)}) %collective-permute-start.7) | collective-permute-done | bytes 65568 | tf_op jit(solution)/shard_map/ppermute | solution.py:216
  28.3 3.2 %collective-permute-done.6 = bf16[32,1024]{1,0:T(8,128)(2,1)S(1)} collective-permute-done((bf16[32,1024]{1,0:T(8,128)(2,1)S(1)}, bf16[32,1024]{1,0:T(8,128)(2,1)S(1)}, u32[]{:S(2)}, u32[]{:S(2)}) %collective-permute-start.6) | collective-permute-done | bytes 65568 | tf_op jit(solution)/shard_map/ppermute | solution.py:216
  31.4 0.0 collective-permute-done.5
  31.5 0.2 collective-permute-done.3
  31.7 0.0 collective-permute-done.2
  31.7 1.3 %convert_add_fusion = f32[256,1024]{1,0:T(8,128)S(1)} fusion(bf16[256,1024]{1,0:T(8,128)(2,1)S(1)} %collective-permute-done.3, f32[256,1024]{1,0:T(8,128)S(1)} %get-tuple-element.27, bf16[256,1024]{1,0:T(8,128)(2,1)} %collective-permute-done.2), kind=kLoop, calls=%fused_computation | loop fusion | flops 1048576 | bytes 3145728 | tf_op jit(solution)/shard_map/add | solution.py:239
  33.0 0.1 dynamic-slice_convert_fusion
  33.0 1.5 %collective-permute-start.11 = (f32[32,1024]{1,0:T(8,128)S(1)}, f32[32,1024]{1,0:T(8,128)S(1)}, u32[]{:S(2)}, u32[]{:S(2)}) collective-permute-start(f32[32,1024]{1,0:T(8,128)S(1)} %convert_add_fusion.2), channel_id=1, source_target_pairs={{0,2},{1,3},{2,0},{3,1},{4,6},{5,7},{6,4},{7,5},{8,10},{9,11},{10,... | collective-permute-start | bytes 393224 | tf_op jit(solution)/shard_map/ppermute | solution.py:216
  34.6 2.6 %collective-permute-start.8 = (bf16[64,1024]{1,0:T(8,128)(2,1)S(1)}, bf16[64,1024]{1,0:T(8,128)(2,1)S(1)}, u32[]{:S(2)}, u32[]{:S(2)}) collective-permute-start(bf16[64,1024]{1,0:T(8,128)(2,1)S(1)} %get-tuple-element.29), channel_id=1, source_target_pairs={{0,8},{1,9},{2,10},{3,11},{4,12},{5,13},{6,14},{7,15},{8,0},{9,1},... | collective-permute-start | bytes 393224 | tf_op jit(solution)/shard_map/ppermute | solution.py:216
  37.1 1.4 %collective-permute-start.9 = (bf16[64,1024]{1,0:T(8,128)(2,1)S(1)}, bf16[64,1024]{1,0:T(8,128)(2,1)S(1)}, u32[]{:S(2)}, u32[]{:S(2)}) collective-permute-start(bf16[64,1024]{1,0:T(8,128)(2,1)S(1)} %get-tuple-element.30), channel_id=1, source_target_pairs={{0,12},{1,13},{2,14},{3,15},{4,8},{5,9},{6,10},{7,11},{8,4},{9,5},... | collective-permute-start | bytes 393224 | tf_op jit(solution)/shard_map/ppermute | solution.py:216
  38.5 0.2 collective-permute-start.10
  38.7 0.0 collective-permute-done.11
  38.7 0.1 collective-permute-start.12
  38.8 0.6 %constant_dynamic-slice_fusion = f32[8,1024]{1,0:T(8,128)} fusion(f32[32,1024]{1,0:T(8,128)S(1)} %convert_add_fusion.2, s32[]{:T(128)S(6)} %select_n.60), kind=kLoop, calls=%fused_computation.16 | loop fusion | bytes 65540 | tf_op jit(solution)/shard_map/dynamic_slice | solution.py:247
  39.5 0.9 %collective-permute-done.12 = f32[64,1024]{1,0:T(8,128)S(1)} collective-permute-done((f32[64,1024]{1,0:T(8,128)S(1)}, f32[64,1024]{1,0:T(8,128)S(1)}, u32[]{:S(2)}, u32[]{:S(2)}) %collective-permute-start.12) | collective-permute-done | bytes 262176 | tf_op jit(solution)/shard_map/ppermute | solution.py:216
  40.4 1.2 %fusion.1 = f32[64,1024]{1,0:T(8,128)} fusion(f32[128,1024]{1,0:T(8,128)S(1)} %constant_dynamic-update-slice_fusion, s32[]{:T(128)S(6)} %select_n.59), kind=kOutput, calls=%fused_computation.11 | convolution fusion | flops 100663296 | bytes 851972 | tf_op jit(solution)/shard_map/dot_general | solution.py:251
  41.6 5.1 %collective-permute-done.8 = bf16[64,1024]{1,0:T(8,128)(2,1)S(1)} collective-permute-done((bf16[64,1024]{1,0:T(8,128)(2,1)S(1)}, bf16[64,1024]{1,0:T(8,128)(2,1)S(1)}, u32[]{:S(2)}, u32[]{:S(2)}) %collective-permute-start.8) | collective-permute-done | bytes 131104 | tf_op jit(solution)/shard_map/ppermute | solution.py:216
  46.7 0.0 collective-permute-done.9
  46.7 0.5 collective-permute-done.10
  47.1 0.8 %convert_add_fusion.1 = f32[64,1024]{1,0:T(8,128)} fusion(bf16[64,1024]{1,0:T(8,128)(2,1)S(1)} %collective-permute-done.10, bf16[64,1024]{1,0:T(8,128)(2,1)S(1)} %collective-permute-done.9, bf16[64,1024]{1,0:T(8,128)(2,1)S(1)} %collective-permute-done.8, f32[256,1024]{1,0:T(8,128)S(1)} %convert_add_fusion, s32[]{:T(128)S(6)} %select_n.55), kind=kLoop, calls=%fused_computation.3 | loop fusion | flops 393216 | bytes 917508 | tf_op jit(solution)/shard_map/add | solution.py:260
  (8 shorter events, 0.2 us)
Async XLA Ops:
  12.3 5.4 %collective-permute-start = (bf16[256,1024]{1,0:T(8,128)(2,1)S(1)}, bf16[256,1024]{1,0:T(8,128)(2,1)S(1)}, u32[]{:S(2)}, u32[]{:S(2)}) collective-permute-start(bf16[256,1024]{1,0:T(8,128)(2,1)S(1)} %get-tuple-element.23.far_send), channel_id=1, source_target_pairs={{0,1},{1,0},{2,3},{3,2},{4,5},{5,4},{6,7},{7,6},{8,9},{9,8},{10,11... | collective-permute-start | bytes 1572872 | tf_op jit(solution)/shard_map/ppermute | solution.py:216
  12.9 1.9 %collective-permute-start.1 = (f32[64,1024]{1,0:T(8,128)S(1)}, f32[64,1024]{1,0:T(8,128)S(1)}, u32[]{:S(2)}, u32[]{:S(2)}) collective-permute-start(f32[64,1024]{1,0:T(8,128)S(1)} %get-tuple-element.25), channel_id=1, source_target_pairs={{0,1},{1,0},{2,3},{3,2},{4,5},{5,4},{6,7},{7,6},{8,9},{9,8},{10,11... | collective-permute-start | bytes 786440 | tf_op jit(solution)/shard_map/ppermute | solution.py:216
  14.8 6.3 %collective-permute-start.4 = (bf16[32,1024]{1,0:T(8,128)(2,1)S(1)}, bf16[32,1024]{1,0:T(8,128)(2,1)S(1)}, u32[]{:S(2)}, u32[]{:S(2)}) collective-permute-start(bf16[32,1024]{1,0:T(8,128)(2,1)S(1)} %slice.17), channel_id=1, source_target_pairs={{0,2},{1,3},{2,0},{3,1},{4,6},{5,7},{6,4},{7,5},{8,10},{9,11},{10,... | collective-permute-start | bytes 196616 | tf_op jit(solution)/shard_map/ppermute | solution.py:216
  17.9 13.8 %collective-permute-start.3 = (bf16[256,1024]{1,0:T(8,128)(2,1)S(1)}, bf16[256,1024]{1,0:T(8,128)(2,1)S(1)}, u32[]{:S(2)}, u32[]{:S(2)}) collective-permute-start(bf16[256,1024]{1,0:T(8,128)(2,1)S(1)} %add_convert_fusion), channel_id=1, source_target_pairs={{0,2},{1,3},{2,0},{3,1},{4,6},{5,7},{6,4},{7,5},{8,10},{9,11},{10,... | collective-permute-start | bytes 1572872 | tf_op jit(solution)/shard_map/ppermute | solution.py:216
  21.1 10.6 %collective-permute-start.2 = (bf16[256,1024]{1,0:T(8,128)(2,1)S(1)}, bf16[256,1024]{1,0:T(8,128)(2,1)}, u32[]{:S(2)}, u32[]{:S(2)}) collective-permute-start(bf16[256,1024]{1,0:T(8,128)(2,1)S(1)} %get-tuple-element.28), channel_id=1, source_target_pairs={{0,1},{1,0},{2,3},{3,2},{4,5},{5,4},{6,7},{7,6},{8,9},{9,8},{10,11... | collective-permute-start | bytes 1572872 | tf_op jit(solution)/shard_map/ppermute | solution.py:216
  21.2 7.1 %collective-permute-start.7 = (bf16[32,1024]{1,0:T(8,128)(2,1)S(1)}, bf16[32,1024]{1,0:T(8,128)(2,1)S(1)}, u32[]{:S(2)}, u32[]{:S(2)}) collective-permute-start(bf16[32,1024]{1,0:T(8,128)(2,1)S(1)} %fusion), channel_id=1, source_target_pairs={{0,12},{1,13},{2,14},{3,15},{4,8},{5,9},{6,10},{7,11},{8,4},{9,5},... | collective-permute-start | bytes 196616 | tf_op jit(solution)/shard_map/ppermute | solution.py:216
  25.3 6.1 %collective-permute-start.6 = (bf16[32,1024]{1,0:T(8,128)(2,1)S(1)}, bf16[32,1024]{1,0:T(8,128)(2,1)S(1)}, u32[]{:S(2)}, u32[]{:S(2)}) collective-permute-start(bf16[32,1024]{1,0:T(8,128)(2,1)S(1)} %fusion), channel_id=1, source_target_pairs={{0,8},{1,9},{2,10},{3,11},{4,12},{5,13},{6,14},{7,15},{8,0},{9,1},... | collective-permute-start | bytes 196616 | tf_op jit(solution)/shard_map/ppermute | solution.py:216
  25.3 6.1 %collective-permute-start.5 = (bf16[32,1024]{1,0:T(8,128)(2,1)S(1)}, bf16[32,1024]{1,0:T(8,128)(2,1)S(1)}, u32[]{:S(2)}, u32[]{:S(2)}) collective-permute-start(bf16[32,1024]{1,0:T(8,128)(2,1)S(1)} %fusion), channel_id=1, source_target_pairs={{0,4},{1,5},{2,6},{3,7},{4,0},{5,1},{6,2},{7,3},{8,12},{9,13},{10,... | collective-permute-start | bytes 196616 | tf_op jit(solution)/shard_map/ppermute | solution.py:216
  33.0 5.7 %collective-permute-start.11 = (f32[32,1024]{1,0:T(8,128)S(1)}, f32[32,1024]{1,0:T(8,128)S(1)}, u32[]{:S(2)}, u32[]{:S(2)}) collective-permute-start(f32[32,1024]{1,0:T(8,128)S(1)} %convert_add_fusion.2), channel_id=1, source_target_pairs={{0,2},{1,3},{2,0},{3,1},{4,6},{5,7},{6,4},{7,5},{8,10},{9,11},{10,... | collective-permute-start | bytes 393224 | tf_op jit(solution)/shard_map/ppermute | solution.py:216
  34.6 12.1 %collective-permute-start.8 = (bf16[64,1024]{1,0:T(8,128)(2,1)S(1)}, bf16[64,1024]{1,0:T(8,128)(2,1)S(1)}, u32[]{:S(2)}, u32[]{:S(2)}) collective-permute-start(bf16[64,1024]{1,0:T(8,128)(2,1)S(1)} %get-tuple-element.29), channel_id=1, source_target_pairs={{0,8},{1,9},{2,10},{3,11},{4,12},{5,13},{6,14},{7,15},{8,0},{9,1},... | collective-permute-start | bytes 393224 | tf_op jit(solution)/shard_map/ppermute | solution.py:216
  37.1 9.5 %collective-permute-start.9 = (bf16[64,1024]{1,0:T(8,128)(2,1)S(1)}, bf16[64,1024]{1,0:T(8,128)(2,1)S(1)}, u32[]{:S(2)}, u32[]{:S(2)}) collective-permute-start(bf16[64,1024]{1,0:T(8,128)(2,1)S(1)} %get-tuple-element.30), channel_id=1, source_target_pairs={{0,12},{1,13},{2,14},{3,15},{4,8},{5,9},{6,10},{7,11},{8,4},{9,5},... | collective-permute-start | bytes 393224 | tf_op jit(solution)/shard_map/ppermute | solution.py:216
  38.5 8.7 %collective-permute-start.10 = (bf16[64,1024]{1,0:T(8,128)(2,1)S(1)}, bf16[64,1024]{1,0:T(8,128)(2,1)S(1)}, u32[]{:S(2)}, u32[]{:S(2)}) collective-permute-start(bf16[64,1024]{1,0:T(8,128)(2,1)S(1)} %get-tuple-element.31), channel_id=1, source_target_pairs={{0,4},{1,5},{2,6},{3,7},{4,0},{5,1},{6,2},{7,3},{8,12},{9,13},{10,... | collective-permute-start | bytes 393224 | tf_op jit(solution)/shard_map/ppermute | solution.py:216
  38.7 1.6 %collective-permute-start.12 = (f32[64,1024]{1,0:T(8,128)S(1)}, f32[64,1024]{1,0:T(8,128)S(1)}, u32[]{:S(2)}, u32[]{:S(2)}) collective-permute-start(f32[64,1024]{1,0:T(8,128)S(1)} %pad_maximum_fusion), channel_id=1, source_target_pairs={{0,1},{1,0},{2,3},{3,2},{4,5},{5,4},{6,7},{7,6},{8,9},{9,8},{10,11... | collective-permute-start | bytes 786440 | tf_op jit(solution)/shard_map/ppermute | solution.py:216

commit v7 on v6

--- a/solution.py
+++ b/solution.py
@@ -223,7 +223,7 @@
         place, features, coef, labels, passage_id, slot_of, per_owner, blk
     )
     masks = [m for m in range(1, devices) if not m & 1 and not m & turn]
-    masks = masks[1:] + masks[:1]
+    masks = masks[1:2] + masks[:1] + masks[2:]
     far_in, sums_in = swap(far_send, 1), swap(sums_send, 1)
     far = (far_keep + far_in.astype(F32)).astype(BF16)
     sums = sums_keep + sums_in

time: 48.1 us -> 47.8 us (level)
  waiting for transfers between devices: 14 us -> 13.3 us
    ppermute x13, waiting for transfers between devices: 14 us -> 13.3 us  [swap(): return lax.ppermute(array, 'rows', [(i, i ^ mask) for i in range(devices)])]
  transfers between devices with their start and end apart: 13 -> 13, of which waited for: 7 -> 7; matrix products, arithmetic and copies ran while one was open for 4% -> 5% of each run, Pallas kernels for 6% -> 6%
where the time goes in v7:
time: 47.8 us; the launch traced here: 47.5 us
  Pallas kernels  14.6 us (31%)
  starting transfers between devices  14.5 us (30%)
  waiting for transfers between devices  13.3 us (28%)
  other arithmetic  2.39 us (5%)
  matrix products  1.19 us (2%)
  between operations  0.76 us (2%)
  local copies, waits for them, and re-layouts  0.73 us (2%)
    ppermute x13, starting transfers between devices, swap(): return lax.ppermute(array, 'rows', [(i, i ^ mask) for i in range(devices)])  14.5 us
    ppermute x13, waiting for transfers between devices, swap(): return lax.ppermute(array, 'rows', [(i, i ^ mask) for i in range(devices)])  13.3 us
    pallas_call x1, Pallas kernels, first(): pl.pallas_call(functools.partial(first_kernel, per_owner, blk, chunks), i...  11.6 us
    pallas_call x1, Pallas kernels, second(): pl.pallas_call(functools.partial(second_kernel, blk, chunks), in_specs=[p...  3.02 us
    add x1, other arithmetic, local(): near = near_keep + near_in.astype(F32) + arrived.astype(F32)  1.28 us
    dot_general x1, matrix products, local(): lax.dot_general(columns, stack, (((0,), (0,)), ((), ())), precision=lax.P...  1.19 us
  transfers between devices with their start and end apart: 13, of which 7 were waited for; matrix products, arithmetic and copies ran while one was open for 5% of the time, Pallas kernels for 6%

profile of v7, /device:TPU:0, one launch (start us, length us, event | category | flops | bytes accessed | tf_op | source)
XLA Modules:
  0.0 47.5 jit_solution(10760843038487602748)
XLA Ops:
  0.6 0.1 pad_add_fusion.place
  0.7 11.6 %scores_and_far.1 = (bf16[4096,1024]{1,0:T(8,128)(2,1)S(1)}, f32[1,4096]{1,0:T(1,128)S(1)}, f32[64,1024]{1,0:T(8,128)S(1)}, f32[64,1024]{1,0:T(8,128)S(1)}, bf16...) custom-call(s32[2]{0:T(128)S(1)} %pad_add_fusion.place, bf16[4096,1024]{1,0:T(8,128)(2,1)} %x_hbm.1, ...), custom_call_target="tpu_custom_call" | custom-call | tf_op jit(solution)/shard_map/scores_and_far/pallas_call | solution.py:162
  12.3 0.5 %collective-permute-start = (bf16[256,1024]{1,0:T(8,128)(2,1)S(1)}, bf16[256,1024]{1,0:T(8,128)(2,1)S(1)}, u32[]{:S(2)}, u32[]{:S(2)}) collective-permute-start(bf16[256,1024]{1,0:T(8,128)(2,1)S(1)} %get-tuple-element.23.far_send), channel_id=1, source_target_pairs={{0,1},{1,0},{2,3},{3,2},{4,5},{5,4},{6,7},{7,6},{8,9},{9,8},{10,11... | collective-permute-start | bytes 1572872 | tf_op jit(solution)/shard_map/ppermute | solution.py:216
  12.9 0.1 collective-permute-start.1
  12.9 1.8 %collective-permute-done.1 = f32[64,1024]{1,0:T(8,128)S(1)} collective-permute-done((f32[64,1024]{1,0:T(8,128)S(1)}, f32[64,1024]{1,0:T(8,128)S(1)}, u32[]{:S(2)}, u32[]{:S(2)}) %collective-permute-start.1) | collective-permute-done | bytes 262176 | tf_op jit(solution)/shard_map/ppermute | solution.py:216
  14.8 2.9 %collective-permute-start.4 = (bf16[32,1024]{1,0:T(8,128)(2,1)S(1)}, bf16[32,1024]{1,0:T(8,128)(2,1)S(1)}, u32[]{:S(2)}, u32[]{:S(2)}) collective-permute-start(bf16[32,1024]{1,0:T(8,128)(2,1)S(1)} %slice.17), channel_id=1, source_target_pairs={{0,2},{1,3},{2,0},{3,1},{4,6},{5,7},{6,4},{7,5},{8,10},{9,11},{10,... | collective-permute-start | bytes 196616 | tf_op jit(solution)/shard_map/ppermute | solution.py:216
  17.8 0.0 collective-permute-done
  17.8 0.2 add_convert_fusion
  17.9 0.1 collective-permute-start.3
  18.0 3.0 %near.1 = (bf16[256,1024]{1,0:T(8,128)(2,1)S(1)}, f32[256,1024]{1,0:T(8,128)S(1)}) custom-call(s32[2]{0:T(128)S(1)} %pad_add_fusion.place, bf16[4096,1024]{1,0:T(8,128)(2,1)S(1)} %get-tuple-element.20.x_ref, f32[1,4096]{1,0:T(1,128)S(1)} %get-tuple-element.26.w_ref, bf16[256,1024]{1,0:T(8,128)(2,1)S(1)} %get-tuple-element.23.far_send, ...), custom_call_target="tpu_custom_call" | custom-call | tf_op jit(solution)/shard_map/near/pallas_call | solution.py:191
  21.1 0.1 collective-permute-start.2
  21.1 0.0 collective-permute-done.4
  21.2 4.2 %collective-permute-start.7 = (bf16[32,1024]{1,0:T(8,128)(2,1)S(1)}, bf16[32,1024]{1,0:T(8,128)(2,1)S(1)}, u32[]{:S(2)}, u32[]{:S(2)}) collective-permute-start(bf16[32,1024]{1,0:T(8,128)(2,1)S(1)} %fusion), channel_id=1, source_target_pairs={{0,12},{1,13},{2,14},{3,15},{4,8},{5,9},{6,10},{7,11},{8,4},{9,5},... | collective-permute-start | bytes 196616 | tf_op jit(solution)/shard_map/ppermute | solution.py:216
  25.3 0.0 collective-permute-start.6
  25.3 0.6 %collective-permute-start.5 = (bf16[32,1024]{1,0:T(8,128)(2,1)S(1)}, bf16[32,1024]{1,0:T(8,128)(2,1)S(1)}, u32[]{:S(2)}, u32[]{:S(2)}) collective-permute-start(bf16[32,1024]{1,0:T(8,128)(2,1)S(1)} %fusion), channel_id=1, source_target_pairs={{0,4},{1,5},{2,6},{3,7},{4,0},{5,1},{6,2},{7,3},{8,12},{9,13},{10,... | collective-permute-start | bytes 196616 | tf_op jit(solution)/shard_map/ppermute | solution.py:216
  26.0 2.3 %collective-permute-done.7 = bf16[32,1024]{1,0:T(8,128)(2,1)S(1)} collective-permute-done((bf16[32,1024]{1,0:T(8,128)(2,1)S(1)}, bf16[32,1024]{1,0:T(8,128)(2,1)S(1)}, u32[]{:S(2)}, u32[]{:S(2)}) %collective-permute-start.7) | collective-permute-done | bytes 65568 | tf_op jit(solution)/shard_map/ppermute | solution.py:216
  28.3 3.2 %collective-permute-done.6 = bf16[32,1024]{1,0:T(8,128)(2,1)S(1)} collective-permute-done((bf16[32,1024]{1,0:T(8,128)(2,1)S(1)}, bf16[32,1024]{1,0:T(8,128)(2,1)S(1)}, u32[]{:S(2)}, u32[]{:S(2)}) %collective-permute-start.6) | collective-permute-done | bytes 65568 | tf_op jit(solution)/shard_map/ppermute | solution.py:216
  31.4 0.0 collective-permute-done.5
  31.5 0.2 collective-permute-done.3
  31.7 0.0 collective-permute-done.2
  31.7 1.3 %convert_add_fusion = f32[256,1024]{1,0:T(8,128)S(1)} fusion(bf16[256,1024]{1,0:T(8,128)(2,1)S(1)} %collective-permute-done.3, f32[256,1024]{1,0:T(8,128)S(1)} %get-tuple-element.27, bf16[256,1024]{1,0:T(8,128)(2,1)} %collective-permute-done.2), kind=kLoop, calls=%fused_computation | loop fusion | flops 1048576 | bytes 3145728 | tf_op jit(solution)/shard_map/add | solution.py:239
  33.0 0.1 dynamic-slice_convert_fusion
  33.0 1.5 %collective-permute-start.11 = (f32[32,1024]{1,0:T(8,128)S(1)}, f32[32,1024]{1,0:T(8,128)S(1)}, u32[]{:S(2)}, u32[]{:S(2)}) collective-permute-start(f32[32,1024]{1,0:T(8,128)S(1)} %convert_add_fusion.2), channel_id=1, source_target_pairs={{0,2},{1,3},{2,0},{3,1},{4,6},{5,7},{6,4},{7,5},{8,10},{9,11},{10,... | collective-permute-start | bytes 393224 | tf_op jit(solution)/shard_map/ppermute | solution.py:216
  34.6 2.6 %collective-permute-start.8 = (bf16[64,1024]{1,0:T(8,128)(2,1)S(1)}, bf16[64,1024]{1,0:T(8,128)(2,1)S(1)}, u32[]{:S(2)}, u32[]{:S(2)}) collective-permute-start(bf16[64,1024]{1,0:T(8,128)(2,1)S(1)} %get-tuple-element.29), channel_id=1, source_target_pairs={{0,8},{1,9},{2,10},{3,11},{4,12},{5,13},{6,14},{7,15},{8,0},{9,1},... | collective-permute-start | bytes 393224 | tf_op jit(solution)/shard_map/ppermute | solution.py:216
  37.1 1.6 %collective-permute-start.9 = (bf16[64,1024]{1,0:T(8,128)(2,1)S(1)}, bf16[64,1024]{1,0:T(8,128)(2,1)S(1)}, u32[]{:S(2)}, u32[]{:S(2)}) collective-permute-start(bf16[64,1024]{1,0:T(8,128)(2,1)S(1)} %get-tuple-element.30), channel_id=1, source_target_pairs={{0,4},{1,5},{2,6},{3,7},{4,0},{5,1},{6,2},{7,3},{8,12},{9,13},{10,... | collective-permute-start | bytes 393224 | tf_op jit(solution)/shard_map/ppermute | solution.py:216
  38.7 0.2 collective-permute-start.10
  38.9 0.0 collective-permute-done.11
  39.0 0.1 collective-permute-start.12
  39.0 0.6 %constant_dynamic-slice_fusion = f32[8,1024]{1,0:T(8,128)} fusion(f32[32,1024]{1,0:T(8,128)S(1)} %convert_add_fusion.2, s32[]{:T(128)S(6)} %select_n.60), kind=kLoop, calls=%fused_computation.16 | loop fusion | bytes 65540 | tf_op jit(solution)/shard_map/dynamic_slice | solution.py:247
  39.7 0.9 %collective-permute-done.12 = f32[64,1024]{1,0:T(8,128)S(1)} collective-permute-done((f32[64,1024]{1,0:T(8,128)S(1)}, f32[64,1024]{1,0:T(8,128)S(1)}, u32[]{:S(2)}, u32[]{:S(2)}) %collective-permute-start.12) | collective-permute-done | bytes 262176 | tf_op jit(solution)/shard_map/ppermute | solution.py:216
  40.6 1.2 %fusion.1 = f32[64,1024]{1,0:T(8,128)} fusion(f32[128,1024]{1,0:T(8,128)S(1)} %constant_dynamic-update-slice_fusion, s32[]{:T(128)S(6)} %select_n.59), kind=kOutput, calls=%fused_computation.11 | convolution fusion | flops 100663296 | bytes 851972 | tf_op jit(solution)/shard_map/dot_general | solution.py:251
  41.8 3.5 %collective-permute-done.8 = bf16[64,1024]{1,0:T(8,128)(2,1)S(1)} collective-permute-done((bf16[64,1024]{1,0:T(8,128)(2,1)S(1)}, bf16[64,1024]{1,0:T(8,128)(2,1)S(1)}, u32[]{:S(2)}, u32[]{:S(2)}) %collective-permute-start.8) | collective-permute-done | bytes 131104 | tf_op jit(solution)/shard_map/ppermute | solution.py:216
  45.3 0.0 collective-permute-done.9
  45.3 1.4 %collective-permute-done.10 = bf16[64,1024]{1,0:T(8,128)(2,1)S(1)} collective-permute-done((bf16[64,1024]{1,0:T(8,128)(2,1)S(1)}, bf16[64,1024]{1,0:T(8,128)(2,1)S(1)}, u32[]{:S(2)}, u32[]{:S(2)}) %collective-permute-start.10) | collective-permute-done | bytes 131104 | tf_op jit(solution)/shard_map/ppermute | solution.py:216
  46.7 0.8 %convert_add_fusion.1 = f32[64,1024]{1,0:T(8,128)} fusion(bf16[64,1024]{1,0:T(8,128)(2,1)S(1)} %collective-permute-done.10, bf16[64,1024]{1,0:T(8,128)(2,1)S(1)} %collective-permute-done.9, bf16[64,1024]{1,0:T(8,128)(2,1)S(1)} %collective-permute-done.8, f32[256,1024]{1,0:T(8,128)S(1)} %convert_add_fusion, s32[]{:T(128)S(6)} %select_n.55), kind=kLoop, calls=%fused_computation.3 | loop fusion | flops 393216 | bytes 917508 | tf_op jit(solution)/shard_map/add | solution.py:260
  (8 shorter events, 0.2 us)
Async XLA Ops:
  12.3 5.4 %collective-permute-start = (bf16[256,1024]{1,0:T(8,128)(2,1)S(1)}, bf16[256,1024]{1,0:T(8,128)(2,1)S(1)}, u32[]{:S(2)}, u32[]{:S(2)}) collective-permute-start(bf16[256,1024]{1,0:T(8,128)(2,1)S(1)} %get-tuple-element.23.far_send), channel_id=1, source_target_pairs={{0,1},{1,0},{2,3},{3,2},{4,5},{5,4},{6,7},{7,6},{8,9},{9,8},{10,11... | collective-permute-start | bytes 1572872 | tf_op jit(solution)/shard_map/ppermute | solution.py:216
  12.9 1.9 %collective-permute-start.1 = (f32[64,1024]{1,0:T(8,128)S(1)}, f32[64,1024]{1,0:T(8,128)S(1)}, u32[]{:S(2)}, u32[]{:S(2)}) collective-permute-start(f32[64,1024]{1,0:T(8,128)S(1)} %get-tuple-element.25), channel_id=1, source_target_pairs={{0,1},{1,0},{2,3},{3,2},{4,5},{5,4},{6,7},{7,6},{8,9},{9,8},{10,11... | collective-permute-start | bytes 786440 | tf_op jit(solution)/shard_map/ppermute | solution.py:216
  14.8 6.3 %collective-permute-start.4 = (bf16[32,1024]{1,0:T(8,128)(2,1)S(1)}, bf16[32,1024]{1,0:T(8,128)(2,1)S(1)}, u32[]{:S(2)}, u32[]{:S(2)}) collective-permute-start(bf16[32,1024]{1,0:T(8,128)(2,1)S(1)} %slice.17), channel_id=1, source_target_pairs={{0,2},{1,3},{2,0},{3,1},{4,6},{5,7},{6,4},{7,5},{8,10},{9,11},{10,... | collective-permute-start | bytes 196616 | tf_op jit(solution)/shard_map/ppermute | solution.py:216
  17.9 13.8 %collective-permute-start.3 = (bf16[256,1024]{1,0:T(8,128)(2,1)S(1)}, bf16[256,1024]{1,0:T(8,128)(2,1)S(1)}, u32[]{:S(2)}, u32[]{:S(2)}) collective-permute-start(bf16[256,1024]{1,0:T(8,128)(2,1)S(1)} %add_convert_fusion), channel_id=1, source_target_pairs={{0,2},{1,3},{2,0},{3,1},{4,6},{5,7},{6,4},{7,5},{8,10},{9,11},{10,... | collective-permute-start | bytes 1572872 | tf_op jit(solution)/shard_map/ppermute | solution.py:216
  21.1 10.6 %collective-permute-start.2 = (bf16[256,1024]{1,0:T(8,128)(2,1)S(1)}, bf16[256,1024]{1,0:T(8,128)(2,1)}, u32[]{:S(2)}, u32[]{:S(2)}) collective-permute-start(bf16[256,1024]{1,0:T(8,128)(2,1)S(1)} %get-tuple-element.28), channel_id=1, source_target_pairs={{0,1},{1,0},{2,3},{3,2},{4,5},{5,4},{6,7},{7,6},{8,9},{9,8},{10,11... | collective-permute-start | bytes 1572872 | tf_op jit(solution)/shard_map/ppermute | solution.py:216
  21.2 7.1 %collective-permute-start.7 = (bf16[32,1024]{1,0:T(8,128)(2,1)S(1)}, bf16[32,1024]{1,0:T(8,128)(2,1)S(1)}, u32[]{:S(2)}, u32[]{:S(2)}) collective-permute-start(bf16[32,1024]{1,0:T(8,128)(2,1)S(1)} %fusion), channel_id=1, source_target_pairs={{0,12},{1,13},{2,14},{3,15},{4,8},{5,9},{6,10},{7,11},{8,4},{9,5},... | collective-permute-start | bytes 196616 | tf_op jit(solution)/shard_map/ppermute | solution.py:216
  25.3 6.1 %collective-permute-start.6 = (bf16[32,1024]{1,0:T(8,128)(2,1)S(1)}, bf16[32,1024]{1,0:T(8,128)(2,1)S(1)}, u32[]{:S(2)}, u32[]{:S(2)}) collective-permute-start(bf16[32,1024]{1,0:T(8,128)(2,1)S(1)} %fusion), channel_id=1, source_target_pairs={{0,8},{1,9},{2,10},{3,11},{4,12},{5,13},{6,14},{7,15},{8,0},{9,1},... | collective-permute-start | bytes 196616 | tf_op jit(solution)/shard_map/ppermute | solution.py:216
  25.3 6.1 %collective-permute-start.5 = (bf16[32,1024]{1,0:T(8,128)(2,1)S(1)}, bf16[32,1024]{1,0:T(8,128)(2,1)S(1)}, u32[]{:S(2)}, u32[]{:S(2)}) collective-permute-start(bf16[32,1024]{1,0:T(8,128)(2,1)S(1)} %fusion), channel_id=1, source_target_pairs={{0,4},{1,5},{2,6},{3,7},{4,0},{5,1},{6,2},{7,3},{8,12},{9,13},{10,... | collective-permute-start | bytes 196616 | tf_op jit(solution)/shard_map/ppermute | solution.py:216
  33.0 5.9 %collective-permute-start.11 = (f32[32,1024]{1,0:T(8,128)S(1)}, f32[32,1024]{1,0:T(8,128)S(1)}, u32[]{:S(2)}, u32[]{:S(2)}) collective-permute-start(f32[32,1024]{1,0:T(8,128)S(1)} %convert_add_fusion.2), channel_id=1, source_target_pairs={{0,2},{1,3},{2,0},{3,1},{4,6},{5,7},{6,4},{7,5},{8,10},{9,11},{10,... | collective-permute-start | bytes 393224 | tf_op jit(solution)/shard_map/ppermute | solution.py:216
  34.6 10.7 %collective-permute-start.8 = (bf16[64,1024]{1,0:T(8,128)(2,1)S(1)}, bf16[64,1024]{1,0:T(8,128)(2,1)S(1)}, u32[]{:S(2)}, u32[]{:S(2)}) collective-permute-start(bf16[64,1024]{1,0:T(8,128)(2,1)S(1)} %get-tuple-element.29), channel_id=1, source_target_pairs={{0,8},{1,9},{2,10},{3,11},{4,12},{5,13},{6,14},{7,15},{8,0},{9,1},... | collective-permute-start | bytes 393224 | tf_op jit(solution)/shard_map/ppermute | solution.py:216
  37.1 8.1 %collective-permute-start.9 = (bf16[64,1024]{1,0:T(8,128)(2,1)S(1)}, bf16[64,1024]{1,0:T(8,128)(2,1)S(1)}, u32[]{:S(2)}, u32[]{:S(2)}) collective-permute-start(bf16[64,1024]{1,0:T(8,128)(2,1)S(1)} %get-tuple-element.30), channel_id=1, source_target_pairs={{0,4},{1,5},{2,6},{3,7},{4,0},{5,1},{6,2},{7,3},{8,12},{9,13},{10,... | collective-permute-start | bytes 393224 | tf_op jit(solution)/shard_map/ppermute | solution.py:216
  38.7 8.0 %collective-permute-start.10 = (bf16[64,1024]{1,0:T(8,128)(2,1)S(1)}, bf16[64,1024]{1,0:T(8,128)(2,1)S(1)}, u32[]{:S(2)}, u32[]{:S(2)}) collective-permute-start(bf16[64,1024]{1,0:T(8,128)(2,1)S(1)} %get-tuple-element.31), channel_id=1, source_target_pairs={{0,12},{1,13},{2,14},{3,15},{4,8},{5,9},{6,10},{7,11},{8,4},{9,5},... | collective-permute-start | bytes 393224 | tf_op jit(solution)/shard_map/ppermute | solution.py:216
  39.0 1.6 %collective-permute-start.12 = (f32[64,1024]{1,0:T(8,128)S(1)}, f32[64,1024]{1,0:T(8,128)S(1)}, u32[]{:S(2)}, u32[]{:S(2)}) collective-permute-start(f32[64,1024]{1,0:T(8,128)S(1)} %pad_maximum_fusion), channel_id=1, source_target_pairs={{0,1},{1,0},{2,3},{3,2},{4,5},{5,4},{6,7},{7,6},{8,9},{9,8},{10,11... | collective-permute-start | bytes 786440 | tf_op jit(solution)/shard_map/ppermute | solution.py:216

commit v8 on v7

--- a/solution.py
+++ b/solution.py
@@ -242,7 +242,7 @@
     parts = [block(rest(m)).astype(BF16) for m in masks]
     for part in sums_parts:
         sums = sums + part.astype(F32)
-    sums, parts = lax.optimization_barrier((sums, parts))
+    sums, _ = lax.optimization_barrier((sums, parts))
     parts = [swap(part, m) for part, m in zip(parts, masks)]
     grad_local = lax.dynamic_slice_in_dim(sums, rest(me) * per_owner, per_owner, 0)
     sums = jnp.concatenate([sums, swap(sums, turn)], axis=0)

time: 47.8 us -> 47.8 us (level)
  transfers between devices with their start and end apart: 13 -> 13, of which waited for: 7 -> 8; matrix products, arithmetic and copies ran while one was open for 5% -> 5% of each run, Pallas kernels for 6% -> 6%
where the time goes in v8:
time: 47.8 us; the launch traced here: 47.5 us
  Pallas kernels  14.6 us (31%)
  starting transfers between devices  14.5 us (30%)
  waiting for transfers between devices  13.3 us (28%)
  other arithmetic  2.39 us (5%)
  matrix products  1.19 us (2%)
  between operations  0.76 us (2%)
  local copies, waits for them, and re-layouts  0.73 us (2%)
    ppermute x13, starting transfers between devices, swap(): return lax.ppermute(array, 'rows', [(i, i ^ mask) for i in range(devices)])  14.5 us
    ppermute x13, waiting for transfers between devices, swap(): return lax.ppermute(array, 'rows', [(i, i ^ mask) for i in range(devices)])  13.3 us
    pallas_call x1, Pallas kernels, first(): pl.pallas_call(functools.partial(first_kernel, per_owner, blk, chunks), i...  11.6 us
    pallas_call x1, Pallas kernels, second(): pl.pallas_call(functools.partial(second_kernel, blk, chunks), in_specs=[p...  3.02 us
    add x1, other arithmetic, local(): near = near_keep + near_in.astype(F32) + arrived.astype(F32)  1.28 us
    dot_general x1, matrix products, local(): lax.dot_general(columns, stack, (((0,), (0,)), ((), ())), precision=lax.P...  1.19 us
  transfers between devices with their start and end apart: 13, of which 8 were waited for; matrix products, arithmetic and copies ran while one was open for 5% of the time, Pallas kernels for 6%

profile of v8, /device:TPU:0, one launch (start us, length us, event | category | flops | bytes accessed | tf_op | source)
XLA Modules:
  0.0 47.5 jit_solution(12000506592990660591)
XLA Ops:
  0.6 0.1 pad_add_fusion.place
  0.7 11.6 %scores_and_far.1 = (bf16[4096,1024]{1,0:T(8,128)(2,1)S(1)}, f32[1,4096]{1,0:T(1,128)S(1)}, f32[64,1024]{1,0:T(8,128)S(1)}, f32[64,1024]{1,0:T(8,128)S(1)}, bf16...) custom-call(s32[2]{0:T(128)S(1)} %pad_add_fusion.place, bf16[4096,1024]{1,0:T(8,128)(2,1)} %x_hbm.1, ...), custom_call_target="tpu_custom_call" | custom-call | tf_op jit(solution)/shard_map/scores_and_far/pallas_call | solution.py:162
  12.3 0.5 %collective-permute-start = (bf16[256,1024]{1,0:T(8,128)(2,1)S(1)}, bf16[256,1024]{1,0:T(8,128)(2,1)S(1)}, u32[]{:S(2)}, u32[]{:S(2)}) collective-permute-start(bf16[256,1024]{1,0:T(8,128)(2,1)S(1)} %get-tuple-element.20.far_send), channel_id=1, source_target_pairs={{0,1},{1,0},{2,3},{3,2},{4,5},{5,4},{6,7},{7,6},{8,9},{9,8},{10,11... | collective-permute-start | bytes 1572872 | tf_op jit(solution)/shard_map/ppermute | solution.py:216
  12.9 0.1 collective-permute-start.1
  12.9 1.8 %collective-permute-done.1 = f32[64,1024]{1,0:T(8,128)S(1)} collective-permute-done((f32[64,1024]{1,0:T(8,128)S(1)}, f32[64,1024]{1,0:T(8,128)S(1)}, u32[]{:S(2)}, u32[]{:S(2)}) %collective-permute-start.1) | collective-permute-done | bytes 262176 | tf_op jit(solution)/shard_map/ppermute | solution.py:216
  14.8 2.9 %collective-permute-start.7 = (bf16[32,1024]{1,0:T(8,128)(2,1)S(1)}, bf16[32,1024]{1,0:T(8,128)(2,1)S(1)}, u32[]{:S(2)}, u32[]{:S(2)}) collective-permute-start(bf16[32,1024]{1,0:T(8,128)(2,1)S(1)} %slice.17), channel_id=1, source_target_pairs={{0,2},{1,3},{2,0},{3,1},{4,6},{5,7},{6,4},{7,5},{8,10},{9,11},{10,... | collective-permute-start | bytes 196616 | tf_op jit(solution)/shard_map/ppermute | solution.py:216
  17.8 0.0 collective-permute-done
  17.8 0.2 add_convert_fusion
  17.9 0.1 collective-permute-start.3
  18.0 3.0 %near.1 = (bf16[256,1024]{1,0:T(8,128)(2,1)S(1)}, f32[256,1024]{1,0:T(8,128)S(1)}) custom-call(s32[2]{0:T(128)S(1)} %pad_add_fusion.place, bf16[4096,1024]{1,0:T(8,128)(2,1)S(1)} %get-tuple-element.17.x_ref, f32[1,4096]{1,0:T(1,128)S(1)} %get-tuple-element.23.w_ref, bf16[256,1024]{1,0:T(8,128)(2,1)S(1)} %get-tuple-element.20.far_send, ...), custom_call_target="tpu_custom_call" | custom-call | tf_op jit(solution)/shard_map/near/pallas_call | solution.py:191
  21.1 0.1 collective-permute-start.2
  21.1 0.0 collective-permute-done.7
  21.2 4.2 %collective-permute-start.10 = (bf16[32,1024]{1,0:T(8,128)(2,1)S(1)}, bf16[32,1024]{1,0:T(8,128)(2,1)S(1)}, u32[]{:S(2)}, u32[]{:S(2)}) collective-permute-start(bf16[32,1024]{1,0:T(8,128)(2,1)S(1)} %fusion), channel_id=1, source_target_pairs={{0,12},{1,13},{2,14},{3,15},{4,8},{5,9},{6,10},{7,11},{8,4},{9,5},... | collective-permute-start | bytes 196616 | tf_op jit(solution)/shard_map/ppermute | solution.py:216
  25.3 0.0 collective-permute-start.8
  25.3 0.6 %collective-permute-start.9 = (bf16[32,1024]{1,0:T(8,128)(2,1)S(1)}, bf16[32,1024]{1,0:T(8,128)(2,1)S(1)}, u32[]{:S(2)}, u32[]{:S(2)}) collective-permute-start(bf16[32,1024]{1,0:T(8,128)(2,1)S(1)} %fusion), channel_id=1, source_target_pairs={{0,8},{1,9},{2,10},{3,11},{4,12},{5,13},{6,14},{7,15},{8,0},{9,1},... | collective-permute-start | bytes 196616 | tf_op jit(solution)/shard_map/ppermute | solution.py:216
  26.0 2.4 %collective-permute-done.10 = bf16[32,1024]{1,0:T(8,128)(2,1)S(1)} collective-permute-done((bf16[32,1024]{1,0:T(8,128)(2,1)S(1)}, bf16[32,1024]{1,0:T(8,128)(2,1)S(1)}, u32[]{:S(2)}, u32[]{:S(2)}) %collective-permute-start.10) | collective-permute-done | bytes 65568 | tf_op jit(solution)/shard_map/ppermute | solution.py:216
  28.3 2.5 %collective-permute-done.8 = bf16[32,1024]{1,0:T(8,128)(2,1)S(1)} collective-permute-done((bf16[32,1024]{1,0:T(8,128)(2,1)S(1)}, bf16[32,1024]{1,0:T(8,128)(2,1)S(1)}, u32[]{:S(2)}, u32[]{:S(2)}) %collective-permute-start.8) | collective-permute-done | bytes 65568 | tf_op jit(solution)/shard_map/ppermute | solution.py:216
  30.9 0.4 collective-permute-done.9
  31.3 0.0 collective-permute-done.2
  31.3 0.4 collective-permute-done.3
  31.7 1.3 %convert_add_fusion = f32[256,1024]{1,0:T(8,128)S(1)} fusion(bf16[256,1024]{1,0:T(8,128)(2,1)S(1)} %collective-permute-done.3, f32[256,1024]{1,0:T(8,128)S(1)} %get-tuple-element.24, bf16[256,1024]{1,0:T(8,128)(2,1)} %collective-permute-done.2), kind=kLoop, calls=%fused_computation | loop fusion | flops 1048576 | bytes 3145728 | tf_op jit(solution)/shard_map/add | solution.py:239
  33.0 0.1 dynamic-slice_convert_fusion
  33.0 1.5 %collective-permute-start.11 = (f32[32,1024]{1,0:T(8,128)S(1)}, f32[32,1024]{1,0:T(8,128)S(1)}, u32[]{:S(2)}, u32[]{:S(2)}) collective-permute-start(f32[32,1024]{1,0:T(8,128)S(1)} %convert_add_fusion.2), channel_id=1, source_target_pairs={{0,2},{1,3},{2,0},{3,1},{4,6},{5,7},{6,4},{7,5},{8,10},{9,11},{10,... | collective-permute-start | bytes 393224 | tf_op jit(solution)/shard_map/ppermute | solution.py:216
  34.5 2.6 %collective-permute-start.4 = (bf16[64,1024]{1,0:T(8,128)(2,1)S(1)}, bf16[64,1024]{1,0:T(8,128)(2,1)S(1)}, u32[]{:S(2)}, u32[]{:S(2)}) collective-permute-start(bf16[64,1024]{1,0:T(8,128)(2,1)S(1)} %get-tuple-element.33), channel_id=1, source_target_pairs={{0,8},{1,9},{2,10},{3,11},{4,12},{5,13},{6,14},{7,15},{8,0},{9,1},... | collective-permute-start | bytes 393224 | tf_op jit(solution)/shard_map/ppermute | solution.py:216
  37.1 1.6 %collective-permute-start.5 = (bf16[64,1024]{1,0:T(8,128)(2,1)S(1)}, bf16[64,1024]{1,0:T(8,128)(2,1)S(1)}, u32[]{:S(2)}, u32[]{:S(2)}) collective-permute-start(bf16[64,1024]{1,0:T(8,128)(2,1)S(1)} %get-tuple-element.32), channel_id=1, source_target_pairs={{0,4},{1,5},{2,6},{3,7},{4,0},{5,1},{6,2},{7,3},{8,12},{9,13},{10,... | collective-permute-start | bytes 393224 | tf_op jit(solution)/shard_map/ppermute | solution.py:216
  38.7 0.2 collective-permute-start.6
  38.9 0.0 collective-permute-done.11
  39.0 0.1 collective-permute-start.12
  39.0 0.6 %constant_dynamic-slice_fusion = f32[8,1024]{1,0:T(8,128)} fusion(f32[32,1024]{1,0:T(8,128)S(1)} %convert_add_fusion.2, s32[]{:T(128)S(6)} %select_n.60), kind=kLoop, calls=%fused_computation.16 | loop fusion | bytes 65540 | tf_op jit(solution)/shard_map/dynamic_slice | solution.py:247
  39.7 0.9 %collective-permute-done.12 = f32[64,1024]{1,0:T(8,128)S(1)} collective-permute-done((f32[64,1024]{1,0:T(8,128)S(1)}, f32[64,1024]{1,0:T(8,128)S(1)}, u32[]{:S(2)}, u32[]{:S(2)}) %collective-permute-start.12) | collective-permute-done | bytes 262176 | tf_op jit(solution)/shard_map/ppermute | solution.py:216
  40.6 1.2 %fusion.1 = f32[64,1024]{1,0:T(8,128)} fusion(f32[128,1024]{1,0:T(8,128)S(1)} %constant_dynamic-update-slice_fusion, s32[]{:T(128)S(6)} %select_n.59), kind=kOutput, calls=%fused_computation.11 | convolution fusion | flops 100663296 | bytes 851972 | tf_op jit(solution)/shard_map/dot_general | solution.py:251
  41.8 3.5 %collective-permute-done.4 = bf16[64,1024]{1,0:T(8,128)(2,1)S(1)} collective-permute-done((bf16[64,1024]{1,0:T(8,128)(2,1)S(1)}, bf16[64,1024]{1,0:T(8,128)(2,1)S(1)}, u32[]{:S(2)}, u32[]{:S(2)}) %collective-permute-start.4) | collective-permute-done | bytes 131104 | tf_op jit(solution)/shard_map/ppermute | solution.py:216
  45.3 0.0 collective-permute-done.5
  45.3 1.4 %collective-permute-done.6 = bf16[64,1024]{1,0:T(8,128)(2,1)S(1)} collective-permute-done((bf16[64,1024]{1,0:T(8,128)(2,1)S(1)}, bf16[64,1024]{1,0:T(8,128)(2,1)S(1)}, u32[]{:S(2)}, u32[]{:S(2)}) %collective-permute-start.6) | collective-permute-done | bytes 131104 | tf_op jit(solution)/shard_map/ppermute | solution.py:216
  46.7 0.8 %convert_add_fusion.1 = f32[64,1024]{1,0:T(8,128)} fusion(bf16[64,1024]{1,0:T(8,128)(2,1)S(1)} %collective-permute-done.6, bf16[64,1024]{1,0:T(8,128)(2,1)S(1)} %collective-permute-done.5, bf16[64,1024]{1,0:T(8,128)(2,1)S(1)} %collective-permute-done.4, f32[256,1024]{1,0:T(8,128)S(1)} %convert_add_fusion, s32[]{:T(128)S(6)} %select_n.55), kind=kLoop, calls=%fused_computation.3 | loop fusion | flops 393216 | bytes 917508 | tf_op jit(solution)/shard_map/add | solution.py:260
  (8 shorter events, 0.2 us)
Async XLA Ops:
  12.3 5.4 %collective-permute-start = (bf16[256,1024]{1,0:T(8,128)(2,1)S(1)}, bf16[256,1024]{1,0:T(8,128)(2,1)S(1)}, u32[]{:S(2)}, u32[]{:S(2)}) collective-permute-start(bf16[256,1024]{1,0:T(8,128)(2,1)S(1)} %get-tuple-element.20.far_send), channel_id=1, source_target_pairs={{0,1},{1,0},{2,3},{3,2},{4,5},{5,4},{6,7},{7,6},{8,9},{9,8},{10,11... | collective-permute-start | bytes 1572872 | tf_op jit(solution)/shard_map/ppermute | solution.py:216
  12.9 1.9 %collective-permute-start.1 = (f32[64,1024]{1,0:T(8,128)S(1)}, f32[64,1024]{1,0:T(8,128)S(1)}, u32[]{:S(2)}, u32[]{:S(2)}) collective-permute-start(f32[64,1024]{1,0:T(8,128)S(1)} %get-tuple-element.22), channel_id=1, source_target_pairs={{0,1},{1,0},{2,3},{3,2},{4,5},{5,4},{6,7},{7,6},{8,9},{9,8},{10,11... | collective-permute-start | bytes 786440 | tf_op jit(solution)/shard_map/ppermute | solution.py:216
  14.8 6.3 %collective-permute-start.7 = (bf16[32,1024]{1,0:T(8,128)(2,1)S(1)}, bf16[32,1024]{1,0:T(8,128)(2,1)S(1)}, u32[]{:S(2)}, u32[]{:S(2)}) collective-permute-start(bf16[32,1024]{1,0:T(8,128)(2,1)S(1)} %slice.17), channel_id=1, source_target_pairs={{0,2},{1,3},{2,0},{3,1},{4,6},{5,7},{6,4},{7,5},{8,10},{9,11},{10,... | collective-permute-start | bytes 196616 | tf_op jit(solution)/shard_map/ppermute | solution.py:216
  17.9 13.8 %collective-permute-start.3 = (bf16[256,1024]{1,0:T(8,128)(2,1)S(1)}, bf16[256,1024]{1,0:T(8,128)(2,1)S(1)}, u32[]{:S(2)}, u32[]{:S(2)}) collective-permute-start(bf16[256,1024]{1,0:T(8,128)(2,1)S(1)} %add_convert_fusion), channel_id=1, source_target_pairs={{0,2},{1,3},{2,0},{3,1},{4,6},{5,7},{6,4},{7,5},{8,10},{9,11},{10,... | collective-permute-start | bytes 1572872 | tf_op jit(solution)/shard_map/ppermute | solution.py:216
  21.1 10.2 %collective-permute-start.2 = (bf16[256,1024]{1,0:T(8,128)(2,1)S(1)}, bf16[256,1024]{1,0:T(8,128)(2,1)}, u32[]{:S(2)}, u32[]{:S(2)}) collective-permute-start(bf16[256,1024]{1,0:T(8,128)(2,1)S(1)} %get-tuple-element.25), channel_id=1, source_target_pairs={{0,1},{1,0},{2,3},{3,2},{4,5},{5,4},{6,7},{7,6},{8,9},{9,8},{10,11... | collective-permute-start | bytes 1572872 | tf_op jit(solution)/shard_map/ppermute | solution.py:216
  21.2 7.2 %collective-permute-start.10 = (bf16[32,1024]{1,0:T(8,128)(2,1)S(1)}, bf16[32,1024]{1,0:T(8,128)(2,1)S(1)}, u32[]{:S(2)}, u32[]{:S(2)}) collective-permute-start(bf16[32,1024]{1,0:T(8,128)(2,1)S(1)} %fusion), channel_id=1, source_target_pairs={{0,12},{1,13},{2,14},{3,15},{4,8},{5,9},{6,10},{7,11},{8,4},{9,5},... | collective-permute-start | bytes 196616 | tf_op jit(solution)/shard_map/ppermute | solution.py:216
  25.3 5.5 %collective-permute-start.8 = (bf16[32,1024]{1,0:T(8,128)(2,1)S(1)}, bf16[32,1024]{1,0:T(8,128)(2,1)S(1)}, u32[]{:S(2)}, u32[]{:S(2)}) collective-permute-start(bf16[32,1024]{1,0:T(8,128)(2,1)S(1)} %fusion), channel_id=1, source_target_pairs={{0,4},{1,5},{2,6},{3,7},{4,0},{5,1},{6,2},{7,3},{8,12},{9,13},{10,... | collective-permute-start | bytes 196616 | tf_op jit(solution)/shard_map/ppermute | solution.py:216
  25.3 5.9 %collective-permute-start.9 = (bf16[32,1024]{1,0:T(8,128)(2,1)S(1)}, bf16[32,1024]{1,0:T(8,128)(2,1)S(1)}, u32[]{:S(2)}, u32[]{:S(2)}) collective-permute-start(bf16[32,1024]{1,0:T(8,128)(2,1)S(1)} %fusion), channel_id=1, source_target_pairs={{0,8},{1,9},{2,10},{3,11},{4,12},{5,13},{6,14},{7,15},{8,0},{9,1},... | collective-permute-start | bytes 196616 | tf_op jit(solution)/shard_map/ppermute | solution.py:216
  33.0 5.9 %collective-permute-start.11 = (f32[32,1024]{1,0:T(8,128)S(1)}, f32[32,1024]{1,0:T(8,128)S(1)}, u32[]{:S(2)}, u32[]{:S(2)}) collective-permute-start(f32[32,1024]{1,0:T(8,128)S(1)} %convert_add_fusion.2), channel_id=1, source_target_pairs={{0,2},{1,3},{2,0},{3,1},{4,6},{5,7},{6,4},{7,5},{8,10},{9,11},{10,... | collective-permute-start | bytes 393224 | tf_op jit(solution)/shard_map/ppermute | solution.py:216
  34.5 10.7 %collective-permute-start.4 = (bf16[64,1024]{1,0:T(8,128)(2,1)S(1)}, bf16[64,1024]{1,0:T(8,128)(2,1)S(1)}, u32[]{:S(2)}, u32[]{:S(2)}) collective-permute-start(bf16[64,1024]{1,0:T(8,128)(2,1)S(1)} %get-tuple-element.33), channel_id=1, source_target_pairs={{0,8},{1,9},{2,10},{3,11},{4,12},{5,13},{6,14},{7,15},{8,0},{9,1},... | collective-permute-start | bytes 393224 | tf_op jit(solution)/shard_map/ppermute | solution.py:216
  37.1 8.1 %collective-permute-start.5 = (bf16[64,1024]{1,0:T(8,128)(2,1)S(1)}, bf16[64,1024]{1,0:T(8,128)(2,1)S(1)}, u32[]{:S(2)}, u32[]{:S(2)}) collective-permute-start(bf16[64,1024]{1,0:T(8,128)(2,1)S(1)} %get-tuple-element.32), channel_id=1, source_target_pairs={{0,4},{1,5},{2,6},{3,7},{4,0},{5,1},{6,2},{7,3},{8,12},{9,13},{10,... | collective-permute-start | bytes 393224 | tf_op jit(solution)/shard_map/ppermute | solution.py:216
  38.7 8.0 %collective-permute-start.6 = (bf16[64,1024]{1,0:T(8,128)(2,1)S(1)}, bf16[64,1024]{1,0:T(8,128)(2,1)S(1)}, u32[]{:S(2)}, u32[]{:S(2)}) collective-permute-start(bf16[64,1024]{1,0:T(8,128)(2,1)S(1)} %get-tuple-element.31), channel_id=1, source_target_pairs={{0,12},{1,13},{2,14},{3,15},{4,8},{5,9},{6,10},{7,11},{8,4},{9,5},... | collective-permute-start | bytes 393224 | tf_op jit(solution)/shard_map/ppermute | solution.py:216
  39.0 1.6 %collective-permute-start.12 = (f32[64,1024]{1,0:T(8,128)S(1)}, f32[64,1024]{1,0:T(8,128)S(1)}, u32[]{:S(2)}, u32[]{:S(2)}) collective-permute-start(f32[64,1024]{1,0:T(8,128)S(1)} %pad_maximum_fusion), channel_id=1, source_target_pairs={{0,1},{1,0},{2,3},{3,2},{4,5},{5,4},{6,7},{7,6},{8,9},{9,8},{10,11... | collective-permute-start | bytes 786440 | tf_op jit(solution)/shard_map/ppermute | solution.py:216
